TPU v7x, 512 devices: a whole 4x8x8 slice. The times are simulated.
512 devices in a mesh: gx: 8 (over z), gy: 8 (over x, core), gz: 8 (over y).
Axes of the slice: x: 4, y: 8, z: 8, core: 2. Of those that a mesh axis runs over, the one named last changes fastest.
Arguments:
- density: float32 [64, 64, 1024], P('gz', 'gy', 'gx'), may hold values from 0.9 to 1.1
- velocity: float32 [3, 64, 64, 1024], P(None, 'gz', 'gy', 'gx'), may hold values from -1.25 to 1.25
- solid: int32 [64, 64, 1024], P('gz', 'gy', 'gx'), may hold values from 0 to 1, as said below
- owner_map: int32 [8, 8, 8, 64, 1], P('gx', 'gy', 'gz'), may hold values from 0 to 63; in each aligned block of 64 rows (0 to 63, 64 to 127, ..., all dimensions but the last counted through in order) at most 2 rows name the same one
- slot_map: int32 [8, 8, 8, 64, 1], P('gx', 'gy', 'gz'), may hold values from 0 to 15
Outputs:
- final_moments: float32 [10, 64, 64, 1024], P(None, 'gz', 'gy', 'gx')
- relaxation: float32 [64, 64, 1024], P('gz', 'gy', 'gx')
- coarse_sums: float32 [8, 8, 8, 16, 160], P('gx', 'gy', 'gz')
Inputs may be any that keep to these rules, and one draw needn't show every extreme that they name: 1 marks a solid cell; every cell of the vertical layer 0 is solid, and above it a column is solid below a building height that is constant over footprints of 4 spanwise by 4 streamwise columns. `owner_map`: of the 64 fine blocks of one device, at most 2 name the same owner.
All inputs are finite; a program needn't handle non-finite values.
Results may differ from a plain program's by a relative error of at most 0.0001.
Values sent between devices are 32-bit elements; how exact they have to be, the bound alone decides.
No kernel may reach another device: no remote copies, remote signals or barrier semaphores. Data moves between devices by JAX's collectives and lax.ppermute only.
A program may use at most 64 MiB of HBM per device.

v0:
```python
import jax
import jax.numpy as jnp
import numpy as np
from jax import lax
from jax.sharding import PartitionSpec as P

ITERS = 2
SLOTS = 16


WALE_COEFF = 0.5
BASE_VISCOSITY = 0.01
WALE_FLOOR = 1e-10
STRESS_PAIRS = ((0, 0), (1, 1), (2, 2), (0, 1), (0, 2), (1, 2))


def with_halo(cells, sides, width):
    for axis, dim in sides:
        count = lax.axis_size(axis)
        head = lax.slice_in_dim(cells, 0, width, axis=dim)
        tail = lax.slice_in_dim(cells, cells.shape[dim] - width, cells.shape[dim], axis=dim)
        cells = jnp.concatenate(
            [
                lax.ppermute(tail, axis, [(i, (i + 1) % count) for i in range(count)]),
                cells,
                lax.ppermute(head, axis, [((i + 1) % count, i) for i in range(count)]),
            ],
            axis=dim,
        )
    return cells


def lattice_tables():
    directions = np.array(
        [
            [0, 0, 0],
            [1, 0, 0],
            [-1, 0, 0],
            [0, 1, 0],
            [0, -1, 0],
            [0, 0, 1],
            [0, 0, -1],
            [1, 1, 0],
            [-1, -1, 0],
            [1, -1, 0],
            [-1, 1, 0],
            [1, 0, 1],
            [-1, 0, -1],
            [1, 0, -1],
            [-1, 0, 1],
            [0, 1, 1],
            [0, -1, -1],
            [0, 1, -1],
            [0, -1, 1],
        ]
    )
    recon_table = np.zeros((19, 10))
    moment_table = np.zeros((10, 19))
    for number in range(19):
        vector = directions[number]
        square = float(np.dot(vector, vector))
        weight = 1.0 / 3.0 if square == 0 else 1.0 / 18.0 if square == 1 else 1.0 / 36.0
        recon_table[number, 0] = weight * (1.0 - 1.5 * (square - 1.0))
        recon_table[number, 1:4] = 3.0 * weight * vector
        moment_table[0, number] = 1.0
        moment_table[1:4, number] = vector
        for column, stress_pair in enumerate(STRESS_PAIRS):
            left_axis, right_axis = stress_pair
            product = float(vector[left_axis] * vector[right_axis])
            moment_table[4 + column, number] = product
            if left_axis == right_axis:
                recon_table[number, 4 + column] = 4.5 * weight * (product - 1.0 / 3.0)
            else:
                recon_table[number, 4 + column] = 9.0 * weight * product
    return (
        directions,
        jnp.asarray(recon_table, jnp.float32),
        jnp.asarray(moment_table, jnp.float32),
    )


def initial_state(density, velocity, fluid):
    momentum = density * velocity * fluid
    members = [density, momentum[0], momentum[1], momentum[2]]
    for left_axis, right_axis in STRESS_PAIRS:
        balance = momentum[left_axis] * momentum[right_axis] / density
        if left_axis == right_axis:
            balance = balance + density / 3.0
        members.append(balance)
    return jnp.stack(members)


def interior(padded, along, offset):
    window = [slice(None)] + [slice(1, padded.shape[1 + dimension] - 1) for dimension in range(3)]
    window[1 + along] = slice(1 + offset, padded.shape[1 + along] - 1 + offset)
    return padded[tuple(window)]


def wale_relaxation(padded):
    forward = [interior(padded, along, 1) for along in range(3)]
    backward = [interior(padded, along, -1) for along in range(3)]
    gradient = [
        [
            0.5 * (forward[column_axis][row_axis] - backward[column_axis][row_axis])
            for column_axis in range(3)
        ]
        for row_axis in range(3)
    ]
    squared = [
        [
            gradient[row_axis][0] * gradient[0][column_axis]
            + gradient[row_axis][1] * gradient[1][column_axis]
            + gradient[row_axis][2] * gradient[2][column_axis]
            for column_axis in range(3)
        ]
        for row_axis in range(3)
    ]
    trace_sq = squared[0][0] + squared[1][1] + squared[2][2]
    strain_norm = 0.0
    deviator_norm = 0.0
    for row_axis in range(3):
        for column_axis in range(3):
            strain = 0.5 * (gradient[row_axis][column_axis] + gradient[column_axis][row_axis])
            deviator = 0.5 * (squared[row_axis][column_axis] + squared[column_axis][row_axis])
            if row_axis == column_axis:
                deviator = deviator - trace_sq / 3.0
            strain_norm = strain_norm + strain * strain
            deviator_norm = deviator_norm + deviator * deviator
    root_dev = jnp.sqrt(deviator_norm)
    eddy_viscosity = (
        WALE_COEFF
        * WALE_COEFF
        * deviator_norm
        * root_dev
        / (
            strain_norm * strain_norm * jnp.sqrt(strain_norm)
            + deviator_norm * jnp.sqrt(root_dev)
            + WALE_FLOOR
        )
    )
    return 0.5 + 3.0 * (BASE_VISCOSITY + eddy_viscosity)


def collide(state, relaxation):
    density = state[0]
    momentum = state[1:4]
    retained = 1.0 - 1.0 / relaxation
    members = [density, momentum[0], momentum[1], momentum[2]]
    for column, stress_pair in enumerate(STRESS_PAIRS):
        left_axis, right_axis = stress_pair
        balance = momentum[left_axis] * momentum[right_axis] / density
        if left_axis == right_axis:
            balance = balance + density / 3.0
        members.append(balance + retained * (state[4 + column] - balance))
    return jnp.stack(members)


def stream(post_pad, directions, recon_table, moment_table):
    size_a = post_pad.shape[1] - 2
    size_b = post_pad.shape[2] - 2
    size_c = post_pad.shape[3] - 2
    populations = jnp.einsum(
        "qm,mxyz->qxyz", recon_table, post_pad, precision=lax.Precision.HIGHEST
    )
    pieces = []
    for number in range(19):
        start_a = 1 - int(directions[number][0])
        start_b = 1 - int(directions[number][1])
        start_c = 1 - int(directions[number][2])
        pieces.append(
            populations[
                number,
                start_a : start_a + size_a,
                start_b : start_b + size_b,
                start_c : start_c + size_c,
            ]
        )
    moved = jnp.stack(pieces)
    return jnp.einsum("mq,qxyz->mxyz", moment_table, moved, precision=lax.Precision.HIGHEST)


def rest_solids(state, fluid):
    density = state[0]
    members = [density, state[1] * fluid, state[2] * fluid, state[3] * fluid]
    for column, stress_pair in enumerate(STRESS_PAIRS):
        if stress_pair[0] == stress_pair[1]:
            members.append(fluid * state[4 + column] + (1.0 - fluid) * density / 3.0)
        else:
            members.append(fluid * state[4 + column])
    return jnp.stack(members)


def per_device(density, velocity, solid, owner_map, slot_map):
    fluid = 1.0 - solid.astype(jnp.float32)
    directions, recon_table, moment_table = lattice_tables()
    state = initial_state(density, velocity, fluid)
    relaxation = density
    for step in range(ITERS):
        speed = state[1:4] / state[0]
        speed_pad = with_halo(speed, (("gx", 3), ("gy", 2), ("gz", 1)), 1)
        relaxation = wale_relaxation(speed_pad)
        post = collide(state, relaxation)
        post_pad = with_halo(post, (("gx", 3), ("gy", 2), ("gz", 1)), 1)
        read = stream(post_pad, directions, recon_table, moment_table)
        state = rest_solids(read, fluid)
    half_z = state.shape[1] // 2
    half_y = state.shape[2] // 2
    half_x = state.shape[3] // 2
    block_count = owner_map.shape[3]
    layer_count = half_x // block_count
    restricted = state.reshape(10, half_z, 2, half_y, 2, half_x, 2).mean(axis=(2, 4, 6))
    blocks = restricted.reshape(10, half_z, half_y, block_count, layer_count).transpose(
        3, 0, 1, 2, 4
    )
    blocks = blocks.reshape(block_count, -1)
    block_width = blocks.shape[1]
    owners = owner_map.reshape(block_count)
    slots = slot_map.reshape(block_count)
    span_y = lax.axis_size("gy")
    span_z = lax.axis_size("gz")
    owner_count = span_y * span_z
    capacity = 2 * block_count // owner_count
    block_ids = jnp.arange(block_count, dtype=jnp.int32)
    earlier = (owners[:, None] == owners[None, :]) & (block_ids[None, :] < block_ids[:, None])
    ranks = jnp.sum(earlier.astype(jnp.int32), axis=1)
    position = owners * capacity + ranks
    buffer_ids = jnp.arange(owner_count * capacity, dtype=jnp.int32)
    placing = buffer_ids[:, None] == position[None, :]
    outgoing = jnp.dot(placing.astype(jnp.float32), blocks, precision=lax.Precision.HIGHEST)
    out_tags = jnp.sum(jnp.where(placing, slots[None, :] + 1, 0), axis=1) - 1
    arrived, arrived_tags = (
        lax.all_to_all(
            outgoing.reshape(owner_count, capacity, block_width),
            ("gy", "gz"),
            split_axis=0,
            concat_axis=0,
            tiled=True,
        ),
        lax.all_to_all(
            out_tags.reshape(owner_count, capacity),
            ("gy", "gz"),
            split_axis=0,
            concat_axis=0,
            tiled=True,
        ),
    )
    slot_ids = jnp.arange(SLOTS, dtype=jnp.int32)
    summing = (slot_ids[:, None] == arrived_tags.reshape(-1)[None, :]).astype(jnp.float32)
    coarse = jnp.dot(summing, arrived.reshape(-1, block_width), precision=lax.Precision.HIGHEST)
    return (state, relaxation, coarse.reshape(1, 1, 1, SLOTS, block_width))


def solution(mesh):
    return jax.shard_map(
        per_device,
        mesh=mesh,
        in_specs=(
            P("gz", "gy", "gx"),
            P(None, "gz", "gy", "gx"),
            P("gz", "gy", "gx"),
            P("gx", "gy", "gz", None, None),
            P("gx", "gy", "gz", None, None),
        ),
        out_specs=(P(None, "gz", "gy", "gx"), P("gz", "gy", "gx"), P("gx", "gy", "gz", None, None)),
        check_vma=False,
    )
```

profile of v0, /device:TPU:1, one launch (start us, length us, event | category | flops | bytes accessed | tf_op | source)
XLA Modules:
  0.0 207.9 jit_solution(12705431242408874024)
XLA Ops:
  2.4 4.8 %collective-permute-start = (f32[3,8,8,1]{3,2,1,0:T(8,128)S(1)}, f32[3,8,8,1]{3,2,1,0:T(8,128)S(1)}, u32[]{:S(2)}, u32[]{:S(2)}) collective-permute-start(f32[3,8,8,1]{3,2,1,0:T(8,128)S(1)} %get-tuple-element.113), channel_id=1, source_target_pairs={{0,64},{64,128},{128,192},{192,256},{256,320},{320,384},{384,448},... | collective-permute-start | bytes 2312 | tf_op jit(solution)/shard_map/ppermute | solution.py:24
  7.3 8.6 %collective-permute-start.1 = (f32[3,8,8,1]{3,2,1,0:T(8,128)S(1)}, f32[3,8,8,1]{3,2,1,0:T(8,128)S(1)}, u32[]{:S(2)}, u32[]{:S(2)}) collective-permute-start(f32[3,8,8,1]{3,2,1,0:T(8,128)S(1)} %get-tuple-element.112), channel_id=1, source_target_pairs={{64,0},{128,64},{192,128},{256,192},{320,256},{384,320},{448,384},... | collective-permute-start | bytes 2312 | tf_op jit(solution)/shard_map/ppermute | solution.py:26
  17.7 2.6 %collective-permute-start.2 = (f32[3,8,1,130]{3,2,1,0:T(1,128)S(1)}, f32[3,8,1,130]{3,2,1,0:T(1,128)S(1)}, u32[]{:S(2)}, u32[]{:S(2)}) collective-permute-start(f32[3,8,1,130]{3,2,1,0:T(1,128)S(1)} %get-tuple-element.104), channel_id=1, source_target_pairs={{0,8},{8,16},{16,24},{24,32},{32,40},{40,48},{48,56},{56,0},{1,9},... | collective-permute-start | bytes 37448 | tf_op jit(solution)/shard_map/ppermute | solution.py:24
  21.3 2.3 %collective-permute-done.3 = f32[3,8,1,130]{3,2,1,0:T(1,128)S(1)} collective-permute-done((f32[3,8,1,130]{3,2,1,0:T(1,128)S(1)}, f32[3,8,1,130]{3,2,1,0:T(1,128)S(1)}, u32[]{:S(2)}, u32[]{:S(2)}) %collective-permute-start.3) | collective-permute-done | bytes 12512 | tf_op jit(solution)/shard_map/ppermute | solution.py:26
  23.7 5.1 %collective-permute-start.4 = (f32[3,1,10,130]{3,2,1,0:T(8,128)S(1)}, f32[3,1,10,130]{3,2,1,0:T(8,128)S(1)}, u32[]{:S(2)}, u32[]{:S(2)}) collective-permute-start(f32[3,1,10,130]{3,2,1,0:T(8,128)S(1)} %get-tuple-element.97), channel_id=1, source_target_pairs={{1,0},{2,1},{3,2},{4,3},{5,4},{6,5},{7,6},{0,7},{9,8},{10,9},{11,1... | collective-permute-start | bytes 46808 | tf_op jit(solution)/shard_map/ppermute | solution.py:26
  28.8 1.9 collective-permute-start.5
  30.8 4.0 %collective-permute-done.5 = f32[3,1,10,130]{3,2,1,0:T(8,128)S(1)} collective-permute-done((f32[3,1,10,130]{3,2,1,0:T(8,128)S(1)}, f32[3,1,10,130]{3,2,1,0:T(8,128)S(1)}, u32[]{:S(2)}, u32[]{:S(2)}) %collective-permute-start.5) | collective-permute-done | bytes 15632 | tf_op jit(solution)/shard_map/ppermute | solution.py:24
  36.0 1.9 collective-permute-start.6
  37.9 5.2 %collective-permute-start.7 = (f32[10,8,8,1]{3,0,2,1:T(8,128)S(1)}, f32[10,8,8,1]{3,0,2,1:T(8,128)S(1)}, u32[]{:S(2)}, u32[]{:S(2)}) collective-permute-start(f32[10,8,8,1]{3,0,2,1:T(8,128)S(1)} %get-tuple-element.94), channel_id=1, source_target_pairs={{64,0},{128,64},{192,128},{256,192},{320,256},{384,320},{448,384},... | collective-permute-start | bytes 7688 | tf_op jit(solution)/shard_map/ppermute | solution.py:26
  43.3 8.5 %collective-permute-done.6 = f32[10,8,8,1]{3,0,2,1:T(8,128)S(1)} collective-permute-done((f32[10,8,8,1]{3,0,2,1:T(8,128)S(1)}, f32[10,8,8,1]{3,0,2,1:T(8,128)S(1)}, u32[]{:S(2)}, u32[]{:S(2)}) %collective-permute-start.6) | collective-permute-done | bytes 2592 | tf_op jit(solution)/shard_map/ppermute | solution.py:24
  52.9 3.8 %collective-permute-start.8 = (f32[10,8,1,130]{3,0,2,1:T(8,128)S(1)}, f32[10,8,1,130]{3,0,2,1:T(8,128)S(1)}, u32[]{:S(2)}, u32[]{:S(2)}) collective-permute-start(f32[10,8,1,130]{3,0,2,1:T(8,128)S(1)} %get-tuple-element.67), channel_id=1, source_target_pairs={{0,8},{8,16},{16,24},{24,32},{32,40},{40,48},{48,56},{56,0},{1,9},... | collective-permute-start | bytes 124808 | tf_op jit(solution)/shard_map/ppermute | solution.py:24
  56.7 1.9 collective-permute-done.8
  58.7 2.4 %collective-permute-done.9 = f32[10,8,1,130]{3,0,2,1:T(8,128)S(1)} collective-permute-done((f32[10,8,1,130]{3,0,2,1:T(8,128)S(1)}, f32[10,8,1,130]{3,0,2,1:T(8,128)S(1)}, u32[]{:S(2)}, u32[]{:S(2)}) %collective-permute-start.9) | collective-permute-done | bytes 41632 | tf_op jit(solution)/shard_map/ppermute | solution.py:26
  61.3 1.9 collective-permute-start.10
  63.2 4.6 %collective-permute-start.11 = (f32[10,1,10,130]{3,0,2,1:T(8,128)S(1)}, f32[10,1,10,130]{3,0,2,1:T(8,128)S(1)}, u32[]{:S(2)}, u32[]{:S(2)}) collective-permute-start(f32[10,1,10,130]{3,0,2,1:T(8,128)S(1)} %get-tuple-element.66), channel_id=1, source_target_pairs={{1,0},{2,1},{3,2},{4,3},{5,4},{6,5},{7,6},{0,7},{9,8},{10,9},{11,1... | collective-permute-start | bytes 156008 | tf_op jit(solution)/shard_map/ppermute | solution.py:26
  67.8 2.5 %collective-permute-done.10 = f32[10,1,10,130]{3,0,2,1:T(8,128)S(1)} collective-permute-done((f32[10,1,10,130]{3,0,2,1:T(8,128)S(1)}, f32[10,1,10,130]{3,0,2,1:T(8,128)S(1)}, u32[]{:S(2)}, u32[]{:S(2)}) %collective-permute-start.10) | collective-permute-done | bytes 52032 | tf_op jit(solution)/shard_map/ppermute | solution.py:24
  71.2 2.3 %fusion = f32[19,10,10,130]{3,0,2,1:T(8,128)S(1)} fusion(f32[19,10,1,1]{0,1,3,2:T(8,128)S(1)} %copy-done.4, f32[10,1,10,130]{3,0,2,1:T(8,128)S(1)} %collective-permute-done.11, f32[10,8,1,130]{3,0,2,1:T(8,128)S(1)} %collective-permute-done.9, f32[10,8,8,1]{3,0,2,1:T(8,128)S(1)} %collective-permute-done.7, f32[10,8,8,128]{3,0,2,1:T(8,128)S(1)} %stack.137, ...), kind=kOutput, calls=%fused_computation | convolution fusion | flops 30420000 | bytes 1508760 | tf_op jit(solution)/shard_map/qm,mxyz->qxyz/dot_general | solution.py:162
  76.5 3.7 %collective-permute-start.12 = (f32[3,8,8,1]{3,2,1,0:T(8,128)S(1)}, f32[3,8,8,1]{3,2,1,0:T(8,128)S(1)}, u32[]{:S(2)}, u32[]{:S(2)}) collective-permute-start(f32[3,8,8,1]{3,2,1,0:T(8,128)S(1)} %get-tuple-element.111), channel_id=1, source_target_pairs={{0,64},{64,128},{128,192},{192,256},{256,320},{320,384},{384,448},... | collective-permute-start | bytes 2312 | tf_op jit(solution)/shard_map/ppermute | solution.py:24
  80.2 3.5 %collective-permute-start.13 = (f32[3,8,8,1]{3,2,1,0:T(8,128)S(1)}, f32[3,8,8,1]{3,2,1,0:T(8,128)S(1)}, u32[]{:S(2)}, u32[]{:S(2)}) collective-permute-start(f32[3,8,8,1]{3,2,1,0:T(8,128)S(1)} %get-tuple-element.110), channel_id=1, source_target_pairs={{64,0},{128,64},{192,128},{256,192},{320,256},{384,320},{448,384},... | collective-permute-start | bytes 2312 | tf_op jit(solution)/shard_map/ppermute | solution.py:26
  83.8 1.8 collective-permute-done.13
  85.8 3.1 %collective-permute-start.14 = (f32[3,8,1,130]{3,2,1,0:T(1,128)S(1)}, f32[3,8,1,130]{3,2,1,0:T(1,128)S(1)}, u32[]{:S(2)}, u32[]{:S(2)}) collective-permute-start(f32[3,8,1,130]{3,2,1,0:T(1,128)S(1)} %get-tuple-element.102), channel_id=1, source_target_pairs={{0,8},{8,16},{16,24},{24,32},{32,40},{40,48},{48,56},{56,0},{1,9},... | collective-permute-start | bytes 37448 | tf_op jit(solution)/shard_map/ppermute | solution.py:24
  89.9 2.5 %collective-permute-done.15 = f32[3,8,1,130]{3,2,1,0:T(1,128)S(1)} collective-permute-done((f32[3,8,1,130]{3,2,1,0:T(1,128)S(1)}, f32[3,8,1,130]{3,2,1,0:T(1,128)S(1)}, u32[]{:S(2)}, u32[]{:S(2)}) %collective-permute-start.15) | collective-permute-done | bytes 12512 | tf_op jit(solution)/shard_map/ppermute | solution.py:26
  92.4 5.2 %collective-permute-start.16 = (f32[3,1,10,130]{3,2,1,0:T(8,128)S(1)}, f32[3,1,10,130]{3,2,1,0:T(8,128)S(1)}, u32[]{:S(2)}, u32[]{:S(2)}) collective-permute-start(f32[3,1,10,130]{3,2,1,0:T(8,128)S(1)} %get-tuple-element.95), channel_id=1, source_target_pairs={{1,0},{2,1},{3,2},{4,3},{5,4},{6,5},{7,6},{0,7},{9,8},{10,9},{11,1... | collective-permute-start | bytes 46808 | tf_op jit(solution)/shard_map/ppermute | solution.py:26
  97.6 1.9 collective-permute-start.17
  99.6 4.1 %collective-permute-done.17 = f32[3,1,10,130]{3,2,1,0:T(8,128)S(1)} collective-permute-done((f32[3,1,10,130]{3,2,1,0:T(8,128)S(1)}, f32[3,1,10,130]{3,2,1,0:T(8,128)S(1)}, u32[]{:S(2)}, u32[]{:S(2)}) %collective-permute-start.17) | collective-permute-done | bytes 15632 | tf_op jit(solution)/shard_map/ppermute | solution.py:24
  104.4 3.4 %collective-permute-start.18 = (f32[10,8,8,1]{3,2,1,0:T(8,128)S(1)}, f32[10,8,8,1]{3,2,1,0:T(8,128)S(1)}, u32[]{:S(2)}, u32[]{:S(2)}) collective-permute-start(f32[10,8,8,1]{3,2,1,0:T(8,128)S(1)} %get-tuple-element.99), channel_id=1, source_target_pairs={{0,64},{64,128},{128,192},{192,256},{256,320},{320,384},{384,448},... | collective-permute-start | bytes 7688 | tf_op jit(solution)/shard_map/ppermute | solution.py:24
  107.8 3.1 %collective-permute-start.19 = (f32[10,8,8,1]{3,2,1,0:T(8,128)S(1)}, f32[10,8,8,1]{3,2,1,0:T(8,128)S(1)}, u32[]{:S(2)}, u32[]{:S(2)}) collective-permute-start(f32[10,8,8,1]{3,2,1,0:T(8,128)S(1)} %get-tuple-element.100), channel_id=1, source_target_pairs={{64,0},{128,64},{192,128},{256,192},{320,256},{384,320},{448,384},... | collective-permute-start | bytes 7688 | tf_op jit(solution)/shard_map/ppermute | solution.py:26
  111.0 3.7 %collective-permute-done.18 = f32[10,8,8,1]{3,2,1,0:T(8,128)S(1)} collective-permute-done((f32[10,8,8,1]{3,2,1,0:T(8,128)S(1)}, f32[10,8,8,1]{3,2,1,0:T(8,128)S(1)}, u32[]{:S(2)}, u32[]{:S(2)}) %collective-permute-start.18) | collective-permute-done | bytes 2592 | tf_op jit(solution)/shard_map/ppermute | solution.py:24
  114.8 1.8 collective-permute-done.19
  117.2 4.5 %collective-permute-start.20 = (f32[10,8,1,130]{3,2,1,0:T(1,128)S(1)}, f32[10,8,1,130]{3,2,1,0:T(1,128)S(1)}, u32[]{:S(2)}, u32[]{:S(2)}) collective-permute-start(f32[10,8,1,130]{3,2,1,0:T(1,128)S(1)} %get-tuple-element.71), channel_id=1, source_target_pairs={{0,8},{8,16},{16,24},{24,32},{32,40},{40,48},{48,56},{56,0},{1,9},... | collective-permute-start | bytes 124808 | tf_op jit(solution)/shard_map/ppermute | solution.py:24
  122.4 8.0 %all-to-all-start = ((s32[64,1,2]{2,1,0:T(1,128)}), s32[64,1,2]{2,1,0:T(1,128)S(1)}, u32[]{:S(2)}, u32[]{:S(2)}) async-start(s32[64,1,2]{2,1,0:T(1,128)} %bitcast.88), calls=%async_computation | async-start | bytes 65536 | tf_op jit(solution)/shard_map/all_to_all | solution.py:239
  130.6 3.3 %collective-permute-start.22 = (f32[10,1,10,130]{3,2,1,0:T(8,128)S(1)}, f32[10,1,10,130]{3,2,1,0:T(8,128)S(1)}, u32[]{:S(2)}, u32[]{:S(2)}) collective-permute-start(f32[10,1,10,130]{3,2,1,0:T(8,128)S(1)} %get-tuple-element.69), channel_id=1, source_target_pairs={{0,1},{1,2},{2,3},{3,4},{4,5},{5,6},{6,7},{7,0},{8,9},{9,10},{10,1... | collective-permute-start | bytes 156008 | tf_op jit(solution)/shard_map/ppermute | solution.py:24
  133.9 3.4 %collective-permute-start.23 = (f32[10,1,10,130]{3,2,1,0:T(8,128)S(1)}, f32[10,1,10,130]{3,2,1,0:T(8,128)S(1)}, u32[]{:S(2)}, u32[]{:S(2)}) collective-permute-start(f32[10,1,10,130]{3,2,1,0:T(8,128)S(1)} %get-tuple-element.70), channel_id=1, source_target_pairs={{1,0},{2,1},{3,2},{4,3},{5,4},{6,5},{7,6},{0,7},{9,8},{10,9},{11,1... | collective-permute-start | bytes 156008 | tf_op jit(solution)/shard_map/ppermute | solution.py:26
  137.3 1.9 collective-permute-done.22
  141.5 2.5 %fusion.14 = f32[19,10,10,130]{3,0,2,1:T(8,128)S(1)} fusion(f32[19,10,1,1]{0,1,3,2:T(8,128)S(1)} %copy-done.4, f32[10,10,10,130]{3,2,1,0:T(8,128)S(1)} %pad_maximum_fusion), kind=kOutput, calls=%fused_computation.15 | convolution fusion | flops 29640000 | bytes 1508760 | tf_op jit(solution)/shard_map/qm,mxyz->qxyz/dot_general | solution.py:162
  147.5 2.1 %stack.161 = f32[1,4,2,4,2,64,2]{6,5,4,3,2,1,0:T(8,128)S(1)} reshape(f32[1,8,8,128]{3,2,1,0:T(8,128)S(1)} %bitcast.373) | data formatting | bytes 65536 | tf_op jit(solution)/shard_map/stack | solution.py:190
  150.2 3.4 %stack.162 = f32[1,4,2,4,2,64,2]{6,5,4,3,2,1,0:T(8,128)} reshape(f32[8,8,128]{2,1,0:T(8,128)S(1)} %get-tuple-element.20) | data formatting | bytes 65536 | tf_op jit(solution)/shard_map/stack | solution.py:190
  153.6 2.3 %copy.135 = f32[1,4,2,4,2,64,2]{5,3,6,4,2,1,0:T(4,128)S(1)} copy(f32[1,4,2,4,2,64,2]{6,5,4,3,2,1,0:T(8,128)} %stack.162) | data formatting | bytes 65536 | tf_op jit(solution)/shard_map/stack | solution.py:190
  157.2 2.1 %stack.163 = f32[1,4,2,4,2,64,2]{6,5,4,3,2,1,0:T(8,128)S(1)} reshape(f32[8,8,128]{2,1,0:T(8,128)S(1)} %get-tuple-element.18) | data formatting | bytes 65536 | tf_op jit(solution)/shard_map/stack | solution.py:190
  160.6 2.1 %stack.164 = f32[1,4,2,4,2,64,2]{6,5,4,3,2,1,0:T(8,128)S(1)} reshape(f32[8,8,128]{2,1,0:T(8,128)S(1)} %get-tuple-element.16) | data formatting | bytes 65536 | tf_op jit(solution)/shard_map/stack | solution.py:190
  164.2 2.1 %stack.165 = f32[1,4,2,4,2,64,2]{6,5,4,3,2,1,0:T(8,128)S(1)} reshape(f32[8,8,128]{2,1,0:T(8,128)S(1)} %get-tuple-element.14) | data formatting | bytes 65536 | tf_op jit(solution)/shard_map/stack | solution.py:190
  167.7 2.1 %stack.166 = f32[1,4,2,4,2,64,2]{6,5,4,3,2,1,0:T(8,128)S(1)} reshape(f32[8,8,128]{2,1,0:T(8,128)S(1)} %get-tuple-element.12) | data formatting | bytes 65536 | tf_op jit(solution)/shard_map/stack | solution.py:190
  171.1 2.1 %stack.167 = f32[1,4,2,4,2,64,2]{6,5,4,3,2,1,0:T(8,128)S(1)} reshape(f32[8,8,128]{2,1,0:T(8,128)S(1)} %get-tuple-element.10) | data formatting | bytes 65536 | tf_op jit(solution)/shard_map/stack | solution.py:190
  174.5 2.1 %stack.168 = f32[1,4,2,4,2,64,2]{6,5,4,3,2,1,0:T(8,128)S(1)} reshape(f32[8,8,128]{2,1,0:T(8,128)S(1)} %get-tuple-element.8) | data formatting | bytes 65536 | tf_op jit(solution)/shard_map/stack | solution.py:190
  177.9 2.1 %stack.169 = f32[1,4,2,4,2,64,2]{6,5,4,3,2,1,0:T(8,128)S(1)} reshape(f32[8,8,128]{2,1,0:T(8,128)S(1)} %get-tuple-element.6) | data formatting | bytes 65536 | tf_op jit(solution)/shard_map/stack | solution.py:190
  181.3 2.1 %stack.170 = f32[1,4,2,4,2,64,2]{6,5,4,3,2,1,0:T(8,128)S(1)} reshape(f32[8,8,128]{2,1,0:T(8,128)S(1)} %get-tuple-element.4) | data formatting | bytes 65536 | tf_op jit(solution)/shard_map/stack | solution.py:190
  185.5 11.6 %all-to-all-start.1 = ((f32[64,2,160]{2,1,0:T(2,128)}), f32[64,2,160]{2,1,0:T(2,128)S(1)}, u32[]{:S(2)}, u32[]{:S(2)}) async-start(f32[64,2,160]{2,1,0:T(2,128)} %copy.145), calls=%async_computation.1 | async-start | bytes 262144 | tf_op jit(solution)/shard_map/all_to_all | solution.py:232
  198.5 8.6 %all-to-all-done.1 = f32[64,2,160]{2,1,0:T(2,128)S(1)} async-done(((f32[64,2,160]{2,1,0:T(2,128)}), f32[64,2,160]{2,1,0:T(2,128)S(1)}, u32[]{:S(2)}, u32[]{:S(2)}) %all-to-all-start.1) | async-done | bytes 81952 | tf_op jit(solution)/shard_map/all_to_all | solution.py:232
  (115 shorter events, 36.1 us)
Async XLA Ops:
  0.6 34.2 %copy-start.2 = (f32[8,8,128]{2,1,0:T(8,128)S(1)}, f32[8,8,128]{2,1,0:T(8,128)}, u32[]{:S(2)}) copy-start(f32[8,8,128]{2,1,0:T(8,128)} %param.7) | copy-start | bytes 98308
  2.4 14.0 %collective-permute-start = (f32[3,8,8,1]{3,2,1,0:T(8,128)S(1)}, f32[3,8,8,1]{3,2,1,0:T(8,128)S(1)}, u32[]{:S(2)}, u32[]{:S(2)}) collective-permute-start(f32[3,8,8,1]{3,2,1,0:T(8,128)S(1)} %get-tuple-element.113), channel_id=1, source_target_pairs={{0,64},{64,128},{128,192},{192,256},{256,320},{320,384},{384,448},... | collective-permute-start | bytes 2312 | tf_op jit(solution)/shard_map/ppermute | solution.py:24
  7.3 10.2 %collective-permute-start.1 = (f32[3,8,8,1]{3,2,1,0:T(8,128)S(1)}, f32[3,8,8,1]{3,2,1,0:T(8,128)S(1)}, u32[]{:S(2)}, u32[]{:S(2)}) collective-permute-start(f32[3,8,8,1]{3,2,1,0:T(8,128)S(1)} %get-tuple-element.112), channel_id=1, source_target_pairs={{64,0},{128,64},{192,128},{256,192},{320,256},{384,320},{448,384},... | collective-permute-start | bytes 2312 | tf_op jit(solution)/shard_map/ppermute | solution.py:26
  17.7 3.6 %collective-permute-start.2 = (f32[3,8,1,130]{3,2,1,0:T(1,128)S(1)}, f32[3,8,1,130]{3,2,1,0:T(1,128)S(1)}, u32[]{:S(2)}, u32[]{:S(2)}) collective-permute-start(f32[3,8,1,130]{3,2,1,0:T(1,128)S(1)} %get-tuple-element.104), channel_id=1, source_target_pairs={{0,8},{8,16},{16,24},{24,32},{32,40},{40,48},{48,56},{56,0},{1,9},... | collective-permute-start | bytes 37448 | tf_op jit(solution)/shard_map/ppermute | solution.py:24
  20.3 3.3 %collective-permute-start.3 = (f32[3,8,1,130]{3,2,1,0:T(1,128)S(1)}, f32[3,8,1,130]{3,2,1,0:T(1,128)S(1)}, u32[]{:S(2)}, u32[]{:S(2)}) collective-permute-start(f32[3,8,1,130]{3,2,1,0:T(1,128)S(1)} %get-tuple-element.103), channel_id=1, source_target_pairs={{8,0},{16,8},{24,16},{32,24},{40,32},{48,40},{56,48},{0,56},{9,1},... | collective-permute-start | bytes 37448 | tf_op jit(solution)/shard_map/ppermute | solution.py:26
  23.7 7.1 %collective-permute-start.4 = (f32[3,1,10,130]{3,2,1,0:T(8,128)S(1)}, f32[3,1,10,130]{3,2,1,0:T(8,128)S(1)}, u32[]{:S(2)}, u32[]{:S(2)}) collective-permute-start(f32[3,1,10,130]{3,2,1,0:T(8,128)S(1)} %get-tuple-element.97), channel_id=1, source_target_pairs={{1,0},{2,1},{3,2},{4,3},{5,4},{6,5},{7,6},{0,7},{9,8},{10,9},{11,1... | collective-permute-start | bytes 46808 | tf_op jit(solution)/shard_map/ppermute | solution.py:26
  28.8 6.0 %collective-permute-start.5 = (f32[3,1,10,130]{3,2,1,0:T(8,128)S(1)}, f32[3,1,10,130]{3,2,1,0:T(8,128)S(1)}, u32[]{:S(2)}, u32[]{:S(2)}) collective-permute-start(f32[3,1,10,130]{3,2,1,0:T(8,128)S(1)} %get-tuple-element.98), channel_id=1, source_target_pairs={{0,1},{1,2},{2,3},{3,4},{4,5},{5,6},{6,7},{7,0},{8,9},{9,10},{10,1... | collective-permute-start | bytes 46808 | tf_op jit(solution)/shard_map/ppermute | solution.py:24
  35.3 7.9 %copy-start.5 = (s32[1,1,1,64,1]{3,4,2,1,0:T(1,128)S(1)}, s32[1,1,1,64,1]{3,4,2,1,0:T(1,128)}, u32[]{:S(2)}) copy-start(s32[1,1,1,64,1]{3,4,2,1,0:T(1,128)} %param.10) | copy-start | bytes 772
  36.0 15.9 %collective-permute-start.6 = (f32[10,8,8,1]{3,0,2,1:T(8,128)S(1)}, f32[10,8,8,1]{3,0,2,1:T(8,128)S(1)}, u32[]{:S(2)}, u32[]{:S(2)}) collective-permute-start(f32[10,8,8,1]{3,0,2,1:T(8,128)S(1)} %get-tuple-element.93), channel_id=1, source_target_pairs={{0,64},{64,128},{128,192},{192,256},{256,320},{320,384},{384,448},... | collective-permute-start | bytes 7688 | tf_op jit(solution)/shard_map/ppermute | solution.py:24
  37.9 14.9 %collective-permute-start.7 = (f32[10,8,8,1]{3,0,2,1:T(8,128)S(1)}, f32[10,8,8,1]{3,0,2,1:T(8,128)S(1)}, u32[]{:S(2)}, u32[]{:S(2)}) collective-permute-start(f32[10,8,8,1]{3,0,2,1:T(8,128)S(1)} %get-tuple-element.94), channel_id=1, source_target_pairs={{64,0},{128,64},{192,128},{256,192},{320,256},{384,320},{448,384},... | collective-permute-start | bytes 7688 | tf_op jit(solution)/shard_map/ppermute | solution.py:26
  43.3 24.5 %copy-start.6 = (s32[1,1,1,64,1]{3,4,2,1,0:T(1,128)S(1)}, s32[1,1,1,64,1]{3,4,2,1,0:T(1,128)}, u32[]{:S(2)}) copy-start(s32[1,1,1,64,1]{3,4,2,1,0:T(1,128)} %param.11) | copy-start | bytes 772
  43.3 27.8 %copy-start.4 = (f32[19,10,1,1]{0,1,3,2:T(8,128)S(1)}, f32[19,10,1,1]{0,1,3,2:T(8,128)}, u32[]{:S(2)}) copy-start(f32[19,10,1,1]{0,1,3,2:T(8,128)} %constant.43) | copy-start | bytes 2284
  52.9 5.7 %collective-permute-start.8 = (f32[10,8,1,130]{3,0,2,1:T(8,128)S(1)}, f32[10,8,1,130]{3,0,2,1:T(8,128)S(1)}, u32[]{:S(2)}, u32[]{:S(2)}) collective-permute-start(f32[10,8,1,130]{3,0,2,1:T(8,128)S(1)} %get-tuple-element.67), channel_id=1, source_target_pairs={{0,8},{8,16},{16,24},{24,32},{32,40},{40,48},{48,56},{56,0},{1,9},... | collective-permute-start | bytes 124808 | tf_op jit(solution)/shard_map/ppermute | solution.py:24
  56.7 4.4 %collective-permute-start.9 = (f32[10,8,1,130]{3,0,2,1:T(8,128)S(1)}, f32[10,8,1,130]{3,0,2,1:T(8,128)S(1)}, u32[]{:S(2)}, u32[]{:S(2)}) collective-permute-start(f32[10,8,1,130]{3,0,2,1:T(8,128)S(1)} %get-tuple-element.68), channel_id=1, source_target_pairs={{8,0},{16,8},{24,16},{32,24},{40,32},{48,40},{56,48},{0,56},{9,1},... | collective-permute-start | bytes 124808 | tf_op jit(solution)/shard_map/ppermute | solution.py:26
  61.3 9.0 %collective-permute-start.10 = (f32[10,1,10,130]{3,0,2,1:T(8,128)S(1)}, f32[10,1,10,130]{3,0,2,1:T(8,128)S(1)}, u32[]{:S(2)}, u32[]{:S(2)}) collective-permute-start(f32[10,1,10,130]{3,0,2,1:T(8,128)S(1)} %get-tuple-element.65), channel_id=1, source_target_pairs={{0,1},{1,2},{2,3},{3,4},{4,5},{5,6},{6,7},{7,0},{8,9},{9,10},{10,1... | collective-permute-start | bytes 156008 | tf_op jit(solution)/shard_map/ppermute | solution.py:24
  63.2 8.0 %collective-permute-start.11 = (f32[10,1,10,130]{3,0,2,1:T(8,128)S(1)}, f32[10,1,10,130]{3,0,2,1:T(8,128)S(1)}, u32[]{:S(2)}, u32[]{:S(2)}) collective-permute-start(f32[10,1,10,130]{3,0,2,1:T(8,128)S(1)} %get-tuple-element.66), channel_id=1, source_target_pairs={{1,0},{2,1},{3,2},{4,3},{5,4},{6,5},{7,6},{0,7},{9,8},{10,9},{11,1... | collective-permute-start | bytes 156008 | tf_op jit(solution)/shard_map/ppermute | solution.py:26
  73.5 2.0 copy-start.3
  74.6 1.8 copy-start
  76.5 7.3 %collective-permute-start.12 = (f32[3,8,8,1]{3,2,1,0:T(8,128)S(1)}, f32[3,8,8,1]{3,2,1,0:T(8,128)S(1)}, u32[]{:S(2)}, u32[]{:S(2)}) collective-permute-start(f32[3,8,8,1]{3,2,1,0:T(8,128)S(1)} %get-tuple-element.111), channel_id=1, source_target_pairs={{0,64},{64,128},{128,192},{192,256},{256,320},{320,384},{384,448},... | collective-permute-start | bytes 2312 | tf_op jit(solution)/shard_map/ppermute | solution.py:24
  80.2 5.4 %collective-permute-start.13 = (f32[3,8,8,1]{3,2,1,0:T(8,128)S(1)}, f32[3,8,8,1]{3,2,1,0:T(8,128)S(1)}, u32[]{:S(2)}, u32[]{:S(2)}) collective-permute-start(f32[3,8,8,1]{3,2,1,0:T(8,128)S(1)} %get-tuple-element.110), channel_id=1, source_target_pairs={{64,0},{128,64},{192,128},{256,192},{320,256},{384,320},{448,384},... | collective-permute-start | bytes 2312 | tf_op jit(solution)/shard_map/ppermute | solution.py:26
  85.8 4.1 %collective-permute-start.14 = (f32[3,8,1,130]{3,2,1,0:T(1,128)S(1)}, f32[3,8,1,130]{3,2,1,0:T(1,128)S(1)}, u32[]{:S(2)}, u32[]{:S(2)}) collective-permute-start(f32[3,8,1,130]{3,2,1,0:T(1,128)S(1)} %get-tuple-element.102), channel_id=1, source_target_pairs={{0,8},{8,16},{16,24},{24,32},{32,40},{40,48},{48,56},{56,0},{1,9},... | collective-permute-start | bytes 37448 | tf_op jit(solution)/shard_map/ppermute | solution.py:24
  88.9 3.4 %collective-permute-start.15 = (f32[3,8,1,130]{3,2,1,0:T(1,128)S(1)}, f32[3,8,1,130]{3,2,1,0:T(1,128)S(1)}, u32[]{:S(2)}, u32[]{:S(2)}) collective-permute-start(f32[3,8,1,130]{3,2,1,0:T(1,128)S(1)} %get-tuple-element.101), channel_id=1, source_target_pairs={{8,0},{16,8},{24,16},{32,24},{40,32},{48,40},{56,48},{0,56},{9,1},... | collective-permute-start | bytes 37448 | tf_op jit(solution)/shard_map/ppermute | solution.py:26
  92.4 7.1 %collective-permute-start.16 = (f32[3,1,10,130]{3,2,1,0:T(8,128)S(1)}, f32[3,1,10,130]{3,2,1,0:T(8,128)S(1)}, u32[]{:S(2)}, u32[]{:S(2)}) collective-permute-start(f32[3,1,10,130]{3,2,1,0:T(8,128)S(1)} %get-tuple-element.95), channel_id=1, source_target_pairs={{1,0},{2,1},{3,2},{4,3},{5,4},{6,5},{7,6},{0,7},{9,8},{10,9},{11,1... | collective-permute-start | bytes 46808 | tf_op jit(solution)/shard_map/ppermute | solution.py:26
  97.6 6.0 %collective-permute-start.17 = (f32[3,1,10,130]{3,2,1,0:T(8,128)S(1)}, f32[3,1,10,130]{3,2,1,0:T(8,128)S(1)}, u32[]{:S(2)}, u32[]{:S(2)}) collective-permute-start(f32[3,1,10,130]{3,2,1,0:T(8,128)S(1)} %get-tuple-element.96), channel_id=1, source_target_pairs={{0,1},{1,2},{2,3},{3,4},{4,5},{5,6},{6,7},{7,0},{8,9},{9,10},{10,1... | collective-permute-start | bytes 46808 | tf_op jit(solution)/shard_map/ppermute | solution.py:24
  104.1 13.1 %copy-start.1 = (f32[8,8,128]{2,1,0:T(8,128)}, f32[8,8,128]{2,1,0:T(8,128)S(1)}, u32[]{:S(2)}) copy-start(f32[8,8,128]{2,1,0:T(8,128)S(1)} %get-tuple-element.22) | copy-start | bytes 98308
  104.4 10.3 %collective-permute-start.18 = (f32[10,8,8,1]{3,2,1,0:T(8,128)S(1)}, f32[10,8,8,1]{3,2,1,0:T(8,128)S(1)}, u32[]{:S(2)}, u32[]{:S(2)}) collective-permute-start(f32[10,8,8,1]{3,2,1,0:T(8,128)S(1)} %get-tuple-element.99), channel_id=1, source_target_pairs={{0,64},{64,128},{128,192},{192,256},{256,320},{320,384},{384,448},... | collective-permute-start | bytes 7688 | tf_op jit(solution)/shard_map/ppermute | solution.py:24
  107.8 8.8 %collective-permute-start.19 = (f32[10,8,8,1]{3,2,1,0:T(8,128)S(1)}, f32[10,8,8,1]{3,2,1,0:T(8,128)S(1)}, u32[]{:S(2)}, u32[]{:S(2)}) collective-permute-start(f32[10,8,8,1]{3,2,1,0:T(8,128)S(1)} %get-tuple-element.100), channel_id=1, source_target_pairs={{64,0},{128,64},{192,128},{256,192},{320,256},{384,320},{448,384},... | collective-permute-start | bytes 7688 | tf_op jit(solution)/shard_map/ppermute | solution.py:26
  117.2 13.2 %collective-permute-start.20 = (f32[10,8,1,130]{3,2,1,0:T(1,128)S(1)}, f32[10,8,1,130]{3,2,1,0:T(1,128)S(1)}, u32[]{:S(2)}, u32[]{:S(2)}) collective-permute-start(f32[10,8,1,130]{3,2,1,0:T(1,128)S(1)} %get-tuple-element.71), channel_id=1, source_target_pairs={{0,8},{8,16},{16,24},{24,32},{32,40},{40,48},{48,56},{56,0},{1,9},... | collective-permute-start | bytes 124808 | tf_op jit(solution)/shard_map/ppermute | solution.py:24
  121.6 8.7 %collective-permute-start.21 = (f32[10,8,1,130]{3,2,1,0:T(1,128)S(1)}, f32[10,8,1,130]{3,2,1,0:T(1,128)S(1)}, u32[]{:S(2)}, u32[]{:S(2)}) collective-permute-start(f32[10,8,1,130]{3,2,1,0:T(1,128)S(1)} %get-tuple-element.72), channel_id=1, source_target_pairs={{8,0},{16,8},{24,16},{32,24},{40,32},{48,40},{56,48},{0,56},{9,1},... | collective-permute-start | bytes 124808 | tf_op jit(solution)/shard_map/ppermute | solution.py:26
  122.4 63.1 %all-to-all-start = ((s32[64,1,2]{2,1,0:T(1,128)}), s32[64,1,2]{2,1,0:T(1,128)S(1)}, u32[]{:S(2)}, u32[]{:S(2)}) async-start(s32[64,1,2]{2,1,0:T(1,128)} %bitcast.88), calls=%async_computation | async-start | bytes 65536 | tf_op jit(solution)/shard_map/all_to_all | solution.py:239
  130.6 8.6 %collective-permute-start.22 = (f32[10,1,10,130]{3,2,1,0:T(8,128)S(1)}, f32[10,1,10,130]{3,2,1,0:T(8,128)S(1)}, u32[]{:S(2)}, u32[]{:S(2)}) collective-permute-start(f32[10,1,10,130]{3,2,1,0:T(8,128)S(1)} %get-tuple-element.69), channel_id=1, source_target_pairs={{0,1},{1,2},{2,3},{3,4},{4,5},{5,6},{6,7},{7,0},{8,9},{9,10},{10,1... | collective-permute-start | bytes 156008 | tf_op jit(solution)/shard_map/ppermute | solution.py:24
  133.9 7.0 %collective-permute-start.23 = (f32[10,1,10,130]{3,2,1,0:T(8,128)S(1)}, f32[10,1,10,130]{3,2,1,0:T(8,128)S(1)}, u32[]{:S(2)}, u32[]{:S(2)}) collective-permute-start(f32[10,1,10,130]{3,2,1,0:T(8,128)S(1)} %get-tuple-element.70), channel_id=1, source_target_pairs={{1,0},{2,1},{3,2},{4,3},{5,4},{6,5},{7,6},{0,7},{9,8},{10,9},{11,1... | collective-permute-start | bytes 156008 | tf_op jit(solution)/shard_map/ppermute | solution.py:26
  185.5 21.5 %all-to-all-start.1 = ((f32[64,2,160]{2,1,0:T(2,128)}), f32[64,2,160]{2,1,0:T(2,128)S(1)}, u32[]{:S(2)}, u32[]{:S(2)}) async-start(f32[64,2,160]{2,1,0:T(2,128)} %copy.145), calls=%async_computation.1 | async-start | bytes 262144 | tf_op jit(solution)/shard_map/all_to_all | solution.py:232
where the time goes:
time: 209 us; the launch traced here: 208 us
  starting transfers between devices  95.1 us (46%)
  waiting for transfers between devices  53.1 us (25%)
  local copies, waits for them, and re-layouts  39.3 us (19%)
  other arithmetic  12.1 us (6%)
  matrix products  6.95 us (3%)
    ppermute x12, starting transfers between devices, with_halo(): lax.ppermute(head, axis, [((i + 1) % count, i) for i in range(count)])  38.7 us
    ppermute x12, starting transfers between devices, with_halo(): lax.ppermute(tail, axis, [(i, (i + 1) % count) for i in range(count)])  36.9 us
    another operation x21, local copies, waits for them, and re-layouts, rest_solids(): return jnp.stack(members)  30.8 us
    ppermute x12, waiting for transfers between devices, with_halo(): lax.ppermute(tail, axis, [(i, (i + 1) % count) for i in range(count)])  29.2 us
    ppermute x12, waiting for transfers between devices, with_halo(): lax.ppermute(head, axis, [((i + 1) % count, i) for i in range(count)])  15.3 us
    all_to_all x1, starting transfers between devices, per_device(): lax.all_to_all(outgoing.reshape(owner_count, capacity, block_width), ('gy...  11.6 us
    all_to_all x1, waiting for transfers between devices, per_device(): lax.all_to_all(outgoing.reshape(owner_count, capacity, block_width), ('gy...  8.57 us
    all_to_all x1, starting transfers between devices, per_device(): lax.all_to_all(out_tags.reshape(owner_count, capacity), ('gy', 'gz'), spl...  7.96 us
  transfers between devices with their start and end apart: 26, of which 20 were waited for; matrix products, arithmetic and copies ran while one was open for 23% of the time, Pallas kernels for 0%

commit v1 on v0

v1 whole, which is shorter than its diff:
```python
import jax
import jax.numpy as jnp
from jax import lax
from jax.experimental import pallas as pl
from jax.experimental.pallas import tpu as pltpu
from jax.sharding import PartitionSpec as P

SLOTS = 16
WALE_COEFF = 0.5
BASE_VISCOSITY = 0.01
WALE_FLOOR = 1e-10
VMEM = pl.BlockSpec(memory_space=pltpu.VMEM)
PARAMS = pltpu.CompilerParams(vmem_limit_bytes=48 * 1024 * 1024)


def f32(*shape):
    return jax.ShapeDtypeStruct(shape, jnp.float32)


def roll(value, shift, axis):
    size = value.shape[axis]
    if isinstance(shift, int):
        shift = shift % size
        if shift == 0:
            return value
    return pltpu.roll(value, shift, axis)


def is_even(axis):
    return lax.rem(lax.axis_index(axis), 2) == 0


def swap(high_face, low_face, axis):
    count = lax.axis_size(axis)
    first = [(i, i ^ 1) for i in range(count)]
    second = [(i, (((i + 1) % count) ^ 1) - 1 if ((i + 1) % count) ^ 1 else count - 1) for i in range(count)]
    return lax.ppermute(high_face, axis, first), lax.ppermute(low_face, axis, second)


def pack_vertical(density, velocity, solid, first, second):
    even = is_even("gz")
    for out, upper in ((first, even), (second, jnp.logical_not(even))):
        planes = pl.ds(jnp.where(upper, 4, 0), 4)
        fluid = 1.0 - solid[planes].astype(jnp.float32)
        out[0] = density[planes]
        for axis in range(3):
            out[1 + axis] = velocity[axis, planes] * fluid
        out[4] = fluid


def pack_spanwise(density, velocity, solid, got_first, got_second, planes, first, second):
    even_z = is_even("gz")
    even_y = is_even("gy")
    fluid = 1.0 - solid[...].astype(jnp.float32)
    planes[0, 4:12] = density[...]
    for axis in range(3):
        planes[1 + axis, 4:12] = velocity[axis] * fluid
    planes[4, 4:12] = fluid
    for field in range(5):
        planes[field, 12:16] = jnp.where(even_z, got_first[field], got_second[field])
        planes[field, 0:4] = jnp.where(even_z, got_second[field], got_first[field])
    front = lax.broadcasted_iota(jnp.int32, (8, 128), 0) < 4
    for field in range(5):
        for pair in range(8):
            one = planes[field, 2 * pair]
            two = planes[field, 2 * pair + 1]
            high = jnp.where(front, roll(one, 4, 0), two)
            low = jnp.where(front, one, roll(two, 4, 0))
            first[field, pair] = jnp.where(even_y, high, low)
            second[field, pair] = jnp.where(even_y, low, high)


def pack_streamwise(planes, got_first, got_second, window, strip, first, second):
    even_y = is_even("gy")
    even_x = is_even("gx")
    front = lax.broadcasted_iota(jnp.int32, (8, 128), 0) < 4
    lane = lax.broadcasted_iota(jnp.int32, (16, 128), 1)
    group, spot = lane // 16, lane % 16
    for field in range(5):
        for pair in range(8):
            above = jnp.where(even_y, got_first[field, pair], got_second[field, pair])
            below = jnp.where(even_y, got_second[field, pair], got_first[field, pair])
            window[field, 2 * pair, 0:8] = planes[field, 2 * pair]
            window[field, 2 * pair + 1, 0:8] = planes[field, 2 * pair + 1]
            window[field, 2 * pair, 8:16] = jnp.where(front, above, roll(below, 4, 0))
            window[field, 2 * pair + 1, 8:16] = jnp.where(front, roll(above, 4, 0), below)
    quarter = lax.broadcasted_iota(jnp.int32, (8, 128), 1) % 16 // 4
    for field in range(5):
        to_right = jnp.zeros((8, 128), jnp.float32)
        to_left = jnp.zeros((8, 128), jnp.float32)
        for half in range(2):
            own = jnp.zeros((16, 128), jnp.float32)
            for number in range(8):
                cells = window[field, 2 * number + half]
                here = group == number
                own = jnp.where(here & (spot < 4), roll(cells, 16 * number + 4, 1), own)
                own = jnp.where(here & (spot >= 12), roll(cells, 16 * number + 12, 1), own)
            strip[field, half] = own
            for part in range(2):
                place = 2 * half + part
                rows = own[8 * part : 8 * part + 8]
                to_right = jnp.where(quarter == place, roll(rows, 4 * place, 1), to_right)
                to_left = jnp.where(quarter == place, roll(rows, 4 * place - 12, 1), to_left)
        first[field] = jnp.where(even_x, to_right, to_left)
        second[field] = jnp.where(even_x, to_left, to_right)


def wale(doubled):
    (g00, g01, g02), (g10, g11, g12), (g20, g21, g22) = doubled
    s01, s02, s12 = g01 + g10, g02 + g20, g12 + g21
    q0, q1, q2 = g00 * g00, g11 * g11, g22 * g22
    strain = 0.25 * ((q0 + q1 + q2) + 0.5 * (s01 * s01 + s02 * s02 + s12 * s12))
    p01, p02, p12 = g01 * g10, g02 * g20, g12 * g21
    d0, d1, d2 = q0 + (p01 + p02), q1 + (p01 + p12), q2 + (p02 + p12)
    third = (d0 + d1 + d2) * (1.0 / 3.0)
    d0, d1, d2 = d0 - third, d1 - third, d2 - third
    d01 = (g00 + g11) * s01 + (g02 * g21 + g12 * g20)
    d02 = (g00 + g22) * s02 + (g01 * g12 + g21 * g10)
    d12 = (g11 + g22) * s12 + (g10 * g02 + g20 * g01)
    deviator = 0.0625 * ((d0 * d0 + d1 * d1 + d2 * d2) + 0.5 * (d01 * d01 + d02 * d02 + d12 * d12))
    root = jnp.sqrt(deviator)
    eddy = (WALE_COEFF * WALE_COEFF) * deviator * root / (
        strain * strain * jnp.sqrt(strain) + deviator * jnp.sqrt(root) + WALE_FLOOR
    )
    return 0.5 + 3.0 * (BASE_VISCOSITY + eddy)


def collide(momentum, speed, stress, relaxation):
    retained = 1.0 - 1.0 / relaxation
    post = []
    for column, (one, two) in enumerate(((0, 0), (1, 1), (2, 2), (0, 1), (0, 2), (1, 2))):
        balance = momentum[one] * speed[two]
        post.append(balance + retained * (stress[column] - balance))
    return post


def leaving(density, momentum, post):
    t36 = density * (1.0 / 36.0) - (post[0] + post[1] + post[2]) * (1.0 / 24.0)
    az, ay, ax = (0.125 * post[k] for k in range(3))
    rzy, rzx, ryx = (0.25 * post[k] for k in range(3, 6))
    nz, ny, nx = ((1.0 / 12.0) * momentum[k] for k in range(3))
    bz, by, bx = t36 + az, t36 + ay, t36 + ax

    def edges(base, cross, one, two):
        plus, minus = base + cross, base - cross
        both, apart = one + two, one - two
        return plus + both, plus - both, minus + apart, minus - apart

    def up(value):
        return roll(value, 1, 0)

    def down(value):
        return roll(value, -1, 0)

    zpp, zmm, zpm, zmp = edges(bz + ay, rzy, nz, ny)
    y_zp = (up(zpp), down(zpm))
    y_zm = (up(zmp), down(zmm))
    xpp, xmm, xpm, xmp = edges(bz + ax, rzx, nz, nx)
    ypp, ymm, ypm, ymp = edges(by + ax, ryx, ny, nx)
    y_plus, y_minus = up(2.0 * (by + ny)), down(2.0 * (by - ny))
    ypp, ymp = up(ypp), down(ymp)
    ypm, ymm = up(ypm), down(ymm)
    x_plus, x_minus = 2.0 * (bx + nx), 2.0 * (bx - nx)
    syy_plus, syy_minus = ypp + ymp, ypm + ymm
    right = (x_plus + syy_plus, ypp - ymp, syy_plus, xpp, xmp)
    left = (x_minus + syy_minus, ypm - ymm, syy_minus, xpm, xmm)
    stay = (12.0 * t36, y_plus, y_minus, 2.0 * (bz + nz), y_zp, 2.0 * (bz - nz), y_zm)
    return stay, right, left


def plane_sums(stay, right, left):
    rest, y_plus, y_minus, z_plus, y_zp, z_minus, y_zm = stay
    syy = y_plus + y_minus
    sxx = right[0] + left[0]
    sums = [
        (rest + syy) + sxx,
        (y_plus - y_minus) + (right[1] + left[1]),
        right[0] - left[0],
        syy + (right[2] + left[2]),
        sxx,
        right[1] - left[1],
    ]
    for face, (one, two), plus, minus in ((z_plus, y_zp, right[3], left[3]), (z_minus, y_zm, right[4], left[4])):
        yy, xx = one + two, plus + minus
        sums += [face + (yy + xx), one - two, plus - minus, yy, xx]
    return sums


def gather_state(here, below, above, fluid):
    density = here[0] + (below[0] + above[0])
    third = density * (1.0 / 3.0)
    momentum = [
        fluid * (below[0] - above[0]),
        fluid * (here[1] + (below[1] + above[1])),
        fluid * (here[2] + (below[2] + above[2])),
    ]
    stress = [
        fluid * ((below[0] + above[0]) - third),
        fluid * ((here[3] + (below[3] + above[3])) - third),
        fluid * ((here[4] + (below[4] + above[4])) - third),
        fluid * (below[1] - above[1]),
        fluid * (below[2] - above[2]),
        fluid * here[5],
    ]
    return density, momentum, stress, third


def two_steps(
    window, own_strip, got_first, got_second, owners, slots, moments, relaxation_out, outgoing,
    state, sums, strip, strip_sums, edge, pooled,
):
    even_x = is_even("gx")
    lane = lax.broadcasted_iota(jnp.int32, (16, 128), 1)
    spot = lane % 16
    first_lane, last_lane = lane == 0, lane == 127
    quarter = lax.broadcasted_iota(jnp.int32, (8, 128), 1) % 16 // 4

    for field in range(5):
        from_right = jnp.where(even_x, got_first[field], got_second[field])
        from_left = jnp.where(even_x, got_second[field], got_first[field])
        for half in range(2):
            for part in range(2):
                place = 2 * half + part
                rows = slice(8 * part, 8 * part + 8)
                own = own_strip[field, half, rows]
                own = jnp.where(quarter == 1, roll(from_right, 4 - 4 * place, 1), own)
                strip[field, half, rows] = jnp.where(quarter == 2, roll(from_left, 8 - 4 * place, 1), own)

    def first_state(ref, where):
        density = ref[(0,) + where]
        speed = [ref[(1 + k,) + where] for k in range(3)]
        momentum = [density * speed[k] for k in range(3)]
        stress = [
            momentum[one] * speed[two] for one, two in ((0, 0), (1, 1), (2, 2), (0, 1), (0, 2), (1, 2))
        ]
        return density, speed, momentum, stress

    def strip_above(ref, number, half):
        return ref[number, 1] if half == 0 else roll(ref[number, 0], -16, 1)

    def strip_below(ref, number, half):
        return ref[number, 0] if half == 1 else roll(ref[number, 1], 16, 1)

    def row_differences(speed):
        return [roll(value, -1, 0) - roll(value, 1, 0) for value in speed]

    def strip_pass(step, half):
        if step == 0:
            density, speed, momentum, stress = first_state(strip, (half,))
        else:
            density = strip[0, half]
            speed = [strip[1 + k, half] for k in range(3)]
            momentum = [strip[5 + k, half] for k in range(3)]
            stress = [strip[8 + k, half] for k in range(6)]
        dz = [strip_above(strip, 1 + k, half) - strip_below(strip, 1 + k, half) for k in range(3)]
        dy = row_differences(speed)
        dx = [roll(value, -1, 1) - roll(value, 1, 1) for value in speed]
        relaxation = wale([[dz[k], dy[k], dx[k]] for k in range(3)])
        stay, right, left = leaving(density, momentum, collide(momentum, speed, stress, relaxation))
        for k in range(5):
            edge[k, half] = right[k]
            edge[5 + k, half] = left[k]
        if step == 0:
            moved_right = [roll(value, 1, 1) for value in right]
            moved_left = [roll(value, -1, 1) for value in left]
            for k, value in enumerate(plane_sums(stay, moved_right, moved_left)):
                strip_sums[k, half] = value

    def from_left_lane(value, ref, number, half, turn):
        return jnp.where(first_lane, roll(ref[number, half], 117 - turn, 1), roll(value, 1, 1))

    def from_right_lane(value, ref, number, half, turn):
        return jnp.where(last_lane, roll(ref[number, half], 123 - turn, 1), roll(value, -1, 1))

    def plane_pass(step, plane, speeds):
        half, turn = lax.rem(plane, 2), lax.div(plane, 2) * 16
        if step == 0:
            density, speed, momentum, stress = first_state(window, (plane,))
        else:
            density = state[0, plane]
            speed = [state[1 + k, plane] for k in range(3)]
            momentum = [state[4 + k, plane] for k in range(3)]
            stress = [state[7 + k, plane] for k in range(6)]
        dz = [speeds[1 + k, plane + 1] - speeds[1 + k, plane - 1] for k in range(3)]
        dy = row_differences(speed)
        dx = [
            from_right_lane(speed[k], strip, 1 + k, half, turn) - from_left_lane(speed[k], strip, 1 + k, half, turn)
            for k in range(3)
        ]
        relaxation = wale([[dz[k], dy[k], dx[k]] for k in range(3)])
        stay, right, left = leaving(density, momentum, collide(momentum, speed, stress, relaxation))
        return relaxation, stay, right, left, half, turn

    def move_lanes(right, left, half, turn):
        moved_right = [from_left_lane(value, edge, k, half, turn) for k, value in enumerate(right)]
        moved_left = [from_right_lane(value, edge, 5 + k, half, turn) for k, value in enumerate(left)]
        return moved_right, moved_left

    for half in range(2):
        strip_pass(0, half)

    def first_sums(plane, carry):
        _, stay, right, left, half, turn = plane_pass(0, plane, window)
        moved_right, moved_left = move_lanes(right, left, half, turn)
        for k, value in enumerate(plane_sums(stay, moved_right, moved_left)):
            sums[k, plane] = value
        return carry

    lax.fori_loop(1, 15, first_sums, 0)

    def first_gather(plane, carry):
        density, momentum, stress, _ = gather_state(
            [sums[k, plane] for k in range(6)],
            [sums[6 + k, plane - 1] for k in range(5)],
            [sums[11 + k, plane + 1] for k in range(5)],
            window[4, plane],
        )
        inverse = 1.0 / density
        state[0, plane] = density
        for k in range(3):
            state[1 + k, plane] = momentum[k] * inverse
            state[4 + k, plane] = momentum[k]
        for k in range(6):
            state[7 + k, plane] = stress[k]
        return carry

    lax.fori_loop(2, 14, first_gather, 0)

    for half in range(2):
        density, momentum, stress, _ = gather_state(
            [strip_sums[k, half] for k in range(6)],
            [strip_below(strip_sums, 6 + k, half) for k in range(5)],
            [strip_above(strip_sums, 11 + k, half) for k in range(5)],
            strip[4, half],
        )
        inverse = 1.0 / density
        strip[0, half] = density
        for k in range(3):
            strip[1 + k, half] = momentum[k] * inverse
            strip[5 + k, half] = momentum[k]
        for k in range(6):
            strip[8 + k, half] = stress[k]
    for half in range(2):
        strip_pass(1, half)

    def second_sums(plane, carry):
        relaxation, stay, right, left, half, turn = plane_pass(1, plane, state)
        moved_right, moved_left = move_lanes(right, left, half, turn)
        for k, value in enumerate(plane_sums(stay, moved_right, moved_left)):
            sums[k, plane] = value

        @pl.when((plane >= 4) & (plane < 12))
        def _():
            relaxation_out[plane - 4] = relaxation[0:8]

        return carry

    lax.fori_loop(3, 13, second_sums, 0)

    def second_gather(pair, carry):
        total = None
        for side in range(2):
            low = 2 * pair + side
            plane = low + 4
            density, momentum, stress, third = gather_state(
                [sums[k, plane, 0:8] for k in range(6)],
                [sums[6 + k, plane - 1, 0:8] for k in range(5)],
                [sums[11 + k, plane + 1, 0:8] for k in range(5)],
                window[4, plane, 0:8],
            )
            members = [density] + momentum + [stress[k] + third for k in range(3)] + stress[3:]
            for k in range(10):
                moments[k, low] = members[k]
            total = members if total is None else [one + two for one, two in zip(total, members)]
        for k in range(10):
            pooled[pl.ds(pl.multiple_of(k * 32 + pair * 8, 8), 8), :] = total[k]
        return carry

    lax.fori_loop(0, 4, second_gather, 0)

    blocks = 0.125 * (pooled[pl.ds(0, 160, stride=2), :] + pooled[pl.ds(1, 160, stride=2), :])
    owner_row = owners[0:1, :]
    lanes_a = lax.broadcasted_iota(jnp.int32, (128, 128), 0)
    lanes_b = lax.broadcasted_iota(jnp.int32, (128, 128), 1)
    owner_column = jnp.transpose(jnp.broadcast_to(owner_row, (128, 128)))
    earlier = (owner_column == owner_row) & (lanes_a // 2 < lanes_b // 2)
    rank = jnp.sum(earlier.astype(jnp.float32), axis=0, keepdims=True) * 0.5
    position = owner_row * 2 + rank.astype(jnp.int32)
    placing = (lanes_a == position).astype(jnp.float32)
    tags = 0.5 * (slots[0:1, :] + 1).astype(jnp.float32)
    payload = jnp.concatenate([blocks, jnp.broadcast_to(tags, (8, 128))], axis=0)
    outgoing[...] = lax.dot_general(
        placing, payload, (((1,), (1,)), ((), ())),
        precision=lax.Precision.HIGHEST, preferred_element_type=jnp.float32,
    )


def sum_slots(arrived, coarse):
    rows = arrived.shape[0]
    slot = lax.broadcasted_iota(jnp.int32, (rows, SLOTS), 1).astype(jnp.float32)
    chosen = (arrived[:, 160:161] == slot + 1.0).astype(jnp.float32)
    coarse[...] = lax.dot_general(
        chosen, arrived[:, 0:160], (((0,), (0,)), ((), ())),
        precision=lax.Precision.HIGHEST, preferred_element_type=jnp.float32,
    )


def call(kernel, outs, name, scratch=()):
    return pl.pallas_call(
        kernel,
        out_shape=outs,
        scratch_shapes=list(scratch),
        compiler_params=PARAMS,
        name=name,
    )


def per_device(density, velocity, solid, owner_map, slot_map):
    first, second = call(pack_vertical, (f32(5, 4, 8, 128),) * 2, "pack_vertical")(density, velocity, solid)
    first, second = swap(first, second, "gz")
    planes, first, second = call(
        pack_spanwise, (f32(5, 16, 8, 128), f32(5, 8, 8, 128), f32(5, 8, 8, 128)), "pack_spanwise"
    )(density, velocity, solid, first, second)
    first, second = swap(first, second, "gy")
    window, strip, first, second = call(
        pack_streamwise,
        (f32(5, 16, 16, 128), f32(5, 2, 16, 128), f32(5, 8, 128), f32(5, 8, 128)),
        "pack_streamwise",
    )(planes, first, second)
    first, second = swap(first, second, "gx")
    owners = jnp.broadcast_to(jnp.repeat(owner_map.reshape(1, 64), 2, axis=1), (8, 128))
    slots = jnp.broadcast_to(jnp.repeat(slot_map.reshape(1, 64), 2, axis=1), (8, 128))
    moments, relaxation, outgoing = call(
        two_steps,
        (f32(10, 8, 8, 128), f32(8, 8, 128), f32(128, 168)),
        "two_steps",
        (
            pltpu.VMEM((13, 16, 16, 128), jnp.float32),
            pltpu.VMEM((16, 16, 16, 128), jnp.float32),
            pltpu.VMEM((14, 2, 16, 128), jnp.float32),
            pltpu.VMEM((16, 2, 16, 128), jnp.float32),
            pltpu.VMEM((10, 2, 16, 128), jnp.float32),
            pltpu.VMEM((320, 128), jnp.float32),
        ),
    )(window, strip, first, second, owners, slots)
    arrived = lax.all_to_all(
        outgoing.reshape(64, 2, 168), ("gy", "gz"), split_axis=0, concat_axis=0, tiled=True
    )
    coarse = call(sum_slots, f32(SLOTS, 160), "sum_slots")(arrived.reshape(128, 168))
    return moments, relaxation, coarse.reshape(1, 1, 1, SLOTS, 160)


def solution(mesh):
    return jax.shard_map(
        per_device,
        mesh=mesh,
        in_specs=(
            P("gz", "gy", "gx"),
            P(None, "gz", "gy", "gx"),
            P("gz", "gy", "gx"),
            P("gx", "gy", "gz", None, None),
            P("gx", "gy", "gz", None, None),
        ),
        out_specs=(P(None, "gz", "gy", "gx"), P("gz", "gy", "gx"), P("gx", "gy", "gz", None, None)),
        check_vma=False,
    )
```

time: 209 us -> 68.4 us (0.33)
  starting transfers between devices: 95.1 us -> 27.4 us
  waiting for transfers between devices: 53.1 us -> 6.85 us
  local copies, waits for them, and re-layouts: 39.3 us -> 3.65 us
  blocking collectives: 0 us -> 19.8 us
  other arithmetic: 12.1 us -> 0 us
  Pallas kernels: 0 us -> 9.43 us
  matrix products: 6.95 us -> 0 us
    ppermute x24 -> x6, starting transfers between devices: 75.6 us -> 27.4 us  [the longest x3 13.9 us: swap(): lax.ppermute(low_face, axis, second)]
    ppermute x24 -> x6, waiting for transfers between devices: 44.5 us -> 6.85 us  [the longest x3 6.84 us: swap(): lax.ppermute(low_face, axis, second)]
    another operation x24 -> x0, local copies, waits for them, and re-layouts: 33.1 us -> none  [the longest x21 30.8 us: rest_solids(): return jnp.stack(members)]
    all_to_all x0 -> x1, blocking collectives: none -> 19.8 us  [per_device(): lax.all_to_all(outgoing.reshape(64, 2, 168), ('gy', 'gz'), split_axis=0,...]
    all_to_all x2 -> x0, starting transfers between devices: 19.5 us -> none  [the longest x1 11.6 us: per_device(): lax.all_to_all(outgoing.reshape(owner_count, capacity, block_width), ('gy...]
    pallas_call x0 -> x5, Pallas kernels: none -> 9.43 us  [the longest x1 7.58 us: per_device(): call(two_steps, (f32(10, 8, 8, 128), f32(8, 8, 128), f32(128, 168)), 'two...]
    all_to_all x2 -> x0, waiting for transfers between devices: 8.57 us -> none  [the longest x1 8.57 us: per_device(): lax.all_to_all(outgoing.reshape(owner_count, capacity, block_width), ('gy...]
    dot_general x6 -> x0, matrix products: 6.95 us -> none  [the longest x2 4.77 us: stream(): jnp.einsum('qm,mxyz->qxyz', recon_table, post_pad, precision=lax.Precisio...]
  transfers between devices with their start and end apart: 26 -> 6, of which waited for: 20 -> 2; matrix products, arithmetic and copies ran while one was open for 23% -> 1% of each run, Pallas kernels for 0% -> 0%
where the time goes in v1:
time: 68.4 us; the launch traced here: 67.9 us
  starting transfers between devices  27.4 us (40%)
  blocking collectives  19.8 us (29%)
  Pallas kernels  9.43 us (14%)
  waiting for transfers between devices  6.85 us (10%)
  local copies, waits for them, and re-layouts  3.65 us (5%)
  between operations  0.76 us (1%)
    all_to_all x1, blocking collectives, per_device(): lax.all_to_all(outgoing.reshape(64, 2, 168), ('gy', 'gz'), split_axis=0,...  19.8 us
    ppermute x3, starting transfers between devices, swap(): lax.ppermute(low_face, axis, second)  13.9 us
    ppermute x3, starting transfers between devices, swap(): lax.ppermute(high_face, axis, first)  13.5 us
    pallas_call x1, Pallas kernels, per_device(): call(two_steps, (f32(10, 8, 8, 128), f32(8, 8, 128), f32(128, 168)), 'two...  7.58 us
    ppermute x3, waiting for transfers between devices, swap(): lax.ppermute(low_face, axis, second)  6.84 us
    unnamed x10, local copies, waits for them, and re-layouts  3.06 us
  transfers between devices with their start and end apart: 6, of which 2 were waited for; matrix products, arithmetic and copies ran while one was open for 1% of the time, Pallas kernels for 0%

profile of v1, /device:TPU:1, one launch (start us, length us, event | category | flops | bytes accessed | tf_op | source)
XLA Modules:
  0.0 67.9 jit_solution(10940362545430107402)
XLA Ops:
  0.6 0.0 copy-start
  0.6 0.9 %copy-done = f32[3,8,8,128]{3,2,1,0:T(8,128)S(1)} copy-done((f32[3,8,8,128]{3,2,1,0:T(8,128)S(1)}, f32[3,8,8,128]{3,2,1,0:T(8,128)}, u32[]{:S(2)}) %copy-start) | copy-done | bytes 98328
  1.5 0.0 copy-start.1
  1.5 0.8 %copy-done.1 = f32[8,8,128]{2,1,0:T(8,128)S(1)} copy-done((f32[8,8,128]{2,1,0:T(8,128)S(1)}, f32[8,8,128]{2,1,0:T(8,128)}, u32[]{:S(2)}) %copy-start.1) | copy-done | bytes 32792
  2.3 0.0 copy-start.2
  2.3 0.8 %copy-done.2 = s32[8,8,128]{2,1,0:T(8,128)S(1)} copy-done((s32[8,8,128]{2,1,0:T(8,128)S(1)}, s32[8,8,128]{2,1,0:T(8,128)}, u32[]{:S(2)}) %copy-start.2) | copy-done | bytes 32792
  3.1 4.0 %collective-permute-start = (f32[5,4,8,128]{3,2,1,0:T(8,128)S(1)}, f32[5,4,8,128]{3,2,1,0:T(8,128)S(1)}, u32[]{:S(2)}, u32[]{:S(2)}) collective-permute-start(f32[5,4,8,128]{3,2,1,0:T(8,128)S(1)} %get-tuple-element.15), channel_id=1, source_target_pairs={{0,1},{1,0},{2,3},{3,2},{4,5},{5,4},{6,7},{7,6},{8,9},{9,8},{10,11... | collective-permute-start | bytes 245768 | tf_op jit(solution)/shard_map/ppermute | solution.py:37
  7.1 4.9 %collective-permute-start.1 = (f32[5,4,8,128]{3,2,1,0:T(8,128)S(1)}, f32[5,4,8,128]{3,2,1,0:T(8,128)S(1)}, u32[]{:S(2)}, u32[]{:S(2)}) collective-permute-start(f32[5,4,8,128]{3,2,1,0:T(8,128)S(1)} %get-tuple-element.16), channel_id=1, source_target_pairs={{0,7},{1,2},{2,1},{3,4},{4,3},{5,6},{6,5},{7,0},{8,15},{9,10},{10,... | collective-permute-start | bytes 245768 | tf_op jit(solution)/shard_map/ppermute | solution.py:37
  12.0 0.0 collective-permute-done.got_first
  12.0 1.8 %collective-permute-done.1.got_second = f32[5,4,8,128]{3,2,1,0:T(8,128)S(1)} collective-permute-done((f32[5,4,8,128]{3,2,1,0:T(8,128)S(1)}, f32[5,4,8,128]{3,2,1,0:T(8,128)S(1)}, u32[]{:S(2)}, u32[]{:S(2)}) %collective-permute-start.1) | collective-permute-done | bytes 81952 | tf_op jit(solution)/shard_map/ppermute | solution.py:37
  13.8 0.1 pack_spanwise.1
  13.9 7.5 %collective-permute-start.2 = (f32[5,8,8,128]{3,2,1,0:T(8,128)S(1)}, f32[5,8,8,128]{3,2,1,0:T(8,128)S(1)}, u32[]{:S(2)}, u32[]{:S(2)}) collective-permute-start(f32[5,8,8,128]{3,2,1,0:T(8,128)S(1)} %get-tuple-element.18), channel_id=1, source_target_pairs={{0,8},{8,0},{16,24},{24,16},{32,40},{40,32},{48,56},{56,48},{1,9},... | collective-permute-start | bytes 491528 | tf_op jit(solution)/shard_map/ppermute | solution.py:37
  21.4 1.9 %collective-permute-start.3 = (f32[5,8,8,128]{3,2,1,0:T(8,128)S(1)}, f32[5,8,8,128]{3,2,1,0:T(8,128)S(1)}, u32[]{:S(2)}, u32[]{:S(2)}) collective-permute-start(f32[5,8,8,128]{3,2,1,0:T(8,128)S(1)} %get-tuple-element.19), channel_id=1, source_target_pairs={{0,56},{8,16},{16,8},{24,32},{32,24},{40,48},{48,40},{56,0},{1,57}... | collective-permute-start | bytes 491528 | tf_op jit(solution)/shard_map/ppermute | solution.py:37
  23.3 0.0 collective-permute-done.2.got_first
  23.3 5.0 %collective-permute-done.3.got_second = f32[5,8,8,128]{3,2,1,0:T(8,128)S(1)} collective-permute-done((f32[5,8,8,128]{3,2,1,0:T(8,128)S(1)}, f32[5,8,8,128]{3,2,1,0:T(8,128)S(1)}, u32[]{:S(2)}, u32[]{:S(2)}) %collective-permute-start.3) | collective-permute-done | bytes 163872 | tf_op jit(solution)/shard_map/ppermute | solution.py:37
  28.3 0.9 %pack_streamwise.1 = (f32[5,16,16,128]{3,2,1,0:T(8,128)S(1)}, f32[5,2,16,128]{3,2,1,0:T(8,128)S(1)}, f32[5,8,128]{2,1,0:T(8,128)S(1)}, f32[5,8,128]{2,1,0:T(8,128)S(1)}) custom-call(f32[5,16,8,128]{3,2,1,0:T(8,128)S(1)} %get-tuple-element.17.planes, f32[5,8,8,128]{3,2,1,0:T(8,128)S(1)} %collective-permute-done.2.got_first, ...), custom_call_target="tpu_custom_call" | custom-call | tf_op jit(solution)/shard_map/pack_streamwise/pallas_call | solution.py:425
  29.2 1.9 %collective-permute-start.4 = (f32[5,8,128]{2,1,0:T(8,128)S(1)}, f32[5,8,128]{2,1,0:T(8,128)S(1)}, u32[]{:S(2)}, u32[]{:S(2)}) collective-permute-start(f32[5,8,128]{2,1,0:T(8,128)S(1)} %get-tuple-element.22), channel_id=1, source_target_pairs={{0,64},{64,0},{128,192},{192,128},{256,320},{320,256},{384,448},{4... | collective-permute-start | bytes 61448 | tf_op jit(solution)/shard_map/ppermute | solution.py:37
  31.1 0.0 copy-start.3
  31.1 7.1 %collective-permute-start.5 = (f32[5,8,128]{2,1,0:T(8,128)S(1)}, f32[5,8,128]{2,1,0:T(8,128)S(1)}, u32[]{:S(2)}, u32[]{:S(2)}) collective-permute-start(f32[5,8,128]{2,1,0:T(8,128)S(1)} %get-tuple-element.23), channel_id=1, source_target_pairs={{0,448},{64,128},{128,64},{192,256},{256,192},{320,384},{384,320},... | collective-permute-start | bytes 61448 | tf_op jit(solution)/shard_map/ppermute | solution.py:37
  38.3 0.0 copy-done.3
  38.3 0.1 broadcast_in_dim.20
  38.4 0.1 broadcast_in_dim.21
  38.5 0.0 copy-start.4
  38.5 0.6 copy-done.4
  39.2 0.1 broadcast_in_dim.23
  39.2 0.1 broadcast_in_dim.24
  39.4 0.0 collective-permute-done.4.got_first
  39.4 0.0 collective-permute-done.5.got_second
  39.4 7.6 %two_steps.1 = (f32[10,8,8,128]{3,2,1,0:T(8,128)}, f32[8,8,128]{2,1,0:T(8,128)}, f32[128,168]{1,0:T(8,128)S(1)}) custom-call(f32[5,16,16,128]{3,2,1,0:T(8,128)S(1)} %get-tuple-element.20.window, f32[5,2,16,128]{3,2,1,0:T(8,128)S(1)} %get-tuple-element.21.own_strip, f32[5,8,128]{2,1,0:T(8,128)S(1)} %collective-permute-done.4.got_first, ...), custom_call_target="tpu_custom_call" | custom-call | tf_op jit(solution)/shard_map/two_steps/pallas_call | solution.py:433
  47.0 0.1 reshape.35
  47.1 19.8 %all_to_all.5 = f32[64,2,168]{2,1,0:T(2,128)S(1)} all-to-all(f32[64,2,168]{2,1,0:T(2,128)S(1)} %reshape.35), channel_id=1, replica_groups=mesh['gx'=8,'gy'=8,'gz'=8] {'gy','gz'}, dimensions={0} | all-to-all | bytes 172032 | tf_op jit(solution)/shard_map/all_to_all | solution.py:446
  66.9 0.1 reshape.36.arrived
  67.0 0.9 %sum_slots.1 = f32[16,160]{1,0:T(8,128)} custom-call(f32[128,168]{1,0:T(8,128)S(1)} %reshape.36.arrived), custom_call_target="tpu_custom_call" | custom-call | tf_op jit(solution)/shard_map/sum_slots/pallas_call | solution.py:449
  (3 shorter events, 0.0 us)
Async XLA Ops:
  0.6 0.9 %copy-start = (f32[3,8,8,128]{3,2,1,0:T(8,128)S(1)}, f32[3,8,8,128]{3,2,1,0:T(8,128)}, u32[]{:S(2)}) copy-start(f32[3,8,8,128]{3,2,1,0:T(8,128)} %velocity.3) | copy-start | bytes 294916
  1.5 0.8 %copy-start.1 = (f32[8,8,128]{2,1,0:T(8,128)S(1)}, f32[8,8,128]{2,1,0:T(8,128)}, u32[]{:S(2)}) copy-start(f32[8,8,128]{2,1,0:T(8,128)} %density.3) | copy-start | bytes 98308
  2.3 0.8 %copy-start.2 = (s32[8,8,128]{2,1,0:T(8,128)S(1)}, s32[8,8,128]{2,1,0:T(8,128)}, u32[]{:S(2)}) copy-start(s32[8,8,128]{2,1,0:T(8,128)} %solid.3) | copy-start | bytes 98308
  3.1 8.9 %collective-permute-start = (f32[5,4,8,128]{3,2,1,0:T(8,128)S(1)}, f32[5,4,8,128]{3,2,1,0:T(8,128)S(1)}, u32[]{:S(2)}, u32[]{:S(2)}) collective-permute-start(f32[5,4,8,128]{3,2,1,0:T(8,128)S(1)} %get-tuple-element.15), channel_id=1, source_target_pairs={{0,1},{1,0},{2,3},{3,2},{4,5},{5,4},{6,7},{7,6},{8,9},{9,8},{10,11... | collective-permute-start | bytes 245768 | tf_op jit(solution)/shard_map/ppermute | solution.py:37
  7.1 6.7 %collective-permute-start.1 = (f32[5,4,8,128]{3,2,1,0:T(8,128)S(1)}, f32[5,4,8,128]{3,2,1,0:T(8,128)S(1)}, u32[]{:S(2)}, u32[]{:S(2)}) collective-permute-start(f32[5,4,8,128]{3,2,1,0:T(8,128)S(1)} %get-tuple-element.16), channel_id=1, source_target_pairs={{0,7},{1,2},{2,1},{3,4},{4,3},{5,6},{6,5},{7,0},{8,15},{9,10},{10,... | collective-permute-start | bytes 245768 | tf_op jit(solution)/shard_map/ppermute | solution.py:37
  13.9 9.5 %collective-permute-start.2 = (f32[5,8,8,128]{3,2,1,0:T(8,128)S(1)}, f32[5,8,8,128]{3,2,1,0:T(8,128)S(1)}, u32[]{:S(2)}, u32[]{:S(2)}) collective-permute-start(f32[5,8,8,128]{3,2,1,0:T(8,128)S(1)} %get-tuple-element.18), channel_id=1, source_target_pairs={{0,8},{8,0},{16,24},{24,16},{32,40},{40,32},{48,56},{56,48},{1,9},... | collective-permute-start | bytes 491528 | tf_op jit(solution)/shard_map/ppermute | solution.py:37
  21.4 6.9 %collective-permute-start.3 = (f32[5,8,8,128]{3,2,1,0:T(8,128)S(1)}, f32[5,8,8,128]{3,2,1,0:T(8,128)S(1)}, u32[]{:S(2)}, u32[]{:S(2)}) collective-permute-start(f32[5,8,8,128]{3,2,1,0:T(8,128)S(1)} %get-tuple-element.19), channel_id=1, source_target_pairs={{0,56},{8,16},{16,8},{24,32},{32,24},{40,48},{48,40},{56,0},{1,57}... | collective-permute-start | bytes 491528 | tf_op jit(solution)/shard_map/ppermute | solution.py:37
  29.2 10.2 %collective-permute-start.4 = (f32[5,8,128]{2,1,0:T(8,128)S(1)}, f32[5,8,128]{2,1,0:T(8,128)S(1)}, u32[]{:S(2)}, u32[]{:S(2)}) collective-permute-start(f32[5,8,128]{2,1,0:T(8,128)S(1)} %get-tuple-element.22), channel_id=1, source_target_pairs={{0,64},{64,0},{128,192},{192,128},{256,320},{320,256},{384,448},{4... | collective-permute-start | bytes 61448 | tf_op jit(solution)/shard_map/ppermute | solution.py:37
  31.1 7.2 %copy-start.3 = (s32[1,1,1,64,1]{3,4,2,1,0:T(1,128)S(1)}, s32[1,1,1,64,1]{3,4,2,1,0:T(1,128)}, u32[]{:S(2)}) copy-start(s32[1,1,1,64,1]{3,4,2,1,0:T(1,128)} %param.8) | copy-start | bytes 772
  31.1 8.3 %collective-permute-start.5 = (f32[5,8,128]{2,1,0:T(8,128)S(1)}, f32[5,8,128]{2,1,0:T(8,128)S(1)}, u32[]{:S(2)}, u32[]{:S(2)}) collective-permute-start(f32[5,8,128]{2,1,0:T(8,128)S(1)} %get-tuple-element.23), channel_id=1, source_target_pairs={{0,448},{64,128},{128,64},{192,256},{256,192},{320,384},{384,320},... | collective-permute-start | bytes 61448 | tf_op jit(solution)/shard_map/ppermute | solution.py:37
  38.5 0.7 copy-start.4

commit v2 on v1

--- a/solution.py
+++ b/solution.py
@@ -6,11 +6,11 @@
 from jax.sharding import PartitionSpec as P
 
 SLOTS = 16
+SPAN_Y = 8
+SPAN_Z = 8
 WALE_COEFF = 0.5
 BASE_VISCOSITY = 0.01
 WALE_FLOOR = 1e-10
-VMEM = pl.BlockSpec(memory_space=pltpu.VMEM)
-PARAMS = pltpu.CompilerParams(vmem_limit_bytes=48 * 1024 * 1024)
 
 
 def f32(*shape):
@@ -30,79 +30,100 @@
     return lax.rem(lax.axis_index(axis), 2) == 0
 
 
-def swap(high_face, low_face, axis):
+def swap(near, far, axis):
     count = lax.axis_size(axis)
-    first = [(i, i ^ 1) for i in range(count)]
-    second = [(i, (((i + 1) % count) ^ 1) - 1 if ((i + 1) % count) ^ 1 else count - 1) for i in range(count)]
-    return lax.ppermute(high_face, axis, first), lax.ppermute(low_face, axis, second)
-
-
-def pack_vertical(density, velocity, solid, first, second):
+    near_pairs = [(i, i ^ 1) for i in range(count)]
+    far_pairs = [(i, (i + 1) % count if i % 2 else (i - 1) % count) for i in range(count)]
+    far = lax.ppermute(far, axis, far_pairs)
+    return lax.ppermute(near, axis, near_pairs), far
+
+
+def pack_vertical(fields, near, far):
     even = is_even("gz")
-    for out, upper in ((first, even), (second, jnp.logical_not(even))):
-        planes = pl.ds(jnp.where(upper, 4, 0), 4)
-        fluid = 1.0 - solid[planes].astype(jnp.float32)
-        out[0] = density[planes]
-        for axis in range(3):
-            out[1 + axis] = velocity[axis, planes] * fluid
-        out[4] = fluid
-
-
-def pack_spanwise(density, velocity, solid, got_first, got_second, planes, first, second):
+    for field in range(5):
+        near[field] = jnp.where(even, fields[field, 4:8], fields[field, 0:4])
+        far[field] = jnp.where(even, fields[field, 0:4], fields[field, 4:8])
+
+
+def pack_spanwise(fields, got_far, got_near, planes, near, far):
     even_z = is_even("gz")
     even_y = is_even("gy")
-    fluid = 1.0 - solid[...].astype(jnp.float32)
-    planes[0, 4:12] = density[...]
-    for axis in range(3):
-        planes[1 + axis, 4:12] = velocity[axis] * fluid
-    planes[4, 4:12] = fluid
-    for field in range(5):
-        planes[field, 12:16] = jnp.where(even_z, got_first[field], got_second[field])
-        planes[field, 0:4] = jnp.where(even_z, got_second[field], got_first[field])
     front = lax.broadcasted_iota(jnp.int32, (8, 128), 0) < 4
     for field in range(5):
+        planes[field, 4:12] = fields[field]
+        planes[field, 12:16] = jnp.where(even_z, got_near[field], got_far[field])
+        planes[field, 0:4] = jnp.where(even_z, got_far[field], got_near[field])
         for pair in range(8):
             one = planes[field, 2 * pair]
             two = planes[field, 2 * pair + 1]
             high = jnp.where(front, roll(one, 4, 0), two)
             low = jnp.where(front, one, roll(two, 4, 0))
-            first[field, pair] = jnp.where(even_y, high, low)
-            second[field, pair] = jnp.where(even_y, low, high)
-
-
-def pack_streamwise(planes, got_first, got_second, window, strip, first, second):
+            near[field, pair] = jnp.where(even_y, high, low)
+            far[field, pair] = jnp.where(even_y, low, high)
+
+
+def pack_streamwise(planes, got_far, got_near, window, faces, near, far):
     even_y = is_even("gy")
     even_x = is_even("gx")
     front = lax.broadcasted_iota(jnp.int32, (8, 128), 0) < 4
-    lane = lax.broadcasted_iota(jnp.int32, (16, 128), 1)
-    group, spot = lane // 16, lane % 16
+    lane = lax.broadcasted_iota(jnp.int32, (8, 128), 1)
     for field in range(5):
+        own = [jnp.zeros((8, 128), jnp.float32) for _ in range(2)]
         for pair in range(8):
-            above = jnp.where(even_y, got_first[field, pair], got_second[field, pair])
-            below = jnp.where(even_y, got_second[field, pair], got_first[field, pair])
-            window[field, 2 * pair, 0:8] = planes[field, 2 * pair]
-            window[field, 2 * pair + 1, 0:8] = planes[field, 2 * pair + 1]
-            window[field, 2 * pair, 8:16] = jnp.where(front, above, roll(below, 4, 0))
-            window[field, 2 * pair + 1, 8:16] = jnp.where(front, roll(above, 4, 0), below)
-    quarter = lax.broadcasted_iota(jnp.int32, (8, 128), 1) % 16 // 4
-    for field in range(5):
-        to_right = jnp.zeros((8, 128), jnp.float32)
-        to_left = jnp.zeros((8, 128), jnp.float32)
-        for half in range(2):
-            own = jnp.zeros((16, 128), jnp.float32)
-            for number in range(8):
-                cells = window[field, 2 * number + half]
-                here = group == number
-                own = jnp.where(here & (spot < 4), roll(cells, 16 * number + 4, 1), own)
-                own = jnp.where(here & (spot >= 12), roll(cells, 16 * number + 12, 1), own)
-            strip[field, half] = own
-            for part in range(2):
-                place = 2 * half + part
-                rows = own[8 * part : 8 * part + 8]
-                to_right = jnp.where(quarter == place, roll(rows, 4 * place, 1), to_right)
-                to_left = jnp.where(quarter == place, roll(rows, 4 * place - 12, 1), to_left)
-        first[field] = jnp.where(even_x, to_right, to_left)
-        second[field] = jnp.where(even_x, to_left, to_right)
+            above = jnp.where(even_y, got_near[field, pair], got_far[field, pair])
+            below = jnp.where(even_y, got_far[field, pair], got_near[field, pair])
+            outer = (jnp.where(front, above, roll(below, 4, 0)), jnp.where(front, roll(above, 4, 0), below))
+            for side in range(2):
+                plane = 2 * pair + side
+                inner = planes[field, plane]
+                window[field, plane, 0:8] = inner
+                window[field, plane, 8:16] = outer[side]
+                here = lane // 8 == plane
+                own[0] = jnp.where(here, roll(inner, 8 * plane + 4, 1), own[0])
+                own[1] = jnp.where(here, roll(outer[side], 8 * plane + 4, 1), own[1])
+        faces[field, 0] = own[0]
+        faces[field, 1] = own[1]
+        even_spot = lane % 8 < 4
+        to_right = jnp.where(even_spot, own[0], roll(own[1], 4, 1))
+        to_left = jnp.where(even_spot, roll(own[0], -4, 1), own[1])
+        near[field] = jnp.where(even_x, to_right, to_left)
+        far[field] = jnp.where(even_x, to_left, to_right)
+
+
+def place_blocks(owners_in, slots_in, placing, tags, owners, slots, arrived):
+    copies = [
+        pltpu.make_async_copy(source, target, arrived.at[number])
+        for number, (source, target) in enumerate(((owners_in, owners), (slots_in, slots)))
+    ]
+    for copy in copies:
+        copy.start()
+    for copy in copies:
+        copy.wait()
+    row = lax.broadcasted_iota(jnp.int32, (64, 128), 0)
+    block = lax.broadcasted_iota(jnp.int32, (64, 128), 1) // 2
+    diagonal = lax.broadcasted_iota(jnp.int32, (64, 64), 0) == lax.broadcasted_iota(jnp.int32, (64, 64), 1)
+    owner_column = jnp.sum(jnp.where(diagonal, owners[...].astype(jnp.float32), 0.0), axis=1, keepdims=True)
+    slot_column = jnp.sum(jnp.where(diagonal, slots[...].astype(jnp.float32), 0.0), axis=1, keepdims=True)
+    owner_row = jnp.sum(jnp.where(row == block, owner_column, 0.0), axis=0, keepdims=True)
+    slot = jnp.sum(jnp.where(row == block, slot_column, 0.0), axis=0, keepdims=True)
+    earlier = (owner_column == owner_row) & (row < block)
+    owner = owner_row.astype(jnp.int32)
+    rank = jnp.sum(jnp.where(earlier, 1.0, 0.0), axis=0, keepdims=True).astype(jnp.int32)
+    position = (lax.rem(owner, SPAN_Z) * SPAN_Y + lax.div(owner, SPAN_Z)) * 2 + rank
+    rows = lax.broadcasted_iota(jnp.int32, (128, 128), 0)
+    placing[...] = (rows == position).astype(jnp.float32)
+    tags[...] = jnp.broadcast_to(0.5 * (slot + 1.0), (16, 128))
+
+
+def pick(chosen, values, contract):
+    chosen = chosen.astype(jnp.bfloat16)
+    total = None
+    for _ in range(3):
+        part = values.astype(jnp.bfloat16)
+        values = values - part.astype(jnp.float32)
+        product = lax.dot_general(chosen, part, (contract, ((), ())), preferred_element_type=jnp.float32)
+        total = product if total is None else total + product
+    return total
 
 
 def wale(doubled):
@@ -206,25 +227,26 @@
 
 
 def two_steps(
-    window, own_strip, got_first, got_second, owners, slots, moments, relaxation_out, outgoing,
+    window, faces, got_far, got_near, placing, tags, moments, relaxation_out, outgoing,
     state, sums, strip, strip_sums, edge, pooled,
 ):
     even_x = is_even("gx")
     lane = lax.broadcasted_iota(jnp.int32, (16, 128), 1)
-    spot = lane % 16
     first_lane, last_lane = lane == 0, lane == 127
     quarter = lax.broadcasted_iota(jnp.int32, (8, 128), 1) % 16 // 4
 
     for field in range(5):
-        from_right = jnp.where(even_x, got_first[field], got_second[field])
-        from_left = jnp.where(even_x, got_second[field], got_first[field])
+        from_right = jnp.where(even_x, got_near[field], got_far[field])
+        from_left = jnp.where(even_x, got_far[field], got_near[field])
         for half in range(2):
             for part in range(2):
-                place = 2 * half + part
-                rows = slice(8 * part, 8 * part + 8)
-                own = own_strip[field, half, rows]
-                own = jnp.where(quarter == 1, roll(from_right, 4 - 4 * place, 1), own)
-                strip[field, half, rows] = jnp.where(quarter == 2, roll(from_left, 8 - 4 * place, 1), own)
+                own = faces[field, part]
+                turn = 8 * half + 4 * part
+                cells = jnp.where(quarter == 0, roll(own, -8 * half, 1), roll(own, 8 - 8 * half, 1))
+                cells = jnp.where(quarter == 1, roll(from_right, 4 - turn, 1), cells)
+                strip[field, half, 8 * part : 8 * part + 8] = jnp.where(
+                    quarter == 2, roll(from_left, 8 - turn, 1), cells
+                )
 
     def first_state(ref, where):
         density = ref[(0,) + where]
@@ -273,7 +295,7 @@
         return jnp.where(last_lane, roll(ref[number, half], 123 - turn, 1), roll(value, -1, 1))
 
     def plane_pass(step, plane, speeds):
-        half, turn = lax.rem(plane, 2), lax.div(plane, 2) * 16
+        half, turn = plane % 2, plane // 2 * 16
         if step == 0:
             density, speed, momentum, stress = first_state(window, (plane,))
         else:
@@ -299,16 +321,13 @@
     for half in range(2):
         strip_pass(0, half)
 
-    def first_sums(plane, carry):
+    for plane in range(1, 15):
         _, stay, right, left, half, turn = plane_pass(0, plane, window)
         moved_right, moved_left = move_lanes(right, left, half, turn)
         for k, value in enumerate(plane_sums(stay, moved_right, moved_left)):
             sums[k, plane] = value
-        return carry
-
-    lax.fori_loop(1, 15, first_sums, 0)
-
-    def first_gather(plane, carry):
+
+    for plane in range(2, 14):
         density, momentum, stress, _ = gather_state(
             [sums[k, plane] for k in range(6)],
             [sums[6 + k, plane - 1] for k in range(5)],
@@ -322,9 +341,6 @@
             state[4 + k, plane] = momentum[k]
         for k in range(6):
             state[7 + k, plane] = stress[k]
-        return carry
-
-    lax.fori_loop(2, 14, first_gather, 0)
 
     for half in range(2):
         density, momentum, stress, _ = gather_state(
@@ -343,21 +359,15 @@
     for half in range(2):
         strip_pass(1, half)
 
-    def second_sums(plane, carry):
+    for plane in range(3, 13):
         relaxation, stay, right, left, half, turn = plane_pass(1, plane, state)
         moved_right, moved_left = move_lanes(right, left, half, turn)
         for k, value in enumerate(plane_sums(stay, moved_right, moved_left)):
             sums[k, plane] = value
-
-        @pl.when((plane >= 4) & (plane < 12))
-        def _():
+        if 4 <= plane < 12:
             relaxation_out[plane - 4] = relaxation[0:8]
 
-        return carry
-
-    lax.fori_loop(3, 13, second_sums, 0)
-
-    def second_gather(pair, carry):
+    for pair in range(4):
         total = None
         for side in range(2):
             low = 2 * pair + side
@@ -373,66 +383,61 @@
                 moments[k, low] = members[k]
             total = members if total is None else [one + two for one, two in zip(total, members)]
         for k in range(10):
-            pooled[pl.ds(pl.multiple_of(k * 32 + pair * 8, 8), 8), :] = total[k]
-        return carry
-
-    lax.fori_loop(0, 4, second_gather, 0)
+            pooled[k * 32 + pair * 8 : k * 32 + pair * 8 + 8, :] = total[k]
 
     blocks = 0.125 * (pooled[pl.ds(0, 160, stride=2), :] + pooled[pl.ds(1, 160, stride=2), :])
-    owner_row = owners[0:1, :]
-    lanes_a = lax.broadcasted_iota(jnp.int32, (128, 128), 0)
-    lanes_b = lax.broadcasted_iota(jnp.int32, (128, 128), 1)
-    owner_column = jnp.transpose(jnp.broadcast_to(owner_row, (128, 128)))
-    earlier = (owner_column == owner_row) & (lanes_a // 2 < lanes_b // 2)
-    rank = jnp.sum(earlier.astype(jnp.float32), axis=0, keepdims=True) * 0.5
-    position = owner_row * 2 + rank.astype(jnp.int32)
-    placing = (lanes_a == position).astype(jnp.float32)
-    tags = 0.5 * (slots[0:1, :] + 1).astype(jnp.float32)
-    payload = jnp.concatenate([blocks, jnp.broadcast_to(tags, (8, 128))], axis=0)
-    outgoing[...] = lax.dot_general(
-        placing, payload, (((1,), (1,)), ((), ())),
-        precision=lax.Precision.HIGHEST, preferred_element_type=jnp.float32,
+    payload = jnp.concatenate([blocks, tags[...]], axis=0)
+    outgoing[...] = pick(placing[...], payload, ((1,), (1,)))
+
+
+def sum_by_slot(arrived, outgoing):
+    row = lax.broadcasted_iota(jnp.int32, (128, 128), 0)
+    column = lax.broadcasted_iota(jnp.int32, (128, 128), 1)
+    tag = jnp.broadcast_to(arrived[:, 160:161], (128, 128))
+    chosen = (column // SLOTS == row // 2 % SPAN_Y) & (tag == (column % SLOTS + 1).astype(jnp.float32))
+    outgoing[...] = pick(chosen.astype(jnp.float32), arrived[:, 0:160], ((0,), (0,)))
+
+
+def sum_senders(arrived, coarse):
+    total = arrived[0]
+    for sender in range(1, arrived.shape[0]):
+        total = total + arrived[sender]
+    coarse[...] = total
+
+
+def call(kernel, outs, name, scratch=(), in_hbm=0, vmem=48):
+    extra = {"in_specs": [pl.BlockSpec(memory_space=pltpu.HBM)] * in_hbm} if in_hbm else {}
+    return pl.pallas_call(
+        kernel, out_shape=outs, scratch_shapes=list(scratch), name=name,
+        compiler_params=pltpu.CompilerParams(vmem_limit_bytes=vmem * 1024 * 1024), **extra
     )
 
 
-def sum_slots(arrived, coarse):
-    rows = arrived.shape[0]
-    slot = lax.broadcasted_iota(jnp.int32, (rows, SLOTS), 1).astype(jnp.float32)
-    chosen = (arrived[:, 160:161] == slot + 1.0).astype(jnp.float32)
-    coarse[...] = lax.dot_general(
-        chosen, arrived[:, 0:160], (((0,), (0,)), ((), ())),
-        precision=lax.Precision.HIGHEST, preferred_element_type=jnp.float32,
-    )
-
-
-def call(kernel, outs, name, scratch=()):
-    return pl.pallas_call(
-        kernel,
-        out_shape=outs,
-        scratch_shapes=list(scratch),
-        compiler_params=PARAMS,
-        name=name,
-    )
-
-
 def per_device(density, velocity, solid, owner_map, slot_map):
-    first, second = call(pack_vertical, (f32(5, 4, 8, 128),) * 2, "pack_vertical")(density, velocity, solid)
-    first, second = swap(first, second, "gz")
-    planes, first, second = call(
+    placing, tags = call(
+        place_blocks,
+        (f32(128, 128), f32(16, 128)),
+        "place_blocks",
+        (pltpu.VMEM((1, 64), jnp.int32), pltpu.VMEM((1, 64), jnp.int32), pltpu.SemaphoreType.DMA((2,))),
+        2,
+    )(owner_map.reshape(1, 64), slot_map.reshape(1, 64))
+    fluid = 1.0 - solid.astype(jnp.float32)
+    fields = jnp.concatenate([density[None], velocity * fluid, fluid[None]])
+    near, far = call(pack_vertical, (f32(5, 4, 8, 128),) * 2, "pack_vertical")(fields)
+    near, far = swap(near, far, "gz")
+    planes, near, far = call(
         pack_spanwise, (f32(5, 16, 8, 128), f32(5, 8, 8, 128), f32(5, 8, 8, 128)), "pack_spanwise"
-    )(density, velocity, solid, first, second)
-    first, second = swap(first, second, "gy")
-    window, strip, first, second = call(
+    )(fields, far, near)
+    near, far = swap(near, far, "gy")
+    window, faces, near, far = call(
         pack_streamwise,
-        (f32(5, 16, 16, 128), f32(5, 2, 16, 128), f32(5, 8, 128), f32(5, 8, 128)),
+        (f32(5, 16, 16, 128), f32(5, 2, 8, 128), f32(5, 8, 128), f32(5, 8, 128)),
         "pack_streamwise",
-    )(planes, first, second)
-    first, second = swap(first, second, "gx")
-    owners = jnp.broadcast_to(jnp.repeat(owner_map.reshape(1, 64), 2, axis=1), (8, 128))
-    slots = jnp.broadcast_to(jnp.repeat(slot_map.reshape(1, 64), 2, axis=1), (8, 128))
+    )(planes, far, near)
+    near, far = swap(near, far, "gx")
     moments, relaxation, outgoing = call(
         two_steps,
-        (f32(10, 8, 8, 128), f32(8, 8, 128), f32(128, 168)),
+        (f32(10, 8, 8, 128), f32(8, 8, 128), f32(128, 176)),
         "two_steps",
         (
             pltpu.VMEM((13, 16, 16, 128), jnp.float32),
@@ -442,11 +447,11 @@
             pltpu.VMEM((10, 2, 16, 128), jnp.float32),
             pltpu.VMEM((320, 128), jnp.float32),
         ),
-    )(window, strip, first, second, owners, slots)
-    arrived = lax.all_to_all(
-        outgoing.reshape(64, 2, 168), ("gy", "gz"), split_axis=0, concat_axis=0, tiled=True
-    )
-    coarse = call(sum_slots, f32(SLOTS, 160), "sum_slots")(arrived.reshape(128, 168))
+    )(window, faces, far, near, placing, tags)
+    arrived = lax.all_to_all(outgoing.reshape(SPAN_Z, 2 * SPAN_Y, 176), "gz", split_axis=0, concat_axis=0, tiled=True)
+    outgoing = call(sum_by_slot, f32(128, 160), "sum_by_slot")(arrived.reshape(128, 176))
+    arrived = lax.all_to_all(outgoing.reshape(SPAN_Y, SLOTS, 160), "gy", split_axis=0, concat_axis=0, tiled=True)
+    coarse = call(sum_senders, f32(SLOTS, 160), "sum_senders")(arrived)
     return moments, relaxation, coarse.reshape(1, 1, 1, SLOTS, 160)
 
 

time: 68.4 us -> 67.5 us (0.987)
  blocking collectives: 19.8 us -> 24.2 us
  Pallas kernels: 9.43 us -> 5.96 us
  local copies, waits for them, and re-layouts: 3.65 us -> 1.5 us
  waiting for transfers between devices: 6.85 us -> 6.02 us
  other arithmetic: 0 us -> 0.82 us
    all_to_all x1 -> x2, blocking collectives: 19.8 us -> 24.2 us  [the longest x1 12.5 us: per_device(): lax.all_to_all(outgoing.reshape(SPAN_Y, SLOTS, 160), 'gy', split_axis=0,...]
    pallas_call x4 -> x6, Pallas kernels: 9.38 us -> 5.91 us  [the longest x1 4.46 us: per_device(): call(two_steps, (f32(10, 8, 8, 128), f32(8, 8, 128), f32(128, 176)), 'two...]
    unnamed x10 -> x8, local copies, waits for them, and re-layouts: 3.06 us -> 1.5 us
    ppermute x6, waiting for transfers between devices: 6.85 us -> 6.02 us  [the longest x3 5.77 us: swap(): return (lax.ppermute(near, axis, near_pairs), far)]
    sub x0 -> x1, other arithmetic: none -> 0.8 us  [per_device(): fluid = 1.0 - solid.astype(jnp.float32)]
  transfers between devices with their start and end apart: 6 -> 6, of which waited for: 2 -> 4; matrix products, arithmetic and copies ran while one was open for 1% -> 0% of each run, Pallas kernels for 0% -> 0%
where the time goes in v2:
time: 67.5 us; the launch traced here: 67.1 us
  starting transfers between devices  27.8 us (41%)
  blocking collectives  24.2 us (36%)
  waiting for transfers between devices  6.02 us (9%)
  Pallas kernels  5.96 us (9%)
  local copies, waits for them, and re-layouts  1.5 us (2%)
  other arithmetic  0.82 us (1%)
  between operations  0.76 us (1%)
    ppermute x3, starting transfers between devices, swap(): far = lax.ppermute(far, axis, far_pairs)  21.2 us
    all_to_all x1, blocking collectives, per_device(): lax.all_to_all(outgoing.reshape(SPAN_Y, SLOTS, 160), 'gy', split_axis=0,...  12.5 us
    all_to_all x1, blocking collectives, per_device(): lax.all_to_all(outgoing.reshape(SPAN_Z, 2 * SPAN_Y, 176), 'gz', split_axi...  11.7 us
    ppermute x3, starting transfers between devices, swap(): return (lax.ppermute(near, axis, near_pairs), far)  6.58 us
    ppermute x3, waiting for transfers between devices, swap(): return (lax.ppermute(near, axis, near_pairs), far)  5.77 us
    pallas_call x1, Pallas kernels, per_device(): call(two_steps, (f32(10, 8, 8, 128), f32(8, 8, 128), f32(128, 176)), 'two...  4.46 us
    unnamed x8, local copies, waits for them, and re-layouts  1.5 us
  transfers between devices with their start and end apart: 6, of which 4 were waited for; matrix products, arithmetic and copies ran while one was open for 0% of the time, Pallas kernels for 0%

profile of v2, /device:TPU:1, one launch (start us, length us, event | category | flops | bytes accessed | tf_op | source)
XLA Modules:
  0.0 67.1 jit_solution(17130158912295667794)
XLA Ops:
  0.6 0.0 copy-start.2
  0.6 0.8 %convert_subtract_fusion = (f32[8,8,128]{2,1,0:T(8,128)S(1)}, f32[1,8,8,128]{3,2,1,0:T(8,128)S(1)}) fusion(s32[8,8,128]{2,1,0:T(8,128)} %param.7), kind=kLoop, calls=%fused_computation.2 | loop fusion | flops 16384 | bytes 98304 | tf_op jit(solution)/shard_map/sub | solution.py:424
  1.4 0.1 copy-done.2
  1.5 0.0 copy-start.3
  1.6 0.7 %copy-done.3 = f32[8,8,128]{2,1,0:T(8,128)S(1)} copy-done((f32[8,8,128]{2,1,0:T(8,128)S(1)}, f32[8,8,128]{2,1,0:T(8,128)}, u32[]{:S(2)}) %copy-start.3) | copy-done | bytes 32792
  2.3 5.9 %collective-permute-start = (f32[5,4,8,128]{3,2,1,0:T(8,128)S(1)}, f32[5,4,8,128]{3,2,1,0:T(8,128)S(1)}, u32[]{:S(2)}, u32[]{:S(2)}) collective-permute-start(f32[5,4,8,128]{3,2,1,0:T(8,128)S(1)} %get-tuple-element.17), channel_id=1, source_target_pairs={{0,7},{1,2},{2,1},{3,4},{4,3},{5,6},{6,5},{7,0},{8,15},{9,10},{10,... | collective-permute-start | bytes 245768 | tf_op jit(solution)/shard_map/ppermute | solution.py:37
  8.3 1.9 %collective-permute-start.1 = (f32[5,4,8,128]{3,2,1,0:T(8,128)S(1)}, f32[5,4,8,128]{3,2,1,0:T(8,128)S(1)}, u32[]{:S(2)}, u32[]{:S(2)}) collective-permute-start(f32[5,4,8,128]{3,2,1,0:T(8,128)S(1)} %get-tuple-element.18), channel_id=1, source_target_pairs={{0,1},{1,0},{2,3},{3,2},{4,5},{5,4},{6,7},{7,6},{8,9},{9,8},{10,11... | collective-permute-start | bytes 245768 | tf_op jit(solution)/shard_map/ppermute | solution.py:38
  10.2 0.0 collective-permute-done.got_far
  10.2 3.2 %collective-permute-done.1.got_near = f32[5,4,8,128]{3,2,1,0:T(8,128)S(1)} collective-permute-done((f32[5,4,8,128]{3,2,1,0:T(8,128)S(1)}, f32[5,4,8,128]{3,2,1,0:T(8,128)S(1)}, u32[]{:S(2)}, u32[]{:S(2)}) %collective-permute-start.1) | collective-permute-done | bytes 81952 | tf_op jit(solution)/shard_map/ppermute | solution.py:38
  13.5 5.1 %collective-permute-start.2 = (f32[5,8,8,128]{3,2,1,0:T(8,128)S(1)}, f32[5,8,8,128]{3,2,1,0:T(8,128)S(1)}, u32[]{:S(2)}, u32[]{:S(2)}) collective-permute-start(f32[5,8,8,128]{3,2,1,0:T(8,128)S(1)} %get-tuple-element.20), channel_id=1, source_target_pairs={{0,56},{8,16},{16,8},{24,32},{32,24},{40,48},{48,40},{56,0},{1,57}... | collective-permute-start | bytes 491528 | tf_op jit(solution)/shard_map/ppermute | solution.py:37
  18.6 2.7 %collective-permute-start.3 = (f32[5,8,8,128]{3,2,1,0:T(8,128)S(1)}, f32[5,8,8,128]{3,2,1,0:T(8,128)S(1)}, u32[]{:S(2)}, u32[]{:S(2)}) collective-permute-start(f32[5,8,8,128]{3,2,1,0:T(8,128)S(1)} %get-tuple-element.21), channel_id=1, source_target_pairs={{0,8},{8,0},{16,24},{24,16},{32,40},{40,32},{48,56},{56,48},{1,9},... | collective-permute-start | bytes 491528 | tf_op jit(solution)/shard_map/ppermute | solution.py:38
  21.4 0.2 collective-permute-done.2.got_far
  21.6 0.8 %collective-permute-done.3.got_near = f32[5,8,8,128]{3,2,1,0:T(8,128)S(1)} collective-permute-done((f32[5,8,8,128]{3,2,1,0:T(8,128)S(1)}, f32[5,8,8,128]{3,2,1,0:T(8,128)S(1)}, u32[]{:S(2)}, u32[]{:S(2)}) %collective-permute-start.3) | collective-permute-done | bytes 163872 | tf_op jit(solution)/shard_map/ppermute | solution.py:38
  22.4 0.4 pack_streamwise.1
  22.8 10.2 %collective-permute-start.4 = (f32[5,8,128]{2,1,0:T(8,128)S(1)}, f32[5,8,128]{2,1,0:T(8,128)S(1)}, u32[]{:S(2)}, u32[]{:S(2)}) collective-permute-start(f32[5,8,128]{2,1,0:T(8,128)S(1)} %get-tuple-element.24), channel_id=1, source_target_pairs={{0,448},{64,128},{128,64},{192,256},{256,192},{320,384},{384,320},... | collective-permute-start | bytes 61448 | tf_op jit(solution)/shard_map/ppermute | solution.py:37
  33.0 1.9 %collective-permute-start.5 = (f32[5,8,128]{2,1,0:T(8,128)S(1)}, f32[5,8,128]{2,1,0:T(8,128)S(1)}, u32[]{:S(2)}, u32[]{:S(2)}) collective-permute-start(f32[5,8,128]{2,1,0:T(8,128)S(1)} %get-tuple-element.25), channel_id=1, source_target_pairs={{0,64},{64,0},{128,192},{192,128},{256,320},{320,256},{384,448},{4... | collective-permute-start | bytes 61448 | tf_op jit(solution)/shard_map/ppermute | solution.py:38
  34.9 0.0 copy-start
  34.9 0.0 copy-start.1
  34.9 0.6 copy-done
  35.5 0.0 copy-done.1
  35.6 0.1 place_blocks.1
  35.7 0.0 collective-permute-done.4.got_far
  35.7 1.8 %collective-permute-done.5.got_near = f32[5,8,128]{2,1,0:T(8,128)S(1)} collective-permute-done((f32[5,8,128]{2,1,0:T(8,128)S(1)}, f32[5,8,128]{2,1,0:T(8,128)S(1)}, u32[]{:S(2)}, u32[]{:S(2)}) %collective-permute-start.5) | collective-permute-done | bytes 20512 | tf_op jit(solution)/shard_map/ppermute | solution.py:38
  37.5 4.5 %two_steps.1 = (f32[10,8,8,128]{3,2,1,0:T(8,128)}, f32[8,8,128]{2,1,0:T(8,128)}, f32[128,176]{1,0:T(8,128)S(1)}) custom-call(f32[5,16,16,128]{3,2,1,0:T(8,128)S(1)} %get-tuple-element.22.window, f32[5,2,8,128]{3,2,1,0:T(8,128)S(1)} %get-tuple-element.23.faces, f32[5,8,128]{2,1,0:T(8,128)S(1)} %collective-permute-done.4.got_far, ...), custom_call_target="tpu_custom_call" | custom-call | tf_op jit(solution)/shard_map/two_steps/pallas_call | solution.py:438
  41.9 11.7 %all_to_all.10 = f32[8,16,176]{2,1,0:T(8,128)S(1)} all-to-all(f32[8,16,176]{2,1,0:T(8,128)S(1)} %bitcast.11), channel_id=1, replica_groups=mesh['gx'=8,'gy'=8,'gz'=8] {'gz'}, dimensions={0} | all-to-all | bytes 180224 | tf_op jit(solution)/shard_map/all_to_all | solution.py:451
  53.7 0.3 sum_by_slot.1
  54.0 12.5 %all_to_all.11.arrived = f32[8,16,160]{2,1,0:T(8,128)S(1)} all-to-all(f32[8,16,160]{2,1,0:T(8,128)S(1)} %bitcast.10), channel_id=1, replica_groups=mesh['gx'=8,'gy'=8,'gz'=8] {'gy'}, dimensions={0} | all-to-all | bytes 163840 | tf_op jit(solution)/shard_map/all_to_all | solution.py:453
  66.5 0.6 sum_senders.1
  (4 shorter events, 0.1 us)
Async XLA Ops:
  0.6 0.9 %copy-start.2 = (f32[3,8,8,128]{3,2,1,0:T(8,128)S(1)}, f32[3,8,8,128]{3,2,1,0:T(8,128)}, u32[]{:S(2)}) copy-start(f32[3,8,8,128]{3,2,1,0:T(8,128)} %param.6) | copy-start | bytes 294916
  1.5 0.8 %copy-start.3 = (f32[8,8,128]{2,1,0:T(8,128)S(1)}, f32[8,8,128]{2,1,0:T(8,128)}, u32[]{:S(2)}) copy-start(f32[8,8,128]{2,1,0:T(8,128)} %param.5) | copy-start | bytes 98308
  2.3 7.9 %collective-permute-start = (f32[5,4,8,128]{3,2,1,0:T(8,128)S(1)}, f32[5,4,8,128]{3,2,1,0:T(8,128)S(1)}, u32[]{:S(2)}, u32[]{:S(2)}) collective-permute-start(f32[5,4,8,128]{3,2,1,0:T(8,128)S(1)} %get-tuple-element.17), channel_id=1, source_target_pairs={{0,7},{1,2},{2,1},{3,4},{4,3},{5,6},{6,5},{7,0},{8,15},{9,10},{10,... | collective-permute-start | bytes 245768 | tf_op jit(solution)/shard_map/ppermute | solution.py:37
  8.3 5.2 %collective-permute-start.1 = (f32[5,4,8,128]{3,2,1,0:T(8,128)S(1)}, f32[5,4,8,128]{3,2,1,0:T(8,128)S(1)}, u32[]{:S(2)}, u32[]{:S(2)}) collective-permute-start(f32[5,4,8,128]{3,2,1,0:T(8,128)S(1)} %get-tuple-element.18), channel_id=1, source_target_pairs={{0,1},{1,0},{2,3},{3,2},{4,5},{5,4},{6,7},{7,6},{8,9},{9,8},{10,11... | collective-permute-start | bytes 245768 | tf_op jit(solution)/shard_map/ppermute | solution.py:38
  13.5 8.1 %collective-permute-start.2 = (f32[5,8,8,128]{3,2,1,0:T(8,128)S(1)}, f32[5,8,8,128]{3,2,1,0:T(8,128)S(1)}, u32[]{:S(2)}, u32[]{:S(2)}) collective-permute-start(f32[5,8,8,128]{3,2,1,0:T(8,128)S(1)} %get-tuple-element.20), channel_id=1, source_target_pairs={{0,56},{8,16},{16,8},{24,32},{32,24},{40,48},{48,40},{56,0},{1,57}... | collective-permute-start | bytes 491528 | tf_op jit(solution)/shard_map/ppermute | solution.py:37
  18.6 3.8 %collective-permute-start.3 = (f32[5,8,8,128]{3,2,1,0:T(8,128)S(1)}, f32[5,8,8,128]{3,2,1,0:T(8,128)S(1)}, u32[]{:S(2)}, u32[]{:S(2)}) collective-permute-start(f32[5,8,8,128]{3,2,1,0:T(8,128)S(1)} %get-tuple-element.21), channel_id=1, source_target_pairs={{0,8},{8,0},{16,24},{24,16},{32,40},{40,32},{48,56},{56,48},{1,9},... | collective-permute-start | bytes 491528 | tf_op jit(solution)/shard_map/ppermute | solution.py:38
  22.8 13.0 %collective-permute-start.4 = (f32[5,8,128]{2,1,0:T(8,128)S(1)}, f32[5,8,128]{2,1,0:T(8,128)S(1)}, u32[]{:S(2)}, u32[]{:S(2)}) collective-permute-start(f32[5,8,128]{2,1,0:T(8,128)S(1)} %get-tuple-element.24), channel_id=1, source_target_pairs={{0,448},{64,128},{128,64},{192,256},{256,192},{320,384},{384,320},... | collective-permute-start | bytes 61448 | tf_op jit(solution)/shard_map/ppermute | solution.py:37
  33.0 4.5 %collective-permute-start.5 = (f32[5,8,128]{2,1,0:T(8,128)S(1)}, f32[5,8,128]{2,1,0:T(8,128)S(1)}, u32[]{:S(2)}, u32[]{:S(2)}) collective-permute-start(f32[5,8,128]{2,1,0:T(8,128)S(1)} %get-tuple-element.25), channel_id=1, source_target_pairs={{0,64},{64,0},{128,192},{192,128},{256,320},{320,256},{384,448},{4... | collective-permute-start | bytes 61448 | tf_op jit(solution)/shard_map/ppermute | solution.py:38
  34.9 0.7 copy-start
  34.9 0.7 copy-start.1

commit v3 on v2

--- a/solution.py
+++ b/solution.py
@@ -6,8 +6,7 @@
 from jax.sharding import PartitionSpec as P
 
 SLOTS = 16
-SPAN_Y = 8
-SPAN_Z = 8
+OWNERS = 64
 WALE_COEFF = 0.5
 BASE_VISCOSITY = 0.01
 WALE_FLOOR = 1e-10
@@ -38,40 +37,48 @@
     return lax.ppermute(near, axis, near_pairs), far
 
 
-def pack_vertical(fields, near, far):
+def ring(high, low, axis):
+    count = lax.axis_size(axis)
+    below = lax.ppermute(high, axis, [(i, (i + 1) % count) for i in range(count)])
+    above = lax.ppermute(low, axis, [((i + 1) % count, i) for i in range(count)])
+    return below, above
+
+
+def pack_vertical(scalars, velocity, near, far):
     even = is_even("gz")
+    for out, upper in ((near, even), (far, jnp.logical_not(even))):
+        planes = pl.ds(jnp.where(upper, 4, 0), 4)
+        fluid = scalars[1, planes]
+        out[0] = scalars[0, planes]
+        for axis in range(3):
+            out[1 + axis] = velocity[axis, planes] * fluid
+        out[4] = fluid
+
+
+def pack_spanwise(scalars, velocity, got_far, got_near, planes, high, low):
+    even_z = is_even("gz")
+    front = lax.broadcasted_iota(jnp.int32, (8, 128), 0) < 4
+    fluid = scalars[1]
     for field in range(5):
-        near[field] = jnp.where(even, fields[field, 4:8], fields[field, 0:4])
-        far[field] = jnp.where(even, fields[field, 0:4], fields[field, 4:8])
-
-
-def pack_spanwise(fields, got_far, got_near, planes, near, far):
-    even_z = is_even("gz")
-    even_y = is_even("gy")
-    front = lax.broadcasted_iota(jnp.int32, (8, 128), 0) < 4
-    for field in range(5):
-        planes[field, 4:12] = fields[field]
+        inner = scalars[0] if field == 0 else fluid if field == 4 else velocity[field - 1] * fluid
+        planes[field, 4:12] = inner
         planes[field, 12:16] = jnp.where(even_z, got_near[field], got_far[field])
         planes[field, 0:4] = jnp.where(even_z, got_far[field], got_near[field])
         for pair in range(8):
             one = planes[field, 2 * pair]
             two = planes[field, 2 * pair + 1]
-            high = jnp.where(front, roll(one, 4, 0), two)
-            low = jnp.where(front, one, roll(two, 4, 0))
-            near[field, pair] = jnp.where(even_y, high, low)
-            far[field, pair] = jnp.where(even_y, low, high)
-
-
-def pack_streamwise(planes, got_far, got_near, window, faces, near, far):
-    even_y = is_even("gy")
+            high[field, pair] = jnp.where(front, roll(one, 4, 0), two)
+            low[field, pair] = jnp.where(front, one, roll(two, 4, 0))
+
+
+def pack_streamwise(planes, got_below, got_above, window, faces, near, far):
     even_x = is_even("gx")
     front = lax.broadcasted_iota(jnp.int32, (8, 128), 0) < 4
     lane = lax.broadcasted_iota(jnp.int32, (8, 128), 1)
     for field in range(5):
         own = [jnp.zeros((8, 128), jnp.float32) for _ in range(2)]
         for pair in range(8):
-            above = jnp.where(even_y, got_near[field, pair], got_far[field, pair])
-            below = jnp.where(even_y, got_far[field, pair], got_near[field, pair])
+            above, below = got_above[field, pair], got_below[field, pair]
             outer = (jnp.where(front, above, roll(below, 4, 0)), jnp.where(front, roll(above, 4, 0), below))
             for side in range(2):
                 plane = 2 * pair + side
@@ -109,7 +116,7 @@
     earlier = (owner_column == owner_row) & (row < block)
     owner = owner_row.astype(jnp.int32)
     rank = jnp.sum(jnp.where(earlier, 1.0, 0.0), axis=0, keepdims=True).astype(jnp.int32)
-    position = (lax.rem(owner, SPAN_Z) * SPAN_Y + lax.div(owner, SPAN_Z)) * 2 + rank
+    position = rank * OWNERS + owner
     rows = lax.broadcasted_iota(jnp.int32, (128, 128), 0)
     placing[...] = (rows == position).astype(jnp.float32)
     tags[...] = jnp.broadcast_to(0.5 * (slot + 1.0), (16, 128))
@@ -226,13 +233,56 @@
     return density, momentum, stress, third
 
 
-def two_steps(
-    window, faces, got_far, got_near, placing, tags, moments, relaxation_out, outgoing,
+PAIRS = ((0, 0), (1, 1), (2, 2), (0, 1), (0, 2), (1, 2))
+
+
+def first_state(ref, where):
+    density = ref[(0,) + where]
+    speed = [ref[(1 + k,) + where] for k in range(3)]
+    momentum = [density * speed[k] for k in range(3)]
+    stress = [momentum[one] * speed[two] for one, two in PAIRS]
+    return density, speed, momentum, stress
+
+
+def row_differences(speed):
+    return [roll(value, -1, 0) - roll(value, 1, 0) for value in speed]
+
+
+def lane_differences(speed):
+    return [roll(value, -1, 1) - roll(value, 1, 1) for value in speed]
+
+
+def step_one(window, state, sums):
+    for plane in range(1, 15):
+        density, speed, momentum, stress = first_state(window, (plane,))
+        dz = [window[1 + k, plane + 1] - window[1 + k, plane - 1] for k in range(3)]
+        dy = row_differences(speed)
+        dx = lane_differences(speed)
+        relaxation = wale([[dz[k], dy[k], dx[k]] for k in range(3)])
+        stay, right, left = leaving(density, momentum, collide(momentum, speed, stress, relaxation))
+        right = [roll(value, 1, 1) for value in right]
+        left = [roll(value, -1, 1) for value in left]
+        for k, value in enumerate(plane_sums(stay, right, left)):
+            sums[k, plane] = value
+    for plane in range(2, 14):
+        density, momentum, stress, _ = gather_state(
+            [sums[k, plane] for k in range(6)],
+            [sums[6 + k, plane - 1] for k in range(5)],
+            [sums[11 + k, plane + 1] for k in range(5)],
+            window[4, plane],
+        )
+        for k, value in enumerate([density] + momentum + stress):
+            state[k, plane - 2] = value
+
+
+def step_two(
+    window, state_one, faces, got_far, got_near, placing, tags, moments, relaxation_out, outgoing,
     state, sums, strip, strip_sums, edge, pooled,
 ):
     even_x = is_even("gx")
     lane = lax.broadcasted_iota(jnp.int32, (16, 128), 1)
     first_lane, last_lane = lane == 0, lane == 127
+    first_two, last_two = lane < 2, lane >= 126
     quarter = lax.broadcasted_iota(jnp.int32, (8, 128), 1) % 16 // 4
 
     for field in range(5):
@@ -248,23 +298,11 @@
                     quarter == 2, roll(from_left, 8 - turn, 1), cells
                 )
 
-    def first_state(ref, where):
-        density = ref[(0,) + where]
-        speed = [ref[(1 + k,) + where] for k in range(3)]
-        momentum = [density * speed[k] for k in range(3)]
-        stress = [
-            momentum[one] * speed[two] for one, two in ((0, 0), (1, 1), (2, 2), (0, 1), (0, 2), (1, 2))
-        ]
-        return density, speed, momentum, stress
-
     def strip_above(ref, number, half):
         return ref[number, 1] if half == 0 else roll(ref[number, 0], -16, 1)
 
     def strip_below(ref, number, half):
         return ref[number, 0] if half == 1 else roll(ref[number, 1], 16, 1)
-
-    def row_differences(speed):
-        return [roll(value, -1, 0) - roll(value, 1, 0) for value in speed]
 
     def strip_pass(step, half):
         if step == 0:
@@ -276,72 +314,16 @@
             stress = [strip[8 + k, half] for k in range(6)]
         dz = [strip_above(strip, 1 + k, half) - strip_below(strip, 1 + k, half) for k in range(3)]
         dy = row_differences(speed)
-        dx = [roll(value, -1, 1) - roll(value, 1, 1) for value in speed]
+        dx = lane_differences(speed)
         relaxation = wale([[dz[k], dy[k], dx[k]] for k in range(3)])
-        stay, right, left = leaving(density, momentum, collide(momentum, speed, stress, relaxation))
-        for k in range(5):
-            edge[k, half] = right[k]
-            edge[5 + k, half] = left[k]
-        if step == 0:
-            moved_right = [roll(value, 1, 1) for value in right]
-            moved_left = [roll(value, -1, 1) for value in left]
-            for k, value in enumerate(plane_sums(stay, moved_right, moved_left)):
-                strip_sums[k, half] = value
-
-    def from_left_lane(value, ref, number, half, turn):
-        return jnp.where(first_lane, roll(ref[number, half], 117 - turn, 1), roll(value, 1, 1))
-
-    def from_right_lane(value, ref, number, half, turn):
-        return jnp.where(last_lane, roll(ref[number, half], 123 - turn, 1), roll(value, -1, 1))
-
-    def plane_pass(step, plane, speeds):
-        half, turn = plane % 2, plane // 2 * 16
-        if step == 0:
-            density, speed, momentum, stress = first_state(window, (plane,))
-        else:
-            density = state[0, plane]
-            speed = [state[1 + k, plane] for k in range(3)]
-            momentum = [state[4 + k, plane] for k in range(3)]
-            stress = [state[7 + k, plane] for k in range(6)]
-        dz = [speeds[1 + k, plane + 1] - speeds[1 + k, plane - 1] for k in range(3)]
-        dy = row_differences(speed)
-        dx = [
-            from_right_lane(speed[k], strip, 1 + k, half, turn) - from_left_lane(speed[k], strip, 1 + k, half, turn)
-            for k in range(3)
-        ]
-        relaxation = wale([[dz[k], dy[k], dx[k]] for k in range(3)])
-        stay, right, left = leaving(density, momentum, collide(momentum, speed, stress, relaxation))
-        return relaxation, stay, right, left, half, turn
-
-    def move_lanes(right, left, half, turn):
-        moved_right = [from_left_lane(value, edge, k, half, turn) for k, value in enumerate(right)]
-        moved_left = [from_right_lane(value, edge, 5 + k, half, turn) for k, value in enumerate(left)]
-        return moved_right, moved_left
+        return leaving(density, momentum, collide(momentum, speed, stress, relaxation))
 
     for half in range(2):
-        strip_pass(0, half)
-
-    for plane in range(1, 15):
-        _, stay, right, left, half, turn = plane_pass(0, plane, window)
-        moved_right, moved_left = move_lanes(right, left, half, turn)
-        for k, value in enumerate(plane_sums(stay, moved_right, moved_left)):
-            sums[k, plane] = value
-
-    for plane in range(2, 14):
-        density, momentum, stress, _ = gather_state(
-            [sums[k, plane] for k in range(6)],
-            [sums[6 + k, plane - 1] for k in range(5)],
-            [sums[11 + k, plane + 1] for k in range(5)],
-            window[4, plane],
-        )
-        inverse = 1.0 / density
-        state[0, plane] = density
-        for k in range(3):
-            state[1 + k, plane] = momentum[k] * inverse
-            state[4 + k, plane] = momentum[k]
-        for k in range(6):
-            state[7 + k, plane] = stress[k]
-
+        stay, right, left = strip_pass(0, half)
+        right = [roll(value, 1, 1) for value in right]
+        left = [roll(value, -1, 1) for value in left]
+        for k, value in enumerate(plane_sums(stay, right, left)):
+            strip_sums[k, half] = value
     for half in range(2):
         density, momentum, stress, _ = gather_state(
             [strip_sums[k, half] for k in range(6)],
@@ -356,26 +338,61 @@
             strip[5 + k, half] = momentum[k]
         for k in range(6):
             strip[8 + k, half] = stress[k]
+
+    for plane in range(2, 14):
+        half, turn = plane % 2, plane // 2 * 16
+        members = []
+        for k, number in enumerate((0, 5, 6, 7, 8, 9, 10, 11, 12, 13)):
+            value = jnp.where(first_two, roll(strip[number, half], -12 - turn, 1), state_one[k, plane - 2])
+            members.append(jnp.where(last_two, roll(strip[number, half], 124 - turn, 1), value))
+        inverse = 1.0 / members[0]
+        for k in range(3):
+            members.append(members[1 + k] * inverse)
+        for k in range(13):
+            state[k, plane] = members[k]
+
     for half in range(2):
-        strip_pass(1, half)
+        _, right, left = strip_pass(1, half)
+        for k in range(5):
+            edge[k, half] = right[k]
+            edge[5 + k, half] = left[k]
 
     for plane in range(3, 13):
-        relaxation, stay, right, left, half, turn = plane_pass(1, plane, state)
-        moved_right, moved_left = move_lanes(right, left, half, turn)
-        for k, value in enumerate(plane_sums(stay, moved_right, moved_left)):
-            sums[k, plane] = value
+        half, turn = plane % 2, plane // 2 * 16
+
+        def from_left_lane(value, ref, number):
+            return jnp.where(first_lane, roll(ref[number, half], 117 - turn, 1), roll(value, 1, 1))
+
+        def from_right_lane(value, ref, number):
+            return jnp.where(last_lane, roll(ref[number, half], 123 - turn, 1), roll(value, -1, 1))
+
+        density = state[0, plane]
+        momentum = [state[1 + k, plane] for k in range(3)]
+        stress = [state[4 + k, plane] for k in range(6)]
+        speed = [state[10 + k, plane] for k in range(3)]
+        dz = [state[10 + k, plane + 1] - state[10 + k, plane - 1] for k in range(3)]
+        dy = row_differences(speed)
+        dx = [
+            from_right_lane(speed[k], strip, 1 + k) - from_left_lane(speed[k], strip, 1 + k)
+            for k in range(3)
+        ]
+        relaxation = wale([[dz[k], dy[k], dx[k]] for k in range(3)])
+        stay, right, left = leaving(density, momentum, collide(momentum, speed, stress, relaxation))
+        right = [from_left_lane(value, edge, k) for k, value in enumerate(right)]
+        left = [from_right_lane(value, edge, 5 + k) for k, value in enumerate(left)]
+        for k, value in enumerate(plane_sums(stay, right, left)):
+            sums[k, plane] = value[0:8]
         if 4 <= plane < 12:
             relaxation_out[plane - 4] = relaxation[0:8]
 
     for pair in range(4):
         total = None
-        for side in range(2):
-            low = 2 * pair + side
+        for low in (2 * pair, 2 * pair + 1):
             plane = low + 4
             density, momentum, stress, third = gather_state(
-                [sums[k, plane, 0:8] for k in range(6)],
-                [sums[6 + k, plane - 1, 0:8] for k in range(5)],
-                [sums[11 + k, plane + 1, 0:8] for k in range(5)],
+                [sums[k, plane] for k in range(6)],
+                [sums[6 + k, plane - 1] for k in range(5)],
+                [sums[11 + k, plane + 1] for k in range(5)],
                 window[4, plane, 0:8],
             )
             members = [density] + momentum + [stress[k] + third for k in range(3)] + stress[3:]
@@ -386,23 +403,23 @@
             pooled[k * 32 + pair * 8 : k * 32 + pair * 8 + 8, :] = total[k]
 
     blocks = 0.125 * (pooled[pl.ds(0, 160, stride=2), :] + pooled[pl.ds(1, 160, stride=2), :])
-    payload = jnp.concatenate([blocks, tags[...]], axis=0)
-    outgoing[...] = pick(placing[...], payload, ((1,), (1,)))
-
-
-def sum_by_slot(arrived, outgoing):
-    row = lax.broadcasted_iota(jnp.int32, (128, 128), 0)
-    column = lax.broadcasted_iota(jnp.int32, (128, 128), 1)
-    tag = jnp.broadcast_to(arrived[:, 160:161], (128, 128))
-    chosen = (column // SLOTS == row // 2 % SPAN_Y) & (tag == (column % SLOTS + 1).astype(jnp.float32))
-    outgoing[...] = pick(chosen.astype(jnp.float32), arrived[:, 0:160], ((0,), (0,)))
-
-
-def sum_senders(arrived, coarse):
-    total = arrived[0]
-    for sender in range(1, arrived.shape[0]):
-        total = total + arrived[sender]
-    coarse[...] = total
+    payload = jnp.concatenate(
+        [blocks, jnp.zeros((32, 128), jnp.float32), tags[...], jnp.zeros((48, 128), jnp.float32)], axis=0
+    )
+    placed = pick(placing[...], payload, ((1,), (1,)))
+    outgoing[:, 0:128] = placed[0:OWNERS, 0:128]
+    outgoing[:, 128:256] = placed[0:OWNERS, 128:256] + roll(placed[OWNERS:, 128:256], 32, 1)
+    outgoing[:, 256:384] = placed[OWNERS:, 0:128]
+
+
+def sum_slots(arrived, coarse):
+    slot = lax.broadcasted_iota(jnp.int32, (OWNERS, 128), 1).astype(jnp.float32)
+    one = (arrived[:, 192:193] == slot + 1.0).astype(jnp.float32)
+    two = (arrived[:, 224:225] == slot + 1.0).astype(jnp.float32)
+    ones = pick(one, arrived[:, 0:256], ((0,), (0,)))[0:SLOTS]
+    twos = pick(two, arrived[:, 128:384], ((0,), (0,)))[0:SLOTS]
+    coarse[:, 0:128] = ones[:, 0:128] + twos[:, 128:256]
+    coarse[:, 128:160] = (ones[:, 128:256] + roll(twos[:, 0:128], -32, 1))[:, 0:32]
 
 
 def call(kernel, outs, name, scratch=(), in_hbm=0, vmem=48):
@@ -421,37 +438,39 @@
         (pltpu.VMEM((1, 64), jnp.int32), pltpu.VMEM((1, 64), jnp.int32), pltpu.SemaphoreType.DMA((2,))),
         2,
     )(owner_map.reshape(1, 64), slot_map.reshape(1, 64))
-    fluid = 1.0 - solid.astype(jnp.float32)
-    fields = jnp.concatenate([density[None], velocity * fluid, fluid[None]])
-    near, far = call(pack_vertical, (f32(5, 4, 8, 128),) * 2, "pack_vertical")(fields)
+    scalars = jnp.concatenate([density[None], 1.0 - solid[None].astype(jnp.float32)])
+    near, far = call(pack_vertical, (f32(5, 4, 8, 128),) * 2, "pack_vertical")(scalars, velocity)
     near, far = swap(near, far, "gz")
-    planes, near, far = call(
+    planes, high, low = call(
         pack_spanwise, (f32(5, 16, 8, 128), f32(5, 8, 8, 128), f32(5, 8, 8, 128)), "pack_spanwise"
-    )(fields, far, near)
-    near, far = swap(near, far, "gy")
+    )(scalars, velocity, far, near)
+    below, above = ring(high, low, "gy")
     window, faces, near, far = call(
         pack_streamwise,
         (f32(5, 16, 16, 128), f32(5, 2, 8, 128), f32(5, 8, 128), f32(5, 8, 128)),
         "pack_streamwise",
-    )(planes, far, near)
+    )(planes, below, above)
     near, far = swap(near, far, "gx")
+    state = call(
+        step_one, f32(10, 12, 16, 128), "step_one", (pltpu.VMEM((16, 16, 16, 128), jnp.float32),)
+    )(window)
     moments, relaxation, outgoing = call(
-        two_steps,
-        (f32(10, 8, 8, 128), f32(8, 8, 128), f32(128, 176)),
-        "two_steps",
+        step_two,
+        (f32(10, 8, 8, 128), f32(8, 8, 128), f32(OWNERS, 384)),
+        "step_two",
         (
             pltpu.VMEM((13, 16, 16, 128), jnp.float32),
-            pltpu.VMEM((16, 16, 16, 128), jnp.float32),
+            pltpu.VMEM((16, 16, 8, 128), jnp.float32),
             pltpu.VMEM((14, 2, 16, 128), jnp.float32),
             pltpu.VMEM((16, 2, 16, 128), jnp.float32),
             pltpu.VMEM((10, 2, 16, 128), jnp.float32),
             pltpu.VMEM((320, 128), jnp.float32),
         ),
-    )(window, faces, far, near, placing, tags)
-    arrived = lax.all_to_all(outgoing.reshape(SPAN_Z, 2 * SPAN_Y, 176), "gz", split_axis=0, concat_axis=0, tiled=True)
-    outgoing = call(sum_by_slot, f32(128, 160), "sum_by_slot")(arrived.reshape(128, 176))
-    arrived = lax.all_to_all(outgoing.reshape(SPAN_Y, SLOTS, 160), "gy", split_axis=0, concat_axis=0, tiled=True)
-    coarse = call(sum_senders, f32(SLOTS, 160), "sum_senders")(arrived)
+    )(window, state, faces, far, near, placing, tags)
+    arrived = lax.all_to_all(
+        outgoing.reshape(OWNERS, 1, 384), ("gy", "gz"), split_axis=0, concat_axis=0, tiled=True
+    )
+    coarse = call(sum_slots, f32(SLOTS, 160), "sum_slots")(arrived.reshape(OWNERS, 384))
     return moments, relaxation, coarse.reshape(1, 1, 1, SLOTS, 160)
 
 

time: 67.5 us -> 57.5 us (0.85)
  blocking collectives: 24.2 us -> 17.3 us
  starting transfers between devices: 27.8 us -> 24.2 us
  waiting for transfers between devices: 6.02 us -> 7.75 us
    all_to_all x2 -> x1, blocking collectives: 24.2 us -> 17.3 us  [per_device(): lax.all_to_all(outgoing.reshape(OWNERS, 1, 384), ('gy', 'gz'), split_axis...]
    ppermute x3 -> x2, starting transfers between devices: 21.2 us -> 16.3 us  [swap(): far = lax.ppermute(far, axis, far_pairs)]
    ppermute x0 -> x2, waiting for transfers between devices: none -> 4.19 us  [the longest x1 2.77 us: ring(): lax.ppermute(low, axis, [((i + 1) % count, i) for i in range(count)])]
    ppermute x0 -> x2, starting transfers between devices: none -> 4.06 us  [the longest x1 3.21 us: ring(): lax.ppermute(high, axis, [(i, (i + 1) % count) for i in range(count)])]
    ppermute x3 -> x2, starting transfers between devices: 6.58 us -> 3.84 us  [swap(): return (lax.ppermute(near, axis, near_pairs), far)]
    ppermute x3 -> x2, waiting for transfers between devices: 5.77 us -> 3.56 us  [swap(): return (lax.ppermute(near, axis, near_pairs), far)]
    unnamed x8 -> x9, local copies, waits for them, and re-layouts: 1.5 us -> 0.77 us
  transfers between devices with their start and end apart: 6 -> 6, of which waited for: 4 -> 4; matrix products, arithmetic and copies ran while one was open for 0% -> 0% of each run, Pallas kernels for 0% -> 3%
where the time goes in v3:
time: 57.5 us; the launch traced here: 57.2 us
  starting transfers between devices  24.2 us (42%)
  blocking collectives  17.3 us (30%)
  waiting for transfers between devices  7.75 us (13%)
  Pallas kernels  5.55 us (10%)
  local copies, waits for them, and re-layouts  0.87 us (2%)
  other arithmetic  0.8 us (1%)
  between operations  0.75 us (1%)
    all_to_all x1, blocking collectives, per_device(): lax.all_to_all(outgoing.reshape(OWNERS, 1, 384), ('gy', 'gz'), split_axis...  17.3 us
    ppermute x2, starting transfers between devices, swap(): far = lax.ppermute(far, axis, far_pairs)  16.3 us
    ppermute x2, starting transfers between devices, swap(): return (lax.ppermute(near, axis, near_pairs), far)  3.84 us
    ppermute x2, waiting for transfers between devices, swap(): return (lax.ppermute(near, axis, near_pairs), far)  3.56 us
    ppermute x1, starting transfers between devices, ring(): lax.ppermute(high, axis, [(i, (i + 1) % count) for i in range(count)])  3.21 us
    ppermute x1, waiting for transfers between devices, ring(): lax.ppermute(low, axis, [((i + 1) % count, i) for i in range(count)])  2.77 us
    pallas_call x1, Pallas kernels, per_device(): call(step_two, (f32(10, 8, 8, 128), f32(8, 8, 128), f32(OWNERS, 384)), 's...  2.53 us
    pallas_call x1, Pallas kernels, per_device(): call(step_one, f32(10, 12, 16, 128), 'step_one', (pltpu.VMEM((16, 16, 16,...  1.44 us
  transfers between devices with their start and end apart: 6, of which 4 were waited for; matrix products, arithmetic and copies ran while one was open for 0% of the time, Pallas kernels for 3%

profile of v3, /device:TPU:1, one launch (start us, length us, event | category | flops | bytes accessed | tf_op | source)
XLA Modules:
  0.0 57.2 jit_solution(10886951404016014669)
XLA Ops:
  0.6 0.0 copy-start.3
  0.6 0.0 copy-start
  0.7 0.8 %subtract_bitcast_fusion = f32[1,8,8,128]{3,2,1,0:T(8,128)S(1)} fusion(s32[8,8,128]{2,1,0:T(8,128)} %param.7), kind=kLoop, calls=%fused_computation.2 | loop fusion | flops 16384 | bytes 65536 | tf_op jit(solution)/shard_map/sub | solution.py:441
  1.4 0.0 copy-done.3
  1.5 0.1 copy-done
  1.6 5.9 %collective-permute-start = (f32[5,4,8,128]{3,2,1,0:T(8,128)S(1)}, f32[5,4,8,128]{3,2,1,0:T(8,128)S(1)}, u32[]{:S(2)}, u32[]{:S(2)}) collective-permute-start(f32[5,4,8,128]{3,2,1,0:T(8,128)S(1)} %get-tuple-element.17), channel_id=1, source_target_pairs={{0,7},{1,2},{2,1},{3,4},{4,3},{5,6},{6,5},{7,0},{8,15},{9,10},{10,... | collective-permute-start | bytes 245768 | tf_op jit(solution)/shard_map/ppermute | solution.py:36
  7.5 1.9 %collective-permute-start.1 = (f32[5,4,8,128]{3,2,1,0:T(8,128)S(1)}, f32[5,4,8,128]{3,2,1,0:T(8,128)S(1)}, u32[]{:S(2)}, u32[]{:S(2)}) collective-permute-start(f32[5,4,8,128]{3,2,1,0:T(8,128)S(1)} %get-tuple-element.18), channel_id=1, source_target_pairs={{0,1},{1,0},{2,3},{3,2},{4,5},{5,4},{6,7},{7,6},{8,9},{9,8},{10,11... | collective-permute-start | bytes 245768 | tf_op jit(solution)/shard_map/ppermute | solution.py:37
  9.4 0.0 collective-permute-done.got_far
  9.4 3.2 %collective-permute-done.1.got_near = f32[5,4,8,128]{3,2,1,0:T(8,128)S(1)} collective-permute-done((f32[5,4,8,128]{3,2,1,0:T(8,128)S(1)}, f32[5,4,8,128]{3,2,1,0:T(8,128)S(1)}, u32[]{:S(2)}, u32[]{:S(2)}) %collective-permute-start.1) | collective-permute-done | bytes 81952 | tf_op jit(solution)/shard_map/ppermute | solution.py:37
  12.7 3.2 %collective-permute-start.2 = (f32[5,8,8,128]{3,2,1,0:T(8,128)S(1)}, f32[5,8,8,128]{3,2,1,0:T(8,128)S(1)}, u32[]{:S(2)}, u32[]{:S(2)}) collective-permute-start(f32[5,8,8,128]{3,2,1,0:T(8,128)S(1)} %get-tuple-element.20), channel_id=1, source_target_pairs={{0,8},{8,16},{16,24},{24,32},{32,40},{40,48},{48,56},{56,0},{1,9},... | collective-permute-start | bytes 491528 | tf_op jit(solution)/shard_map/ppermute | solution.py:42
  16.0 0.8 %collective-permute-start.3 = (f32[5,8,8,128]{3,2,1,0:T(8,128)S(1)}, f32[5,8,8,128]{3,2,1,0:T(8,128)S(1)}, u32[]{:S(2)}, u32[]{:S(2)}) collective-permute-start(f32[5,8,8,128]{3,2,1,0:T(8,128)S(1)} %get-tuple-element.21), channel_id=1, source_target_pairs={{8,0},{16,8},{24,16},{32,24},{40,32},{48,40},{56,48},{0,56},{9,1},... | collective-permute-start | bytes 491528 | tf_op jit(solution)/shard_map/ppermute | solution.py:43
  16.8 1.4 %collective-permute-done.2.got_below = f32[5,8,8,128]{3,2,1,0:T(8,128)S(1)} collective-permute-done((f32[5,8,8,128]{3,2,1,0:T(8,128)S(1)}, f32[5,8,8,128]{3,2,1,0:T(8,128)S(1)}, u32[]{:S(2)}, u32[]{:S(2)}) %collective-permute-start.2) | collective-permute-done | bytes 163872 | tf_op jit(solution)/shard_map/ppermute | solution.py:42
  18.2 2.8 %collective-permute-done.3.got_above = f32[5,8,8,128]{3,2,1,0:T(8,128)S(1)} collective-permute-done((f32[5,8,8,128]{3,2,1,0:T(8,128)S(1)}, f32[5,8,8,128]{3,2,1,0:T(8,128)S(1)}, u32[]{:S(2)}, u32[]{:S(2)}) %collective-permute-start.3) | collective-permute-done | bytes 163872 | tf_op jit(solution)/shard_map/ppermute | solution.py:43
  21.0 0.4 pack_streamwise.1
  21.4 10.4 %collective-permute-start.4 = (f32[5,8,128]{2,1,0:T(8,128)S(1)}, f32[5,8,128]{2,1,0:T(8,128)S(1)}, u32[]{:S(2)}, u32[]{:S(2)}) collective-permute-start(f32[5,8,128]{2,1,0:T(8,128)S(1)} %get-tuple-element.24), channel_id=1, source_target_pairs={{0,448},{64,128},{128,64},{192,256},{256,192},{320,384},{384,320},... | collective-permute-start | bytes 61448 | tf_op jit(solution)/shard_map/ppermute | solution.py:36
  31.7 1.9 %collective-permute-start.5 = (f32[5,8,128]{2,1,0:T(8,128)S(1)}, f32[5,8,128]{2,1,0:T(8,128)S(1)}, u32[]{:S(2)}, u32[]{:S(2)}) collective-permute-start(f32[5,8,128]{2,1,0:T(8,128)S(1)} %get-tuple-element.25), channel_id=1, source_target_pairs={{0,64},{64,0},{128,192},{192,128},{256,320},{320,256},{384,448},{4... | collective-permute-start | bytes 61448 | tf_op jit(solution)/shard_map/ppermute | solution.py:37
  33.7 0.0 copy-start.1
  33.7 0.0 copy-start.2
  33.7 0.6 %copy-done.1 = s32[1,1,1,64,1]{3,4,2,1,0:T(1,128)S(1)} copy-done((s32[1,1,1,64,1]{3,4,2,1,0:T(1,128)S(1)}, s32[1,1,1,64,1]{3,4,2,1,0:T(1,128)}, u32[]{:S(2)}) %copy-start.1) | copy-done | bytes 280
  34.3 0.0 copy-done.2
  34.3 0.1 place_blocks.1
  34.5 1.4 %step_one.1.state_one = f32[10,12,16,128]{3,2,1,0:T(8,128)S(1)} custom-call(f32[5,16,16,128]{3,2,1,0:T(8,128)S(1)} %get-tuple-element.22.window), custom_call_target="tpu_custom_call" | custom-call | tf_op jit(solution)/shard_map/step_one/pallas_call | solution.py:454
  35.9 0.0 collective-permute-done.4.got_far
  36.0 0.3 collective-permute-done.5.got_near
  36.3 2.5 %step_two.1 = (f32[10,8,8,128]{3,2,1,0:T(8,128)}, f32[8,8,128]{2,1,0:T(8,128)}, f32[64,384]{1,0:T(8,128)S(1)}) custom-call(f32[5,16,16,128]{3,2,1,0:T(8,128)S(1)} %get-tuple-element.22.window, f32[10,12,16,128]{3,2,1,0:T(8,128)S(1)} %step_one.1.state_one, f32[5,2,8,128]{3,2,1,0:T(8,128)S(1)} %get-tuple-element.23.faces, ...), custom_call_target="tpu_custom_call" | custom-call | tf_op jit(solution)/shard_map/step_two/pallas_call | solution.py:457
  38.8 0.1 copy.8
  38.9 17.3 %all_to_all.5 = f32[64,1,384]{2,1,0:T(1,128)S(1)} all-to-all(f32[64,1,384]{2,1,0:T(1,128)S(1)} %copy.8), channel_id=1, replica_groups=mesh['gx'=8,'gy'=8,'gz'=8] {'gy','gz'}, dimensions={0} | all-to-all | bytes 196608 | tf_op jit(solution)/shard_map/all_to_all | solution.py:470
  56.2 1.0 %sum_slots.1 = f32[16,160]{1,0:T(8,128)} custom-call(f32[64,384]{1,0:T(8,128)S(1)} %bitcast.10), custom_call_target="tpu_custom_call" | custom-call | tf_op jit(solution)/shard_map/sum_slots/pallas_call | solution.py:473
  (4 shorter events, 0.1 us)
Async XLA Ops:
  0.6 0.8 %copy-start.3 = (f32[8,8,128]{2,1,0:T(8,128)S(1)}, f32[8,8,128]{2,1,0:T(8,128)}, u32[]{:S(2)}) copy-start(f32[8,8,128]{2,1,0:T(8,128)} %param.5) | copy-start | bytes 98308
  0.6 0.9 %copy-start = (f32[3,8,8,128]{3,2,1,0:T(8,128)S(1)}, f32[3,8,8,128]{3,2,1,0:T(8,128)}, u32[]{:S(2)}) copy-start(f32[3,8,8,128]{3,2,1,0:T(8,128)} %velocity.3) | copy-start | bytes 294916
  1.6 7.9 %collective-permute-start = (f32[5,4,8,128]{3,2,1,0:T(8,128)S(1)}, f32[5,4,8,128]{3,2,1,0:T(8,128)S(1)}, u32[]{:S(2)}, u32[]{:S(2)}) collective-permute-start(f32[5,4,8,128]{3,2,1,0:T(8,128)S(1)} %get-tuple-element.17), channel_id=1, source_target_pairs={{0,7},{1,2},{2,1},{3,4},{4,3},{5,6},{6,5},{7,0},{8,15},{9,10},{10,... | collective-permute-start | bytes 245768 | tf_op jit(solution)/shard_map/ppermute | solution.py:36
  7.5 5.2 %collective-permute-start.1 = (f32[5,4,8,128]{3,2,1,0:T(8,128)S(1)}, f32[5,4,8,128]{3,2,1,0:T(8,128)S(1)}, u32[]{:S(2)}, u32[]{:S(2)}) collective-permute-start(f32[5,4,8,128]{3,2,1,0:T(8,128)S(1)} %get-tuple-element.18), channel_id=1, source_target_pairs={{0,1},{1,0},{2,3},{3,2},{4,5},{5,4},{6,7},{7,6},{8,9},{9,8},{10,11... | collective-permute-start | bytes 245768 | tf_op jit(solution)/shard_map/ppermute | solution.py:37
  12.7 5.5 %collective-permute-start.2 = (f32[5,8,8,128]{3,2,1,0:T(8,128)S(1)}, f32[5,8,8,128]{3,2,1,0:T(8,128)S(1)}, u32[]{:S(2)}, u32[]{:S(2)}) collective-permute-start(f32[5,8,8,128]{3,2,1,0:T(8,128)S(1)} %get-tuple-element.20), channel_id=1, source_target_pairs={{0,8},{8,16},{16,24},{24,32},{32,40},{40,48},{48,56},{56,0},{1,9},... | collective-permute-start | bytes 491528 | tf_op jit(solution)/shard_map/ppermute | solution.py:42
  16.0 5.0 %collective-permute-start.3 = (f32[5,8,8,128]{3,2,1,0:T(8,128)S(1)}, f32[5,8,8,128]{3,2,1,0:T(8,128)S(1)}, u32[]{:S(2)}, u32[]{:S(2)}) collective-permute-start(f32[5,8,8,128]{3,2,1,0:T(8,128)S(1)} %get-tuple-element.21), channel_id=1, source_target_pairs={{8,0},{16,8},{24,16},{32,24},{40,32},{48,40},{56,48},{0,56},{9,1},... | collective-permute-start | bytes 491528 | tf_op jit(solution)/shard_map/ppermute | solution.py:43
  21.4 14.6 %collective-permute-start.4 = (f32[5,8,128]{2,1,0:T(8,128)S(1)}, f32[5,8,128]{2,1,0:T(8,128)S(1)}, u32[]{:S(2)}, u32[]{:S(2)}) collective-permute-start(f32[5,8,128]{2,1,0:T(8,128)S(1)} %get-tuple-element.24), channel_id=1, source_target_pairs={{0,448},{64,128},{128,64},{192,256},{256,192},{320,384},{384,320},... | collective-permute-start | bytes 61448 | tf_op jit(solution)/shard_map/ppermute | solution.py:36
  31.7 4.5 %collective-permute-start.5 = (f32[5,8,128]{2,1,0:T(8,128)S(1)}, f32[5,8,128]{2,1,0:T(8,128)S(1)}, u32[]{:S(2)}, u32[]{:S(2)}) collective-permute-start(f32[5,8,128]{2,1,0:T(8,128)S(1)} %get-tuple-element.25), channel_id=1, source_target_pairs={{0,64},{64,0},{128,192},{192,128},{256,320},{320,256},{384,448},{4... | collective-permute-start | bytes 61448 | tf_op jit(solution)/shard_map/ppermute | solution.py:37
  33.7 0.7 %copy-start.1 = (s32[1,1,1,64,1]{3,4,2,1,0:T(1,128)S(1)}, s32[1,1,1,64,1]{3,4,2,1,0:T(1,128)}, u32[]{:S(2)}) copy-start(s32[1,1,1,64,1]{3,4,2,1,0:T(1,128)} %param.8) | copy-start | bytes 772
  33.7 0.7 %copy-start.2 = (s32[1,1,1,64,1]{3,4,2,1,0:T(1,128)S(1)}, s32[1,1,1,64,1]{3,4,2,1,0:T(1,128)}, u32[]{:S(2)}) copy-start(s32[1,1,1,64,1]{3,4,2,1,0:T(1,128)} %param.9) | copy-start | bytes 772

commit v4 on v3

--- a/solution.py
+++ b/solution.py
@@ -29,14 +29,6 @@
     return lax.rem(lax.axis_index(axis), 2) == 0
 
 
-def swap(near, far, axis):
-    count = lax.axis_size(axis)
-    near_pairs = [(i, i ^ 1) for i in range(count)]
-    far_pairs = [(i, (i + 1) % count if i % 2 else (i - 1) % count) for i in range(count)]
-    far = lax.ppermute(far, axis, far_pairs)
-    return lax.ppermute(near, axis, near_pairs), far
-
-
 def ring(high, low, axis):
     count = lax.axis_size(axis)
     below = lax.ppermute(high, axis, [(i, (i + 1) % count) for i in range(count)])
@@ -44,9 +36,34 @@
     return below, above
 
 
-def pack_vertical(scalars, velocity, near, far):
-    even = is_even("gz")
-    for out, upper in ((near, even), (far, jnp.logical_not(even))):
+def vertical_rings(one, two):
+    span_y, span_z = lax.axis_size("gy"), lax.axis_size("gz")
+    places = [(y, z) for y in range(span_y) for z in range(span_z)]
+
+    def pairs(sense):
+        return [
+            (y * span_z + z, y * span_z + (z + (sense if y % 2 == 0 else -sense)) % span_z) for y, z in places
+        ]
+
+    return lax.ppermute(one, ("gy", "gz"), pairs(1)), lax.ppermute(two, ("gy", "gz"), pairs(-1))
+
+
+def streamwise_swaps(one, two):
+    span_x, span_y = lax.axis_size("gx"), lax.axis_size("gy")
+    places = [(x, y) for x in range(span_x) for y in range(span_y)]
+
+    def pairs(shift):
+        return [
+            (x * span_y + y, (x + (1 if (x + y + shift) % 2 == 0 else -1)) % span_x * span_y + y)
+            for x, y in places
+        ]
+
+    return lax.ppermute(one, ("gx", "gy"), pairs(0)), lax.ppermute(two, ("gx", "gy"), pairs(1))
+
+
+def pack_vertical(scalars, velocity, one, two):
+    even = is_even("gy")
+    for out, upper in ((one, even), (two, jnp.logical_not(even))):
         planes = pl.ds(jnp.where(upper, 4, 0), 4)
         fluid = scalars[1, planes]
         out[0] = scalars[0, planes]
@@ -55,15 +72,16 @@
         out[4] = fluid
 
 
-def pack_spanwise(scalars, velocity, got_far, got_near, planes, high, low):
-    even_z = is_even("gz")
+def pack_spanwise(scalars, velocity, got_one, got_two, placing, planes, high, low):
+    del placing
+    even = is_even("gy")
     front = lax.broadcasted_iota(jnp.int32, (8, 128), 0) < 4
     fluid = scalars[1]
     for field in range(5):
         inner = scalars[0] if field == 0 else fluid if field == 4 else velocity[field - 1] * fluid
         planes[field, 4:12] = inner
-        planes[field, 12:16] = jnp.where(even_z, got_near[field], got_far[field])
-        planes[field, 0:4] = jnp.where(even_z, got_far[field], got_near[field])
+        planes[field, 12:16] = jnp.where(even, got_two[field], got_one[field])
+        planes[field, 0:4] = jnp.where(even, got_one[field], got_two[field])
         for pair in range(8):
             one = planes[field, 2 * pair]
             two = planes[field, 2 * pair + 1]
@@ -71,8 +89,8 @@
             low[field, pair] = jnp.where(front, one, roll(two, 4, 0))
 
 
-def pack_streamwise(planes, got_below, got_above, window, faces, near, far):
-    even_x = is_even("gx")
+def pack_streamwise(planes, got_below, got_above, window, faces, one, two):
+    rightward = is_even("gx") == is_even("gy")
     front = lax.broadcasted_iota(jnp.int32, (8, 128), 0) < 4
     lane = lax.broadcasted_iota(jnp.int32, (8, 128), 1)
     for field in range(5):
@@ -93,8 +111,8 @@
         even_spot = lane % 8 < 4
         to_right = jnp.where(even_spot, own[0], roll(own[1], 4, 1))
         to_left = jnp.where(even_spot, roll(own[0], -4, 1), own[1])
-        near[field] = jnp.where(even_x, to_right, to_left)
-        far[field] = jnp.where(even_x, to_left, to_right)
+        one[field] = jnp.where(rightward, to_right, to_left)
+        two[field] = jnp.where(rightward, to_left, to_right)
 
 
 def place_blocks(owners_in, slots_in, placing, tags, owners, slots, arrived):
@@ -276,18 +294,18 @@
 
 
 def step_two(
-    window, state_one, faces, got_far, got_near, placing, tags, moments, relaxation_out, outgoing,
-    state, sums, strip, strip_sums, edge, pooled,
+    window, state_one, faces, got_one, got_two, placing, tags, moments_out, relaxation_out, outgoing,
+    state, sums, strip, strip_sums, edge, pooled, moments, relaxations, left_sems,
 ):
-    even_x = is_even("gx")
+    rightward = is_even("gx") == is_even("gy")
     lane = lax.broadcasted_iota(jnp.int32, (16, 128), 1)
     first_lane, last_lane = lane == 0, lane == 127
     first_two, last_two = lane < 2, lane >= 126
     quarter = lax.broadcasted_iota(jnp.int32, (8, 128), 1) % 16 // 4
 
     for field in range(5):
-        from_right = jnp.where(even_x, got_near[field], got_far[field])
-        from_left = jnp.where(even_x, got_far[field], got_near[field])
+        from_right = jnp.where(rightward, got_one[field], got_two[field])
+        from_left = jnp.where(rightward, got_two[field], got_one[field])
         for half in range(2):
             for part in range(2):
                 own = faces[field, part]
@@ -383,7 +401,9 @@
         for k, value in enumerate(plane_sums(stay, right, left)):
             sums[k, plane] = value[0:8]
         if 4 <= plane < 12:
-            relaxation_out[plane - 4] = relaxation[0:8]
+            relaxations[plane - 4] = relaxation[0:8]
+    copies = [pltpu.make_async_copy(relaxations, relaxation_out, left_sems.at[4])]
+    copies[0].start()
 
     for pair in range(4):
         total = None
@@ -401,6 +421,9 @@
             total = members if total is None else [one + two for one, two in zip(total, members)]
         for k in range(10):
             pooled[k * 32 + pair * 8 : k * 32 + pair * 8 + 8, :] = total[k]
+        done = pl.ds(2 * pair, 2)
+        copies.append(pltpu.make_async_copy(moments.at[:, done], moments_out.at[:, done], left_sems.at[pair]))
+        copies[-1].start()
 
     blocks = 0.125 * (pooled[pl.ds(0, 160, stride=2), :] + pooled[pl.ds(1, 160, stride=2), :])
     payload = jnp.concatenate(
@@ -410,23 +433,36 @@
     outgoing[:, 0:128] = placed[0:OWNERS, 0:128]
     outgoing[:, 128:256] = placed[0:OWNERS, 128:256] + roll(placed[OWNERS:, 128:256], 32, 1)
     outgoing[:, 256:384] = placed[OWNERS:, 0:128]
+    for copy in copies:
+        copy.wait()
 
 
 def sum_slots(arrived, coarse):
-    slot = lax.broadcasted_iota(jnp.int32, (OWNERS, 128), 1).astype(jnp.float32)
-    one = (arrived[:, 192:193] == slot + 1.0).astype(jnp.float32)
-    two = (arrived[:, 224:225] == slot + 1.0).astype(jnp.float32)
-    ones = pick(one, arrived[:, 0:256], ((0,), (0,)))[0:SLOTS]
-    twos = pick(two, arrived[:, 128:384], ((0,), (0,)))[0:SLOTS]
-    coarse[:, 0:128] = ones[:, 0:128] + twos[:, 128:256]
-    coarse[:, 128:160] = (ones[:, 128:256] + roll(twos[:, 0:128], -32, 1))[:, 0:32]
-
-
-def call(kernel, outs, name, scratch=(), in_hbm=0, vmem=48):
+    slot = lax.broadcasted_iota(jnp.int32, (2 * OWNERS, SLOTS), 1).astype(jnp.float32)
+    shared = arrived[:, 128:256]
+    tag = jnp.concatenate([shared[:, 64:65], shared[:, 96:97]], axis=0)
+    blocks = jnp.concatenate(
+        [
+            jnp.concatenate([arrived[:, 0:128], arrived[:, 256:384]], axis=0),
+            jnp.concatenate([shared, roll(shared, -32, 1)], axis=0),
+        ],
+        axis=1,
+    )
+    total = pick((tag == slot + 1.0).astype(jnp.float32), blocks, ((0,), (0,)))
+    coarse[...] = total[:, 0:160]
+
+
+def call(kernel, outs, name, scratch=(), in_hbm=0, out_spaces=None):
     extra = {"in_specs": [pl.BlockSpec(memory_space=pltpu.HBM)] * in_hbm} if in_hbm else {}
+    if out_spaces:
+        extra["out_specs"] = tuple(pl.BlockSpec(memory_space=space) for space in out_spaces)
     return pl.pallas_call(
-        kernel, out_shape=outs, scratch_shapes=list(scratch), name=name,
-        compiler_params=pltpu.CompilerParams(vmem_limit_bytes=vmem * 1024 * 1024), **extra
+        kernel,
+        out_shape=outs,
+        scratch_shapes=list(scratch),
+        name=name,
+        compiler_params=pltpu.CompilerParams(vmem_limit_bytes=48 * 1024 * 1024),
+        **extra,
     )
 
 
@@ -439,18 +475,18 @@
         2,
     )(owner_map.reshape(1, 64), slot_map.reshape(1, 64))
     scalars = jnp.concatenate([density[None], 1.0 - solid[None].astype(jnp.float32)])
-    near, far = call(pack_vertical, (f32(5, 4, 8, 128),) * 2, "pack_vertical")(scalars, velocity)
-    near, far = swap(near, far, "gz")
+    one, two = call(pack_vertical, (f32(5, 4, 8, 128),) * 2, "pack_vertical")(scalars, velocity)
+    one, two = vertical_rings(one, two)
     planes, high, low = call(
         pack_spanwise, (f32(5, 16, 8, 128), f32(5, 8, 8, 128), f32(5, 8, 8, 128)), "pack_spanwise"
-    )(scalars, velocity, far, near)
+    )(scalars, velocity, one, two, placing)
     below, above = ring(high, low, "gy")
-    window, faces, near, far = call(
+    window, faces, one, two = call(
         pack_streamwise,
         (f32(5, 16, 16, 128), f32(5, 2, 8, 128), f32(5, 8, 128), f32(5, 8, 128)),
         "pack_streamwise",
     )(planes, below, above)
-    near, far = swap(near, far, "gx")
+    one, two = streamwise_swaps(one, two)
     state = call(
         step_one, f32(10, 12, 16, 128), "step_one", (pltpu.VMEM((16, 16, 16, 128), jnp.float32),)
     )(window)
@@ -465,8 +501,12 @@
             pltpu.VMEM((16, 2, 16, 128), jnp.float32),
             pltpu.VMEM((10, 2, 16, 128), jnp.float32),
             pltpu.VMEM((320, 128), jnp.float32),
+            pltpu.VMEM((10, 8, 8, 128), jnp.float32),
+            pltpu.VMEM((8, 8, 128), jnp.float32),
+            pltpu.SemaphoreType.DMA((5,)),
         ),
-    )(window, state, faces, far, near, placing, tags)
+        out_spaces=(pltpu.HBM, pltpu.HBM, pltpu.VMEM),
+    )(window, state, faces, one, two, placing, tags)
     arrived = lax.all_to_all(
         outgoing.reshape(OWNERS, 1, 384), ("gy", "gz"), split_axis=0, concat_axis=0, tiled=True
     )

time: 57.5 us -> 58.1 us (1.010)
  blocking collectives: 17.3 us -> 19.3 us
  waiting for transfers between devices: 7.75 us -> 6.23 us
    ppermute x1, starting transfers between devices: 3.21 us -> 0.11 us  [ring(): lax.ppermute(high, axis, [(i, (i + 1) % count) for i in range(count)])]
    ppermute x1, starting transfers between devices: 0.84 us -> 3.58 us  [ring(): lax.ppermute(low, axis, [((i + 1) % count, i) for i in range(count)])]
    ppermute x1, waiting for transfers between devices: 2.77 us -> 0.3 us  [ring(): lax.ppermute(low, axis, [((i + 1) % count, i) for i in range(count)])]
    all_to_all x1, blocking collectives: 17.3 us -> 19.3 us  [per_device(): lax.all_to_all(outgoing.reshape(OWNERS, 1, 384), ('gy', 'gz'), split_axis...]
    ppermute x4, waiting for transfers between devices: 3.56 us -> 5.07 us  [the longest x1 3.63 us: vertical_rings(): lax.ppermute(two, ('gy', 'gz'), pairs(-1))]
    ppermute x4, starting transfers between devices: 20.1 us -> 20.7 us  [the longest x1 11 us: streamwise_swaps(): lax.ppermute(one, ('gx', 'gy'), pairs(0))]
where the time goes in v4:
time: 58.1 us; the launch traced here: 57.9 us
  starting transfers between devices  24.4 us (42%)
  blocking collectives  19.3 us (33%)
  waiting for transfers between devices  6.23 us (11%)
  Pallas kernels  5.46 us (9%)
  local copies, waits for them, and re-layouts  0.87 us (1%)
  other arithmetic  0.8 us (1%)
  between operations  0.76 us (1%)
    all_to_all x1, blocking collectives, per_device(): lax.all_to_all(outgoing.reshape(OWNERS, 1, 384), ('gy', 'gz'), split_axis...  19.3 us
    ppermute x1, starting transfers between devices, streamwise_swaps(): lax.ppermute(one, ('gx', 'gy'), pairs(0))  11 us
    ppermute x1, starting transfers between devices, vertical_rings(): lax.ppermute(one, ('gy', 'gz'), pairs(1))  5.93 us
    ppermute x1, waiting for transfers between devices, vertical_rings(): lax.ppermute(two, ('gy', 'gz'), pairs(-1))  3.63 us
    ppermute x1, starting transfers between devices, ring(): lax.ppermute(low, axis, [((i + 1) % count, i) for i in range(count)])  3.58 us
    pallas_call x1, Pallas kernels, per_device(): call(step_two, (f32(10, 8, 8, 128), f32(8, 8, 128), f32(OWNERS, 384)), 's...  2.52 us
    ppermute x1, starting transfers between devices, vertical_rings(): lax.ppermute(two, ('gy', 'gz'), pairs(-1))  1.92 us
    ppermute x1, starting transfers between devices, streamwise_swaps(): lax.ppermute(two, ('gx', 'gy'), pairs(1))  1.92 us
  transfers between devices with their start and end apart: 6, of which 4 were waited for; matrix products, arithmetic and copies ran while one was open for 0% of the time, Pallas kernels for 3%

profile of v4, /device:TPU:1, one launch (start us, length us, event | category | flops | bytes accessed | tf_op | source)
XLA Modules:
  0.0 57.9 jit_solution(16919913193533252100)
XLA Ops:
  0.6 0.0 copy-start.3
  0.6 0.0 copy-start
  0.7 0.8 %subtract_bitcast_fusion = f32[1,8,8,128]{3,2,1,0:T(8,128)S(1)} fusion(s32[8,8,128]{2,1,0:T(8,128)} %param.7), kind=kLoop, calls=%fused_computation.2 | loop fusion | flops 16384 | bytes 65536 | tf_op jit(solution)/shard_map/sub | solution.py:477
  1.4 0.0 copy-done.3
  1.5 0.1 copy-done
  1.6 5.9 %collective-permute-start = (f32[5,4,8,128]{3,2,1,0:T(8,128)S(1)}, f32[5,4,8,128]{3,2,1,0:T(8,128)S(1)}, u32[]{:S(2)}, u32[]{:S(2)}) collective-permute-start(f32[5,4,8,128]{3,2,1,0:T(8,128)S(1)} %get-tuple-element.17), channel_id=1, source_target_pairs={{0,1},{1,2},{2,3},{3,4},{4,5},{5,6},{6,7},{7,0},{8,15},{9,8},{10,9... | collective-permute-start | bytes 245768 | tf_op jit(solution)/shard_map/ppermute | solution.py:48
  7.5 1.9 %collective-permute-start.1 = (f32[5,4,8,128]{3,2,1,0:T(8,128)S(1)}, f32[5,4,8,128]{3,2,1,0:T(8,128)S(1)}, u32[]{:S(2)}, u32[]{:S(2)}) collective-permute-start(f32[5,4,8,128]{3,2,1,0:T(8,128)S(1)} %get-tuple-element.18), channel_id=1, source_target_pairs={{0,7},{1,0},{2,1},{3,2},{4,3},{5,4},{6,5},{7,6},{8,9},{9,10},{10,1... | collective-permute-start | bytes 245768 | tf_op jit(solution)/shard_map/ppermute | solution.py:48
  9.4 0.0 copy-start.1
  9.5 0.0 copy-start.2
  9.5 0.6 %copy-done.1 = s32[1,1,1,64,1]{3,4,2,1,0:T(1,128)S(1)} copy-done((s32[1,1,1,64,1]{3,4,2,1,0:T(1,128)S(1)}, s32[1,1,1,64,1]{3,4,2,1,0:T(1,128)}, u32[]{:S(2)}) %copy-start.1) | copy-done | bytes 280
  10.1 0.0 copy-done.2
  10.1 0.1 place_blocks.1
  10.3 0.0 collective-permute-done.got_one
  10.3 3.6 %collective-permute-done.1.got_two = f32[5,4,8,128]{3,2,1,0:T(8,128)S(1)} collective-permute-done((f32[5,4,8,128]{3,2,1,0:T(8,128)S(1)}, f32[5,4,8,128]{3,2,1,0:T(8,128)S(1)}, u32[]{:S(2)}, u32[]{:S(2)}) %collective-permute-start.1) | collective-permute-done | bytes 81952 | tf_op jit(solution)/shard_map/ppermute | solution.py:48
  14.0 0.1 collective-permute-start.2
  14.1 3.6 %collective-permute-start.3 = (f32[5,8,8,128]{3,2,1,0:T(8,128)S(1)}, f32[5,8,8,128]{3,2,1,0:T(8,128)S(1)}, u32[]{:S(2)}, u32[]{:S(2)}) collective-permute-start(f32[5,8,8,128]{3,2,1,0:T(8,128)S(1)} %get-tuple-element.22), channel_id=1, source_target_pairs={{8,0},{16,8},{24,16},{32,24},{40,32},{48,40},{56,48},{0,56},{9,1},... | collective-permute-start | bytes 491528 | tf_op jit(solution)/shard_map/ppermute | solution.py:35
  17.6 0.9 %collective-permute-done.2.got_below = f32[5,8,8,128]{3,2,1,0:T(8,128)S(1)} collective-permute-done((f32[5,8,8,128]{3,2,1,0:T(8,128)S(1)}, f32[5,8,8,128]{3,2,1,0:T(8,128)S(1)}, u32[]{:S(2)}, u32[]{:S(2)}) %collective-permute-start.2) | collective-permute-done | bytes 163872 | tf_op jit(solution)/shard_map/ppermute | solution.py:34
  18.5 0.3 collective-permute-done.3.got_above
  18.8 0.4 pack_streamwise.1
  19.2 11.0 %collective-permute-start.4 = (f32[5,8,128]{2,1,0:T(8,128)S(1)}, f32[5,8,128]{2,1,0:T(8,128)S(1)}, u32[]{:S(2)}, u32[]{:S(2)}) collective-permute-start(f32[5,8,128]{2,1,0:T(8,128)S(1)} %get-tuple-element.25), channel_id=1, source_target_pairs={{0,64},{8,456},{16,80},{24,472},{32,96},{40,488},{48,112},{56,504}... | collective-permute-start | bytes 61448 | tf_op jit(solution)/shard_map/ppermute | solution.py:61
  30.1 1.9 %collective-permute-start.5 = (f32[5,8,128]{2,1,0:T(8,128)S(1)}, f32[5,8,128]{2,1,0:T(8,128)S(1)}, u32[]{:S(2)}, u32[]{:S(2)}) collective-permute-start(f32[5,8,128]{2,1,0:T(8,128)S(1)} %get-tuple-element.26), channel_id=1, source_target_pairs={{0,448},{8,72},{16,464},{24,88},{32,480},{40,104},{48,496},{56,120... | collective-permute-start | bytes 61448 | tf_op jit(solution)/shard_map/ppermute | solution.py:61
  32.1 1.4 %step_one.1.state_one = f32[10,12,16,128]{3,2,1,0:T(8,128)S(1)} custom-call(f32[5,16,16,128]{3,2,1,0:T(8,128)S(1)} %get-tuple-element.23.window), custom_call_target="tpu_custom_call" | custom-call | tf_op jit(solution)/shard_map/step_one/pallas_call | solution.py:490
  33.5 0.0 collective-permute-done.4.got_one
  33.5 1.4 %collective-permute-done.5.got_two = f32[5,8,128]{2,1,0:T(8,128)S(1)} collective-permute-done((f32[5,8,128]{2,1,0:T(8,128)S(1)}, f32[5,8,128]{2,1,0:T(8,128)S(1)}, u32[]{:S(2)}, u32[]{:S(2)}) %collective-permute-start.5) | collective-permute-done | bytes 20512 | tf_op jit(solution)/shard_map/ppermute | solution.py:61
  35.0 2.5 %step_two.1 = (f32[10,8,8,128]{3,2,1,0:T(8,128)}, f32[8,8,128]{2,1,0:T(8,128)}, f32[64,384]{1,0:T(8,128)S(1)}) custom-call(f32[5,16,16,128]{3,2,1,0:T(8,128)S(1)} %get-tuple-element.23.window, f32[10,12,16,128]{3,2,1,0:T(8,128)S(1)} %step_one.1.state_one, f32[5,2,8,128]{3,2,1,0:T(8,128)S(1)} %get-tuple-element.24.faces, ...), custom_call_target="tpu_custom_call" | custom-call | tf_op jit(solution)/shard_map/step_two/pallas_call | solution.py:493
  37.5 0.1 copy.8
  37.6 19.3 %all_to_all.5 = f32[64,1,384]{2,1,0:T(1,128)S(1)} all-to-all(f32[64,1,384]{2,1,0:T(1,128)S(1)} %copy.8), channel_id=1, replica_groups=mesh['gx'=8,'gy'=8,'gz'=8] {'gy','gz'}, dimensions={0} | all-to-all | bytes 196608 | tf_op jit(solution)/shard_map/all_to_all | solution.py:510
  56.9 0.9 %sum_slots.1 = f32[16,160]{1,0:T(8,128)} custom-call(f32[64,384]{1,0:T(8,128)S(1)} %bitcast.10), custom_call_target="tpu_custom_call" | custom-call | tf_op jit(solution)/shard_map/sum_slots/pallas_call | solution.py:513
  (4 shorter events, 0.1 us)
Async XLA Ops:
  0.6 0.8 %copy-start.3 = (f32[8,8,128]{2,1,0:T(8,128)S(1)}, f32[8,8,128]{2,1,0:T(8,128)}, u32[]{:S(2)}) copy-start(f32[8,8,128]{2,1,0:T(8,128)} %param.5) | copy-start | bytes 98308
  0.6 0.9 %copy-start = (f32[3,8,8,128]{3,2,1,0:T(8,128)S(1)}, f32[3,8,8,128]{3,2,1,0:T(8,128)}, u32[]{:S(2)}) copy-start(f32[3,8,8,128]{3,2,1,0:T(8,128)} %velocity.3) | copy-start | bytes 294916
  1.6 8.7 %collective-permute-start = (f32[5,4,8,128]{3,2,1,0:T(8,128)S(1)}, f32[5,4,8,128]{3,2,1,0:T(8,128)S(1)}, u32[]{:S(2)}, u32[]{:S(2)}) collective-permute-start(f32[5,4,8,128]{3,2,1,0:T(8,128)S(1)} %get-tuple-element.17), channel_id=1, source_target_pairs={{0,1},{1,2},{2,3},{3,4},{4,5},{5,6},{6,7},{7,0},{8,15},{9,8},{10,9... | collective-permute-start | bytes 245768 | tf_op jit(solution)/shard_map/ppermute | solution.py:48
  7.5 6.4 %collective-permute-start.1 = (f32[5,4,8,128]{3,2,1,0:T(8,128)S(1)}, f32[5,4,8,128]{3,2,1,0:T(8,128)S(1)}, u32[]{:S(2)}, u32[]{:S(2)}) collective-permute-start(f32[5,4,8,128]{3,2,1,0:T(8,128)S(1)} %get-tuple-element.18), channel_id=1, source_target_pairs={{0,7},{1,0},{2,1},{3,2},{4,3},{5,4},{6,5},{7,6},{8,9},{9,10},{10,1... | collective-permute-start | bytes 245768 | tf_op jit(solution)/shard_map/ppermute | solution.py:48
  9.4 0.7 %copy-start.1 = (s32[1,1,1,64,1]{3,4,2,1,0:T(1,128)S(1)}, s32[1,1,1,64,1]{3,4,2,1,0:T(1,128)}, u32[]{:S(2)}) copy-start(s32[1,1,1,64,1]{3,4,2,1,0:T(1,128)} %param.8) | copy-start | bytes 772
  9.5 0.7 %copy-start.2 = (s32[1,1,1,64,1]{3,4,2,1,0:T(1,128)S(1)}, s32[1,1,1,64,1]{3,4,2,1,0:T(1,128)}, u32[]{:S(2)}) copy-start(s32[1,1,1,64,1]{3,4,2,1,0:T(1,128)} %param.9) | copy-start | bytes 772
  14.0 4.6 %collective-permute-start.2 = (f32[5,8,8,128]{3,2,1,0:T(8,128)S(1)}, f32[5,8,8,128]{3,2,1,0:T(8,128)S(1)}, u32[]{:S(2)}, u32[]{:S(2)}) collective-permute-start(f32[5,8,8,128]{3,2,1,0:T(8,128)S(1)} %get-tuple-element.21), channel_id=1, source_target_pairs={{0,8},{8,16},{16,24},{24,32},{32,40},{40,48},{48,56},{56,0},{1,9},... | collective-permute-start | bytes 491528 | tf_op jit(solution)/shard_map/ppermute | solution.py:34
  14.1 4.7 %collective-permute-start.3 = (f32[5,8,8,128]{3,2,1,0:T(8,128)S(1)}, f32[5,8,8,128]{3,2,1,0:T(8,128)S(1)}, u32[]{:S(2)}, u32[]{:S(2)}) collective-permute-start(f32[5,8,8,128]{3,2,1,0:T(8,128)S(1)} %get-tuple-element.22), channel_id=1, source_target_pairs={{8,0},{16,8},{24,16},{32,24},{40,32},{48,40},{56,48},{0,56},{9,1},... | collective-permute-start | bytes 491528 | tf_op jit(solution)/shard_map/ppermute | solution.py:35
  19.2 14.3 %collective-permute-start.4 = (f32[5,8,128]{2,1,0:T(8,128)S(1)}, f32[5,8,128]{2,1,0:T(8,128)S(1)}, u32[]{:S(2)}, u32[]{:S(2)}) collective-permute-start(f32[5,8,128]{2,1,0:T(8,128)S(1)} %get-tuple-element.25), channel_id=1, source_target_pairs={{0,64},{8,456},{16,80},{24,472},{32,96},{40,488},{48,112},{56,504}... | collective-permute-start | bytes 61448 | tf_op jit(solution)/shard_map/ppermute | solution.py:61
  30.1 4.8 %collective-permute-start.5 = (f32[5,8,128]{2,1,0:T(8,128)S(1)}, f32[5,8,128]{2,1,0:T(8,128)S(1)}, u32[]{:S(2)}, u32[]{:S(2)}) collective-permute-start(f32[5,8,128]{2,1,0:T(8,128)S(1)} %get-tuple-element.26), channel_id=1, source_target_pairs={{0,448},{8,72},{16,464},{24,88},{32,480},{40,104},{48,496},{56,120... | collective-permute-start | bytes 61448 | tf_op jit(solution)/shard_map/ppermute | solution.py:61

commit v5 on v3

--- a/solution.py
+++ b/solution.py
@@ -6,7 +6,8 @@
 from jax.sharding import PartitionSpec as P
 
 SLOTS = 16
-OWNERS = 64
+SPAN_Y = 8
+SPAN_Z = 8
 WALE_COEFF = 0.5
 BASE_VISCOSITY = 0.01
 WALE_FLOOR = 1e-10
@@ -29,19 +30,19 @@
     return lax.rem(lax.axis_index(axis), 2) == 0
 
 
+def ring(high, low, axis):
+    count = lax.axis_size(axis)
+    below = lax.ppermute(high, axis, [(i, (i + 1) % count) for i in range(count)])
+    above = lax.ppermute(low, axis, [((i + 1) % count, i) for i in range(count)])
+    return below, above
+
+
 def swap(near, far, axis):
     count = lax.axis_size(axis)
     near_pairs = [(i, i ^ 1) for i in range(count)]
     far_pairs = [(i, (i + 1) % count if i % 2 else (i - 1) % count) for i in range(count)]
     far = lax.ppermute(far, axis, far_pairs)
     return lax.ppermute(near, axis, near_pairs), far
-
-
-def ring(high, low, axis):
-    count = lax.axis_size(axis)
-    below = lax.ppermute(high, axis, [(i, (i + 1) % count) for i in range(count)])
-    above = lax.ppermute(low, axis, [((i + 1) % count, i) for i in range(count)])
-    return below, above
 
 
 def pack_vertical(scalars, velocity, near, far):
@@ -55,15 +56,16 @@
         out[4] = fluid
 
 
-def pack_spanwise(scalars, velocity, got_far, got_near, planes, high, low):
-    even_z = is_even("gz")
+def pack_spanwise(scalars, velocity, got_far, got_near, placing, planes, high, low):
+    del placing
+    even = is_even("gz")
     front = lax.broadcasted_iota(jnp.int32, (8, 128), 0) < 4
     fluid = scalars[1]
     for field in range(5):
         inner = scalars[0] if field == 0 else fluid if field == 4 else velocity[field - 1] * fluid
         planes[field, 4:12] = inner
-        planes[field, 12:16] = jnp.where(even_z, got_near[field], got_far[field])
-        planes[field, 0:4] = jnp.where(even_z, got_far[field], got_near[field])
+        planes[field, 12:16] = jnp.where(even, got_near[field], got_far[field])
+        planes[field, 0:4] = jnp.where(even, got_far[field], got_near[field])
         for pair in range(8):
             one = planes[field, 2 * pair]
             two = planes[field, 2 * pair + 1]
@@ -116,7 +118,7 @@
     earlier = (owner_column == owner_row) & (row < block)
     owner = owner_row.astype(jnp.int32)
     rank = jnp.sum(jnp.where(earlier, 1.0, 0.0), axis=0, keepdims=True).astype(jnp.int32)
-    position = rank * OWNERS + owner
+    position = (lax.rem(owner, SPAN_Z) * SPAN_Y + lax.div(owner, SPAN_Z)) * 2 + rank
     rows = lax.broadcasted_iota(jnp.int32, (128, 128), 0)
     placing[...] = (rows == position).astype(jnp.float32)
     tags[...] = jnp.broadcast_to(0.5 * (slot + 1.0), (16, 128))
@@ -276,8 +278,8 @@
 
 
 def step_two(
-    window, state_one, faces, got_far, got_near, placing, tags, moments, relaxation_out, outgoing,
-    state, sums, strip, strip_sums, edge, pooled,
+    window, state_one, faces, got_far, got_near, placing, tags, moments_out, relaxation_out, outgoing,
+    state, sums, strip, strip_sums, edge, pooled, moments, relaxations, left_sems,
 ):
     even_x = is_even("gx")
     lane = lax.broadcasted_iota(jnp.int32, (16, 128), 1)
@@ -383,7 +385,9 @@
         for k, value in enumerate(plane_sums(stay, right, left)):
             sums[k, plane] = value[0:8]
         if 4 <= plane < 12:
-            relaxation_out[plane - 4] = relaxation[0:8]
+            relaxations[plane - 4] = relaxation[0:8]
+    copies = [pltpu.make_async_copy(relaxations, relaxation_out, left_sems.at[4])]
+    copies[0].start()
 
     for pair in range(4):
         total = None
@@ -401,32 +405,36 @@
             total = members if total is None else [one + two for one, two in zip(total, members)]
         for k in range(10):
             pooled[k * 32 + pair * 8 : k * 32 + pair * 8 + 8, :] = total[k]
+        done = pl.ds(2 * pair, 2)
+        copies.append(pltpu.make_async_copy(moments.at[:, done], moments_out.at[:, done], left_sems.at[pair]))
+        copies[-1].start()
 
     blocks = 0.125 * (pooled[pl.ds(0, 160, stride=2), :] + pooled[pl.ds(1, 160, stride=2), :])
-    payload = jnp.concatenate(
-        [blocks, jnp.zeros((32, 128), jnp.float32), tags[...], jnp.zeros((48, 128), jnp.float32)], axis=0
-    )
-    placed = pick(placing[...], payload, ((1,), (1,)))
-    outgoing[:, 0:128] = placed[0:OWNERS, 0:128]
-    outgoing[:, 128:256] = placed[0:OWNERS, 128:256] + roll(placed[OWNERS:, 128:256], 32, 1)
-    outgoing[:, 256:384] = placed[OWNERS:, 0:128]
-
-
-def sum_slots(arrived, coarse):
-    slot = lax.broadcasted_iota(jnp.int32, (OWNERS, 128), 1).astype(jnp.float32)
-    one = (arrived[:, 192:193] == slot + 1.0).astype(jnp.float32)
-    two = (arrived[:, 224:225] == slot + 1.0).astype(jnp.float32)
-    ones = pick(one, arrived[:, 0:256], ((0,), (0,)))[0:SLOTS]
-    twos = pick(two, arrived[:, 128:384], ((0,), (0,)))[0:SLOTS]
-    coarse[:, 0:128] = ones[:, 0:128] + twos[:, 128:256]
-    coarse[:, 128:160] = (ones[:, 128:256] + roll(twos[:, 0:128], -32, 1))[:, 0:32]
-
-
-def call(kernel, outs, name, scratch=(), in_hbm=0, vmem=48):
+    payload = jnp.concatenate([blocks, tags[...]], axis=0)
+    outgoing[...] = pick(placing[...], payload, ((1,), (1,)))
+    for copy in copies:
+        copy.wait()
+
+
+def sum_by_slot(arrived, sums):
+    row = lax.broadcasted_iota(jnp.int32, (128, 128), 0)
+    column = lax.broadcasted_iota(jnp.int32, (128, 128), 1)
+    tag = jnp.broadcast_to(arrived[:, 160:161], (128, 128))
+    chosen = (column // SLOTS == row // 2 % SPAN_Y) & (tag == (column % SLOTS + 1).astype(jnp.float32))
+    sums[...] = pick(chosen.astype(jnp.float32), arrived[:, 0:160], ((0,), (0,)))
+
+
+def call(kernel, outs, name, scratch=(), in_hbm=0, out_spaces=None):
     extra = {"in_specs": [pl.BlockSpec(memory_space=pltpu.HBM)] * in_hbm} if in_hbm else {}
+    if out_spaces:
+        extra["out_specs"] = tuple(pl.BlockSpec(memory_space=space) for space in out_spaces)
     return pl.pallas_call(
-        kernel, out_shape=outs, scratch_shapes=list(scratch), name=name,
-        compiler_params=pltpu.CompilerParams(vmem_limit_bytes=vmem * 1024 * 1024), **extra
+        kernel,
+        out_shape=outs,
+        scratch_shapes=list(scratch),
+        name=name,
+        compiler_params=pltpu.CompilerParams(vmem_limit_bytes=48 * 1024 * 1024),
+        **extra,
     )
 
 
@@ -443,7 +451,7 @@
     near, far = swap(near, far, "gz")
     planes, high, low = call(
         pack_spanwise, (f32(5, 16, 8, 128), f32(5, 8, 8, 128), f32(5, 8, 8, 128)), "pack_spanwise"
-    )(scalars, velocity, far, near)
+    )(scalars, velocity, far, near, placing)
     below, above = ring(high, low, "gy")
     window, faces, near, far = call(
         pack_streamwise,
@@ -456,7 +464,7 @@
     )(window)
     moments, relaxation, outgoing = call(
         step_two,
-        (f32(10, 8, 8, 128), f32(8, 8, 128), f32(OWNERS, 384)),
+        (f32(10, 8, 8, 128), f32(8, 8, 128), f32(128, 176)),
         "step_two",
         (
             pltpu.VMEM((13, 16, 16, 128), jnp.float32),
@@ -465,12 +473,17 @@
             pltpu.VMEM((16, 2, 16, 128), jnp.float32),
             pltpu.VMEM((10, 2, 16, 128), jnp.float32),
             pltpu.VMEM((320, 128), jnp.float32),
+            pltpu.VMEM((10, 8, 8, 128), jnp.float32),
+            pltpu.VMEM((8, 8, 128), jnp.float32),
+            pltpu.SemaphoreType.DMA((5,)),
         ),
+        out_spaces=(pltpu.HBM, pltpu.HBM, pltpu.VMEM),
     )(window, state, faces, far, near, placing, tags)
     arrived = lax.all_to_all(
-        outgoing.reshape(OWNERS, 1, 384), ("gy", "gz"), split_axis=0, concat_axis=0, tiled=True
+        outgoing.reshape(SPAN_Z, 2 * SPAN_Y, 176), "gz", split_axis=0, concat_axis=0, tiled=True
     )
-    coarse = call(sum_slots, f32(SLOTS, 160), "sum_slots")(arrived.reshape(OWNERS, 384))
+    sums = call(sum_by_slot, f32(128, 160), "sum_by_slot")(arrived.reshape(128, 176))
+    coarse = lax.psum_scatter(sums, "gy", scatter_dimension=0, tiled=True)
     return moments, relaxation, coarse.reshape(1, 1, 1, SLOTS, 160)
 
 

time: 57.5 us -> 93.2 us (1.62)
  waiting for transfers between devices: 7.75 us -> 35.4 us
  between operations: 0.75 us -> 14.1 us
  blocking collectives: 17.3 us -> 11.6 us
    reduce_scatter x0 -> x1, waiting for transfers between devices: none -> 27.6 us  [per_device(): coarse = lax.psum_scatter(sums, 'gy', scatter_dimension=0, tiled=True)]
    all_to_all x1, blocking collectives: 17.3 us -> 11.6 us  [per_device(): lax.all_to_all(outgoing.reshape(SPAN_Z, 2 * SPAN_Y, 176), 'gz', split_axi...]
  transfers between devices with their start and end apart: 6 -> 7, of which waited for: 4 -> 5; matrix products, arithmetic and copies ran while one was open for 0% -> 0% of each run, Pallas kernels for 3% -> 2%
where the time goes in v5:
time: 93.2 us; the launch traced here: 92.4 us
  waiting for transfers between devices  35.4 us (38%)
  starting transfers between devices  24.2 us (26%)
  between operations  14.1 us (15%)
  blocking collectives  11.6 us (12%)
  Pallas kernels  5.47 us (6%)
    reduce_scatter x1, waiting for transfers between devices, per_device(): coarse = lax.psum_scatter(sums, 'gy', scatter_dimension=0, tiled=True)  27.6 us
    ppermute x2, starting transfers between devices, swap(): far = lax.ppermute(far, axis, far_pairs)  16.3 us
    all_to_all x1, blocking collectives, per_device(): lax.all_to_all(outgoing.reshape(SPAN_Z, 2 * SPAN_Y, 176), 'gz', split_axi...  11.6 us
    ppermute x2, starting transfers between devices, swap(): return (lax.ppermute(near, axis, near_pairs), far)  3.84 us
    ppermute x2, waiting for transfers between devices, swap(): return (lax.ppermute(near, axis, near_pairs), far)  3.56 us
    ppermute x1, starting transfers between devices, ring(): lax.ppermute(high, axis, [(i, (i + 1) % count) for i in range(count)])  3.21 us
    ppermute x1, waiting for transfers between devices, ring(): lax.ppermute(low, axis, [((i + 1) % count, i) for i in range(count)])  2.77 us
    pallas_call x1, Pallas kernels, per_device(): call(step_two, (f32(10, 8, 8, 128), f32(8, 8, 128), f32(128, 176)), 'step...  2.49 us
  transfers between devices with their start and end apart: 7, of which 5 were waited for; matrix products, arithmetic and copies ran while one was open for 0% of the time, Pallas kernels for 2%

profile of v5, /device:TPU:1, one launch (start us, length us, event | category | flops | bytes accessed | tf_op | source)
XLA Modules:
  0.0 92.4 jit_solution(2378586259501732716)
XLA Ops:
  7.2 0.0 copy-start.3
  7.2 0.0 copy-start
  7.2 0.0 reduce-scatter.2.cloned.1.call-start
  7.2 0.8 subtract_bitcast_fusion
  8.0 0.0 copy-done.3
  8.0 0.1 copy-done
  8.1 5.9 %collective-permute-start = (f32[5,4,8,128]{3,2,1,0:T(8,128)S(1)}, f32[5,4,8,128]{3,2,1,0:T(8,128)S(1)}, u32[]{:S(2)}, u32[]{:S(2)}) collective-permute-start(f32[5,4,8,128]{3,2,1,0:T(8,128)S(1)} %get-tuple-element.17), channel_id=1, source_target_pairs={{0,7},{1,2},{2,1},{3,4},{4,3},{5,6},{6,5},{7,0},{8,15},{9,10},{10,... | collective-permute-start | bytes 245768 | tf_op jit(solution)/shard_map/ppermute | solution.py:44
  14.0 1.9 %collective-permute-start.1 = (f32[5,4,8,128]{3,2,1,0:T(8,128)S(1)}, f32[5,4,8,128]{3,2,1,0:T(8,128)S(1)}, u32[]{:S(2)}, u32[]{:S(2)}) collective-permute-start(f32[5,4,8,128]{3,2,1,0:T(8,128)S(1)} %get-tuple-element.18), channel_id=1, source_target_pairs={{0,1},{1,0},{2,3},{3,2},{4,5},{5,4},{6,7},{7,6},{8,9},{9,8},{10,11... | collective-permute-start | bytes 245768 | tf_op jit(solution)/shard_map/ppermute | solution.py:45
  16.0 0.0 copy-start.1
  16.0 0.0 copy-start.2
  16.0 0.6 copy-done.1
  16.6 0.0 copy-done.2
  16.6 0.1 place_blocks.1
  16.8 0.0 collective-permute-done.got_far
  16.8 2.4 %collective-permute-done.1.got_near = f32[5,4,8,128]{3,2,1,0:T(8,128)S(1)} collective-permute-done((f32[5,4,8,128]{3,2,1,0:T(8,128)S(1)}, f32[5,4,8,128]{3,2,1,0:T(8,128)S(1)}, u32[]{:S(2)}, u32[]{:S(2)}) %collective-permute-start.1) | collective-permute-done | bytes 81952 | tf_op jit(solution)/shard_map/ppermute | solution.py:45
  19.3 3.2 %collective-permute-start.2 = (f32[5,8,8,128]{3,2,1,0:T(8,128)S(1)}, f32[5,8,8,128]{3,2,1,0:T(8,128)S(1)}, u32[]{:S(2)}, u32[]{:S(2)}) collective-permute-start(f32[5,8,8,128]{3,2,1,0:T(8,128)S(1)} %get-tuple-element.21), channel_id=1, source_target_pairs={{0,8},{8,16},{16,24},{24,32},{32,40},{40,48},{48,56},{56,0},{1,9},... | collective-permute-start | bytes 491528 | tf_op jit(solution)/shard_map/ppermute | solution.py:35
  22.5 0.8 collective-permute-start.3
  23.3 1.4 %collective-permute-done.2.got_below = f32[5,8,8,128]{3,2,1,0:T(8,128)S(1)} collective-permute-done((f32[5,8,8,128]{3,2,1,0:T(8,128)S(1)}, f32[5,8,8,128]{3,2,1,0:T(8,128)S(1)}, u32[]{:S(2)}, u32[]{:S(2)}) %collective-permute-start.2) | collective-permute-done | bytes 163872 | tf_op jit(solution)/shard_map/ppermute | solution.py:35
  24.7 2.8 %collective-permute-done.3.got_above = f32[5,8,8,128]{3,2,1,0:T(8,128)S(1)} collective-permute-done((f32[5,8,8,128]{3,2,1,0:T(8,128)S(1)}, f32[5,8,8,128]{3,2,1,0:T(8,128)S(1)}, u32[]{:S(2)}, u32[]{:S(2)}) %collective-permute-start.3) | collective-permute-done | bytes 163872 | tf_op jit(solution)/shard_map/ppermute | solution.py:36
  27.5 0.4 pack_streamwise.1
  27.9 10.4 %collective-permute-start.4 = (f32[5,8,128]{2,1,0:T(8,128)S(1)}, f32[5,8,128]{2,1,0:T(8,128)S(1)}, u32[]{:S(2)}, u32[]{:S(2)}) collective-permute-start(f32[5,8,128]{2,1,0:T(8,128)S(1)} %get-tuple-element.25), channel_id=1, source_target_pairs={{0,448},{64,128},{128,64},{192,256},{256,192},{320,384},{384,320},... | collective-permute-start | bytes 61448 | tf_op jit(solution)/shard_map/ppermute | solution.py:44
  38.3 1.9 %collective-permute-start.5 = (f32[5,8,128]{2,1,0:T(8,128)S(1)}, f32[5,8,128]{2,1,0:T(8,128)S(1)}, u32[]{:S(2)}, u32[]{:S(2)}) collective-permute-start(f32[5,8,128]{2,1,0:T(8,128)S(1)} %get-tuple-element.26), channel_id=1, source_target_pairs={{0,64},{64,0},{128,192},{192,128},{256,320},{320,256},{384,448},{4... | collective-permute-start | bytes 61448 | tf_op jit(solution)/shard_map/ppermute | solution.py:45
  40.2 1.4 %step_one.1.state_one = f32[10,12,16,128]{3,2,1,0:T(8,128)S(1)} custom-call(f32[5,16,16,128]{3,2,1,0:T(8,128)S(1)} %get-tuple-element.23.window), custom_call_target="tpu_custom_call" | custom-call | tf_op jit(solution)/shard_map/step_one/pallas_call | solution.py:462
  41.6 0.0 collective-permute-done.4.got_far
  41.6 1.1 %collective-permute-done.5.got_near = f32[5,8,128]{2,1,0:T(8,128)S(1)} collective-permute-done((f32[5,8,128]{2,1,0:T(8,128)S(1)}, f32[5,8,128]{2,1,0:T(8,128)S(1)}, u32[]{:S(2)}, u32[]{:S(2)}) %collective-permute-start.5) | collective-permute-done | bytes 20512 | tf_op jit(solution)/shard_map/ppermute | solution.py:45
  42.8 2.5 %step_two.1 = (f32[10,8,8,128]{3,2,1,0:T(8,128)}, f32[8,8,128]{2,1,0:T(8,128)}, f32[128,176]{1,0:T(8,128)S(1)}) custom-call(f32[5,16,16,128]{3,2,1,0:T(8,128)S(1)} %get-tuple-element.23.window, f32[10,12,16,128]{3,2,1,0:T(8,128)S(1)} %step_one.1.state_one, f32[5,2,8,128]{3,2,1,0:T(8,128)S(1)} %get-tuple-element.24.faces, ...), custom_call_target="tpu_custom_call" | custom-call | tf_op jit(solution)/shard_map/step_two/pallas_call | solution.py:465
  45.3 11.6 %all_to_all.5 = f32[8,16,176]{2,1,0:T(8,128)S(1)} all-to-all(f32[8,16,176]{2,1,0:T(8,128)S(1)} %bitcast.9), channel_id=1, replica_groups=mesh['gx'=8,'gy'=8,'gz'=8] {'gz'}, dimensions={0} | all-to-all | bytes 180224 | tf_op jit(solution)/shard_map/all_to_all | solution.py:482
  56.9 1.0 %sum_by_slot.1 = f32[128,160]{1,0:T(8,128)} custom-call(f32[128,176]{1,0:T(8,128)S(1)} %bitcast.8), custom_call_target="tpu_custom_call" | custom-call | tf_op jit(solution)/shard_map/sum_by_slot/pallas_call | solution.py:485
  57.9 0.0 reduce-scatter.2.cloned.1.call-update
  57.9 27.6 %reduce-scatter.2.cloned.1.call-done = f32[16,160]{1,0:T(8,128)} async-done(((f32[128,160]{1,0:T(8,128)}), f32[16,160]{1,0:T(8,128)}) %reduce-scatter.2.cloned.1.call-update) | async-done | bytes 10256 | tf_op jit(solution)/shard_map/reduce_scatter | solution.py:486
  (3 shorter events, 0.1 us)
Async XLA Ops:
  7.2 0.8 copy-start.3
  7.2 0.9 copy-start
  7.2 78.3 %reduce-scatter.2.cloned.1.call-start = ((), (), s32[]{:S(2)}) async-start(), calls=%async_computation.2 | async-start | bytes 147456 | tf_op jit(solution)/shard_map/reduce_scatter | solution.py:486
  8.1 8.7 %collective-permute-start = (f32[5,4,8,128]{3,2,1,0:T(8,128)S(1)}, f32[5,4,8,128]{3,2,1,0:T(8,128)S(1)}, u32[]{:S(2)}, u32[]{:S(2)}) collective-permute-start(f32[5,4,8,128]{3,2,1,0:T(8,128)S(1)} %get-tuple-element.17), channel_id=1, source_target_pairs={{0,7},{1,2},{2,1},{3,4},{4,3},{5,6},{6,5},{7,0},{8,15},{9,10},{10,... | collective-permute-start | bytes 245768 | tf_op jit(solution)/shard_map/ppermute | solution.py:44
  14.0 5.2 %collective-permute-start.1 = (f32[5,4,8,128]{3,2,1,0:T(8,128)S(1)}, f32[5,4,8,128]{3,2,1,0:T(8,128)S(1)}, u32[]{:S(2)}, u32[]{:S(2)}) collective-permute-start(f32[5,4,8,128]{3,2,1,0:T(8,128)S(1)} %get-tuple-element.18), channel_id=1, source_target_pairs={{0,1},{1,0},{2,3},{3,2},{4,5},{5,4},{6,7},{7,6},{8,9},{9,8},{10,11... | collective-permute-start | bytes 245768 | tf_op jit(solution)/shard_map/ppermute | solution.py:45
  16.0 0.7 copy-start.1
  16.0 0.7 copy-start.2
  19.3 5.5 %collective-permute-start.2 = (f32[5,8,8,128]{3,2,1,0:T(8,128)S(1)}, f32[5,8,8,128]{3,2,1,0:T(8,128)S(1)}, u32[]{:S(2)}, u32[]{:S(2)}) collective-permute-start(f32[5,8,8,128]{3,2,1,0:T(8,128)S(1)} %get-tuple-element.21), channel_id=1, source_target_pairs={{0,8},{8,16},{16,24},{24,32},{32,40},{40,48},{48,56},{56,0},{1,9},... | collective-permute-start | bytes 491528 | tf_op jit(solution)/shard_map/ppermute | solution.py:35
  22.5 5.0 %collective-permute-start.3 = (f32[5,8,8,128]{3,2,1,0:T(8,128)S(1)}, f32[5,8,8,128]{3,2,1,0:T(8,128)S(1)}, u32[]{:S(2)}, u32[]{:S(2)}) collective-permute-start(f32[5,8,8,128]{3,2,1,0:T(8,128)S(1)} %get-tuple-element.22), channel_id=1, source_target_pairs={{8,0},{16,8},{24,16},{32,24},{40,32},{48,40},{56,48},{0,56},{9,1},... | collective-permute-start | bytes 491528 | tf_op jit(solution)/shard_map/ppermute | solution.py:36
  27.9 13.8 %collective-permute-start.4 = (f32[5,8,128]{2,1,0:T(8,128)S(1)}, f32[5,8,128]{2,1,0:T(8,128)S(1)}, u32[]{:S(2)}, u32[]{:S(2)}) collective-permute-start(f32[5,8,128]{2,1,0:T(8,128)S(1)} %get-tuple-element.25), channel_id=1, source_target_pairs={{0,448},{64,128},{128,64},{192,256},{256,192},{320,384},{384,320},... | collective-permute-start | bytes 61448 | tf_op jit(solution)/shard_map/ppermute | solution.py:44
  38.3 4.5 %collective-permute-start.5 = (f32[5,8,128]{2,1,0:T(8,128)S(1)}, f32[5,8,128]{2,1,0:T(8,128)S(1)}, u32[]{:S(2)}, u32[]{:S(2)}) collective-permute-start(f32[5,8,128]{2,1,0:T(8,128)S(1)} %get-tuple-element.26), channel_id=1, source_target_pairs={{0,64},{64,0},{128,192},{192,128},{256,320},{320,256},{384,448},{4... | collective-permute-start | bytes 61448 | tf_op jit(solution)/shard_map/ppermute | solution.py:45
Sparse Core Ops, SparseCore 0:
  58.0 27.4 reduce-scatter.1

commit v6 on v5

--- a/solution.py
+++ b/solution.py
@@ -6,8 +6,7 @@
 from jax.sharding import PartitionSpec as P
 
 SLOTS = 16
-SPAN_Y = 8
-SPAN_Z = 8
+OWNERS = 64
 WALE_COEFF = 0.5
 BASE_VISCOSITY = 0.01
 WALE_FLOOR = 1e-10
@@ -48,48 +47,98 @@
 def pack_vertical(scalars, velocity, near, far):
     even = is_even("gz")
     for out, upper in ((near, even), (far, jnp.logical_not(even))):
-        planes = pl.ds(jnp.where(upper, 4, 0), 4)
-        fluid = scalars[1, planes]
-        out[0] = scalars[0, planes]
+
+        def face(depth):
+            return pl.ds(jnp.where(upper, 8 - depth, 0), depth)
+
         for axis in range(3):
-            out[1 + axis] = velocity[axis, planes] * fluid
-        out[4] = fluid
+            out[4 * axis : 4 * axis + 4] = velocity[axis, face(4)] * scalars[1, face(4)]
+        out[12:15] = scalars[0, face(3)]
+        out[15:17] = scalars[1, face(2)]
 
 
 def pack_spanwise(scalars, velocity, got_far, got_near, placing, planes, high, low):
     del placing
     even = is_even("gz")
-    front = lax.broadcasted_iota(jnp.int32, (8, 128), 0) < 4
+    row = lax.broadcasted_iota(jnp.int32, (8, 128), 0)
+    front = row < 4
+
+    def got_above(first, last):
+        return jnp.where(even, got_near[first:last], got_far[first:last])
+
+    def got_below(first, last):
+        return jnp.where(even, got_far[first:last], got_near[first:last])
+
     fluid = scalars[1]
-    for field in range(5):
-        inner = scalars[0] if field == 0 else fluid if field == 4 else velocity[field - 1] * fluid
-        planes[field, 4:12] = inner
-        planes[field, 12:16] = jnp.where(even, got_near[field], got_far[field])
-        planes[field, 0:4] = jnp.where(even, got_far[field], got_near[field])
+    planes[0, 4:12] = scalars[0]
+    planes[0, 12:15] = got_above(12, 15)
+    planes[0, 1:4] = got_below(12, 15)
+    planes[0, 15] = jnp.ones((8, 128), jnp.float32)
+    planes[0, 0] = jnp.ones((8, 128), jnp.float32)
+    for axis in range(3):
+        planes[1 + axis, 4:12] = velocity[axis] * fluid
+        planes[1 + axis, 12:16] = got_above(4 * axis, 4 * axis + 4)
+        planes[1 + axis, 0:4] = got_below(4 * axis, 4 * axis + 4)
+    planes[4, 4:12] = fluid
+    planes[4, 12:14] = got_above(15, 17)
+    planes[4, 2:4] = got_below(15, 17)
+    planes[4, 14:16] = jnp.zeros((2, 8, 128), jnp.float32)
+    planes[4, 0:2] = jnp.zeros((2, 8, 128), jnp.float32)
+
+    def pack(place, field, one, two):
+        one, two = planes[field, one], planes[field, two]
+        high[place] = jnp.where(front, roll(one, 4, 0), two)
+        low[place] = jnp.where(front, one, roll(two, 4, 0))
+
+    for axis in range(3):
         for pair in range(8):
-            one = planes[field, 2 * pair]
-            two = planes[field, 2 * pair + 1]
-            high[field, pair] = jnp.where(front, roll(one, 4, 0), two)
-            low[field, pair] = jnp.where(front, one, roll(two, 4, 0))
+            pack(8 * axis + pair, 1 + axis, 2 * pair, 2 * pair + 1)
+    for pair in range(7):
+        pack(24 + pair, 0, 2 * pair + 1, 2 * pair + 2)
+    for place in range(3):
+        upper, lower = None, None
+        for part in range(4):
+            cells = planes[4, 2 + 4 * place + part]
+            moved_high, moved_low = roll(cells, 2 * part + 2, 0), roll(cells, 2 * part, 0)
+            upper = moved_high if part == 0 else jnp.where(row // 2 == part, moved_high, upper)
+            lower = moved_low if part == 0 else jnp.where(row // 2 == part, moved_low, lower)
+        high[31 + place] = upper
+        low[31 + place] = lower
 
 
 def pack_streamwise(planes, got_below, got_above, window, faces, near, far):
     even_x = is_even("gx")
-    front = lax.broadcasted_iota(jnp.int32, (8, 128), 0) < 4
+    row = lax.broadcasted_iota(jnp.int32, (8, 128), 0)
+    front = row < 4
     lane = lax.broadcasted_iota(jnp.int32, (8, 128), 1)
+
+    def outer_rows(field, plane):
+        if field == 4:
+            if not 2 <= plane < 14:
+                return jnp.zeros((8, 128), jnp.float32)
+            place, part = 31 + (plane - 2) // 4, (plane - 2) % 4
+            below = jnp.where(row >= 6, roll(got_below[place], 6 - 2 * part, 0), 0.0)
+            return jnp.where(row < 2, roll(got_above[place], -2 * part, 0), below)
+        if field == 0:
+            if not 1 <= plane < 15:
+                return jnp.ones((8, 128), jnp.float32)
+            place, second = 24 + (plane - 1) // 2, (plane - 1) % 2
+        else:
+            place, second = 8 * (field - 1) + plane // 2, plane % 2
+        above, below = got_above[place], got_below[place]
+        if second:
+            return jnp.where(front, roll(above, 4, 0), below)
+        return jnp.where(front, above, roll(below, 4, 0))
+
     for field in range(5):
         own = [jnp.zeros((8, 128), jnp.float32) for _ in range(2)]
-        for pair in range(8):
-            above, below = got_above[field, pair], got_below[field, pair]
-            outer = (jnp.where(front, above, roll(below, 4, 0)), jnp.where(front, roll(above, 4, 0), below))
-            for side in range(2):
-                plane = 2 * pair + side
-                inner = planes[field, plane]
-                window[field, plane, 0:8] = inner
-                window[field, plane, 8:16] = outer[side]
-                here = lane // 8 == plane
-                own[0] = jnp.where(here, roll(inner, 8 * plane + 4, 1), own[0])
-                own[1] = jnp.where(here, roll(outer[side], 8 * plane + 4, 1), own[1])
+        for plane in range(16):
+            inner, outer = planes[field, plane], outer_rows(field, plane)
+            window[field, plane, 0:8] = inner
+            window[field, plane, 8:16] = outer
+            here = lane // 8 == plane
+            own[0] = jnp.where(here, roll(inner, 8 * plane + 4, 1), own[0])
+            own[1] = jnp.where(here, roll(outer, 8 * plane + 4, 1), own[1])
         faces[field, 0] = own[0]
         faces[field, 1] = own[1]
         even_spot = lane % 8 < 4
@@ -118,7 +167,7 @@
     earlier = (owner_column == owner_row) & (row < block)
     owner = owner_row.astype(jnp.int32)
     rank = jnp.sum(jnp.where(earlier, 1.0, 0.0), axis=0, keepdims=True).astype(jnp.int32)
-    position = (lax.rem(owner, SPAN_Z) * SPAN_Y + lax.div(owner, SPAN_Z)) * 2 + rank
+    position = rank * OWNERS + owner
     rows = lax.broadcasted_iota(jnp.int32, (128, 128), 0)
     placing[...] = (rows == position).astype(jnp.float32)
     tags[...] = jnp.broadcast_to(0.5 * (slot + 1.0), (16, 128))
@@ -410,18 +459,30 @@
         copies[-1].start()
 
     blocks = 0.125 * (pooled[pl.ds(0, 160, stride=2), :] + pooled[pl.ds(1, 160, stride=2), :])
-    payload = jnp.concatenate([blocks, tags[...]], axis=0)
-    outgoing[...] = pick(placing[...], payload, ((1,), (1,)))
+    payload = jnp.concatenate(
+        [blocks, jnp.zeros((32, 128), jnp.float32), tags[...], jnp.zeros((48, 128), jnp.float32)], axis=0
+    )
+    placed = pick(placing[...], payload, ((1,), (1,)))
+    outgoing[:, 0:128] = placed[0:OWNERS, 0:128]
+    outgoing[:, 128:256] = placed[0:OWNERS, 128:256] + roll(placed[OWNERS:, 128:256], 32, 1)
+    outgoing[:, 256:384] = placed[OWNERS:, 0:128]
     for copy in copies:
         copy.wait()
 
 
-def sum_by_slot(arrived, sums):
-    row = lax.broadcasted_iota(jnp.int32, (128, 128), 0)
-    column = lax.broadcasted_iota(jnp.int32, (128, 128), 1)
-    tag = jnp.broadcast_to(arrived[:, 160:161], (128, 128))
-    chosen = (column // SLOTS == row // 2 % SPAN_Y) & (tag == (column % SLOTS + 1).astype(jnp.float32))
-    sums[...] = pick(chosen.astype(jnp.float32), arrived[:, 0:160], ((0,), (0,)))
+def sum_slots(arrived, coarse):
+    slot = lax.broadcasted_iota(jnp.int32, (2 * OWNERS, SLOTS), 1).astype(jnp.float32)
+    shared = arrived[:, 128:256]
+    tag = jnp.concatenate([shared[:, 64:65], shared[:, 96:97]], axis=0)
+    blocks = jnp.concatenate(
+        [
+            jnp.concatenate([arrived[:, 0:128], arrived[:, 256:384]], axis=0),
+            jnp.concatenate([shared, roll(shared, -32, 1)], axis=0),
+        ],
+        axis=1,
+    )
+    total = pick((tag == slot + 1.0).astype(jnp.float32), blocks, ((0,), (0,)))
+    coarse[...] = total[:, 0:160]
 
 
 def call(kernel, outs, name, scratch=(), in_hbm=0, out_spaces=None):
@@ -447,10 +508,10 @@
         2,
     )(owner_map.reshape(1, 64), slot_map.reshape(1, 64))
     scalars = jnp.concatenate([density[None], 1.0 - solid[None].astype(jnp.float32)])
-    near, far = call(pack_vertical, (f32(5, 4, 8, 128),) * 2, "pack_vertical")(scalars, velocity)
+    near, far = call(pack_vertical, (f32(17, 8, 128),) * 2, "pack_vertical")(scalars, velocity)
     near, far = swap(near, far, "gz")
     planes, high, low = call(
-        pack_spanwise, (f32(5, 16, 8, 128), f32(5, 8, 8, 128), f32(5, 8, 8, 128)), "pack_spanwise"
+        pack_spanwise, (f32(5, 16, 8, 128), f32(34, 8, 128), f32(34, 8, 128)), "pack_spanwise"
     )(scalars, velocity, far, near, placing)
     below, above = ring(high, low, "gy")
     window, faces, near, far = call(
@@ -464,7 +525,7 @@
     )(window)
     moments, relaxation, outgoing = call(
         step_two,
-        (f32(10, 8, 8, 128), f32(8, 8, 128), f32(128, 176)),
+        (f32(10, 8, 8, 128), f32(8, 8, 128), f32(OWNERS, 384)),
         "step_two",
         (
             pltpu.VMEM((13, 16, 16, 128), jnp.float32),
@@ -480,10 +541,9 @@
         out_spaces=(pltpu.HBM, pltpu.HBM, pltpu.VMEM),
     )(window, state, faces, far, near, placing, tags)
     arrived = lax.all_to_all(
-        outgoing.reshape(SPAN_Z, 2 * SPAN_Y, 176), "gz", split_axis=0, concat_axis=0, tiled=True
+        outgoing.reshape(OWNERS, 1, 384), ("gy", "gz"), split_axis=0, concat_axis=0, tiled=True
     )
-    sums = call(sum_by_slot, f32(128, 160), "sum_by_slot")(arrived.reshape(128, 176))
-    coarse = lax.psum_scatter(sums, "gy", scatter_dimension=0, tiled=True)
+    coarse = call(sum_slots, f32(SLOTS, 160), "sum_slots")(arrived.reshape(OWNERS, 384))
     return moments, relaxation, coarse.reshape(1, 1, 1, SLOTS, 160)
 
 

time: 93.2 us -> 57 us (0.61)
  waiting for transfers between devices: 35.4 us -> 7.36 us
  between operations: 14.1 us -> 0.76 us
  blocking collectives: 11.6 us -> 17.3 us
    reduce_scatter x1 -> x0, waiting for transfers between devices: 27.6 us -> none  [per_device(): coarse = lax.psum_scatter(sums, 'gy', scatter_dimension=0, tiled=True)]
    all_to_all x1, blocking collectives: 11.6 us -> 17.3 us  [per_device(): lax.all_to_all(outgoing.reshape(OWNERS, 1, 384), ('gy', 'gz'), split_axis...]
  transfers between devices with their start and end apart: 7 -> 6, of which waited for: 5 -> 4; matrix products, arithmetic and copies ran while one was open for 0% -> 0% of each run, Pallas kernels for 2% -> 3%
where the time goes in v6:
time: 57 us; the launch traced here: 56.7 us
  starting transfers between devices  24.2 us (42%)
  blocking collectives  17.3 us (30%)
  waiting for transfers between devices  7.36 us (13%)
  Pallas kernels  5.44 us (10%)
  local copies, waits for them, and re-layouts  0.87 us (2%)
  other arithmetic  0.8 us (1%)
  between operations  0.76 us (1%)
    all_to_all x1, blocking collectives, per_device(): lax.all_to_all(outgoing.reshape(OWNERS, 1, 384), ('gy', 'gz'), split_axis...  17.3 us
    ppermute x2, starting transfers between devices, swap(): far = lax.ppermute(far, axis, far_pairs)  16.3 us
    ppermute x2, starting transfers between devices, swap(): return (lax.ppermute(near, axis, near_pairs), far)  3.84 us
    ppermute x2, waiting for transfers between devices, swap(): return (lax.ppermute(near, axis, near_pairs), far)  3.42 us
    ppermute x1, starting transfers between devices, ring(): lax.ppermute(high, axis, [(i, (i + 1) % count) for i in range(count)])  3.21 us
    ppermute x1, waiting for transfers between devices, ring(): lax.ppermute(low, axis, [((i + 1) % count, i) for i in range(count)])  2.75 us
    pallas_call x1, Pallas kernels, per_device(): call(step_two, (f32(10, 8, 8, 128), f32(8, 8, 128), f32(OWNERS, 384)), 's...  2.51 us
    pallas_call x1, Pallas kernels, per_device(): call(step_one, f32(10, 12, 16, 128), 'step_one', (pltpu.VMEM((16, 16, 16,...  1.44 us
  transfers between devices with their start and end apart: 6, of which 4 were waited for; matrix products, arithmetic and copies ran while one was open for 0% of the time, Pallas kernels for 3%

profile of v6, /device:TPU:1, one launch (start us, length us, event | category | flops | bytes accessed | tf_op | source)
XLA Modules:
  0.0 56.7 jit_solution(6705081263509915394)
XLA Ops:
  0.6 0.0 copy-start.3
  0.6 0.0 copy-start
  0.7 0.8 %subtract_bitcast_fusion = f32[1,8,8,128]{3,2,1,0:T(8,128)S(1)} fusion(s32[8,8,128]{2,1,0:T(8,128)} %param.7), kind=kLoop, calls=%fused_computation.2 | loop fusion | flops 16384 | bytes 65536 | tf_op jit(solution)/shard_map/sub | solution.py:510
  1.4 0.0 copy-done.3
  1.5 0.1 copy-done
  1.6 5.9 %collective-permute-start = (f32[17,8,128]{2,1,0:T(8,128)S(1)}, f32[17,8,128]{2,1,0:T(8,128)S(1)}, u32[]{:S(2)}, u32[]{:S(2)}) collective-permute-start(f32[17,8,128]{2,1,0:T(8,128)S(1)} %get-tuple-element.17), channel_id=1, source_target_pairs={{0,7},{1,2},{2,1},{3,4},{4,3},{5,6},{6,5},{7,0},{8,15},{9,10},{10,... | collective-permute-start | bytes 208904 | tf_op jit(solution)/shard_map/ppermute | solution.py:43
  7.5 1.9 %collective-permute-start.1 = (f32[17,8,128]{2,1,0:T(8,128)S(1)}, f32[17,8,128]{2,1,0:T(8,128)S(1)}, u32[]{:S(2)}, u32[]{:S(2)}) collective-permute-start(f32[17,8,128]{2,1,0:T(8,128)S(1)} %get-tuple-element.18), channel_id=1, source_target_pairs={{0,1},{1,0},{2,3},{3,2},{4,5},{5,4},{6,7},{7,6},{8,9},{9,8},{10,11... | collective-permute-start | bytes 208904 | tf_op jit(solution)/shard_map/ppermute | solution.py:44
  9.4 0.0 copy-start.1
  9.4 0.0 copy-start.2
  9.5 0.6 %copy-done.1 = s32[1,1,1,64,1]{3,4,2,1,0:T(1,128)S(1)} copy-done((s32[1,1,1,64,1]{3,4,2,1,0:T(1,128)S(1)}, s32[1,1,1,64,1]{3,4,2,1,0:T(1,128)}, u32[]{:S(2)}) %copy-start.1) | copy-done | bytes 280
  10.1 0.0 copy-done.2
  10.1 0.1 place_blocks.1
  10.3 0.0 collective-permute-done.got_far
  10.3 2.3 %collective-permute-done.1.got_near = f32[17,8,128]{2,1,0:T(8,128)S(1)} collective-permute-done((f32[17,8,128]{2,1,0:T(8,128)S(1)}, f32[17,8,128]{2,1,0:T(8,128)S(1)}, u32[]{:S(2)}, u32[]{:S(2)}) %collective-permute-start.1) | collective-permute-done | bytes 69664 | tf_op jit(solution)/shard_map/ppermute | solution.py:44
  12.6 3.2 %collective-permute-start.2 = (f32[34,8,128]{2,1,0:T(8,128)S(1)}, f32[34,8,128]{2,1,0:T(8,128)S(1)}, u32[]{:S(2)}, u32[]{:S(2)}) collective-permute-start(f32[34,8,128]{2,1,0:T(8,128)S(1)} %get-tuple-element.21), channel_id=1, source_target_pairs={{0,8},{8,16},{16,24},{24,32},{32,40},{40,48},{48,56},{56,0},{1,9},... | collective-permute-start | bytes 417800 | tf_op jit(solution)/shard_map/ppermute | solution.py:34
  15.8 0.8 %collective-permute-start.3 = (f32[34,8,128]{2,1,0:T(8,128)S(1)}, f32[34,8,128]{2,1,0:T(8,128)S(1)}, u32[]{:S(2)}, u32[]{:S(2)}) collective-permute-start(f32[34,8,128]{2,1,0:T(8,128)S(1)} %get-tuple-element.22), channel_id=1, source_target_pairs={{8,0},{16,8},{24,16},{32,24},{40,32},{48,40},{56,48},{0,56},{9,1},... | collective-permute-start | bytes 417800 | tf_op jit(solution)/shard_map/ppermute | solution.py:35
  16.7 1.2 %collective-permute-done.2.got_below = f32[34,8,128]{2,1,0:T(8,128)S(1)} collective-permute-done((f32[34,8,128]{2,1,0:T(8,128)S(1)}, f32[34,8,128]{2,1,0:T(8,128)S(1)}, u32[]{:S(2)}, u32[]{:S(2)}) %collective-permute-start.2) | collective-permute-done | bytes 139296 | tf_op jit(solution)/shard_map/ppermute | solution.py:34
  17.8 2.8 %collective-permute-done.3.got_above = f32[34,8,128]{2,1,0:T(8,128)S(1)} collective-permute-done((f32[34,8,128]{2,1,0:T(8,128)S(1)}, f32[34,8,128]{2,1,0:T(8,128)S(1)}, u32[]{:S(2)}, u32[]{:S(2)}) %collective-permute-start.3) | collective-permute-done | bytes 139296 | tf_op jit(solution)/shard_map/ppermute | solution.py:35
  20.6 0.4 pack_streamwise.1
  21.0 10.4 %collective-permute-start.4 = (f32[5,8,128]{2,1,0:T(8,128)S(1)}, f32[5,8,128]{2,1,0:T(8,128)S(1)}, u32[]{:S(2)}, u32[]{:S(2)}) collective-permute-start(f32[5,8,128]{2,1,0:T(8,128)S(1)} %get-tuple-element.25), channel_id=1, source_target_pairs={{0,448},{64,128},{128,64},{192,256},{256,192},{320,384},{384,320},... | collective-permute-start | bytes 61448 | tf_op jit(solution)/shard_map/ppermute | solution.py:43
  31.3 1.9 %collective-permute-start.5 = (f32[5,8,128]{2,1,0:T(8,128)S(1)}, f32[5,8,128]{2,1,0:T(8,128)S(1)}, u32[]{:S(2)}, u32[]{:S(2)}) collective-permute-start(f32[5,8,128]{2,1,0:T(8,128)S(1)} %get-tuple-element.26), channel_id=1, source_target_pairs={{0,64},{64,0},{128,192},{192,128},{256,320},{320,256},{384,448},{4... | collective-permute-start | bytes 61448 | tf_op jit(solution)/shard_map/ppermute | solution.py:44
  33.3 1.4 %step_one.1.state_one = f32[10,12,16,128]{3,2,1,0:T(8,128)S(1)} custom-call(f32[5,16,16,128]{3,2,1,0:T(8,128)S(1)} %get-tuple-element.23.window), custom_call_target="tpu_custom_call" | custom-call | tf_op jit(solution)/shard_map/step_one/pallas_call | solution.py:523
  34.7 0.0 collective-permute-done.4.got_far
  34.7 1.1 %collective-permute-done.5.got_near = f32[5,8,128]{2,1,0:T(8,128)S(1)} collective-permute-done((f32[5,8,128]{2,1,0:T(8,128)S(1)}, f32[5,8,128]{2,1,0:T(8,128)S(1)}, u32[]{:S(2)}, u32[]{:S(2)}) %collective-permute-start.5) | collective-permute-done | bytes 20512 | tf_op jit(solution)/shard_map/ppermute | solution.py:44
  35.9 2.5 %step_two.1 = (f32[10,8,8,128]{3,2,1,0:T(8,128)}, f32[8,8,128]{2,1,0:T(8,128)}, f32[64,384]{1,0:T(8,128)S(1)}) custom-call(f32[5,16,16,128]{3,2,1,0:T(8,128)S(1)} %get-tuple-element.23.window, f32[10,12,16,128]{3,2,1,0:T(8,128)S(1)} %step_one.1.state_one, f32[5,2,8,128]{3,2,1,0:T(8,128)S(1)} %get-tuple-element.24.faces, ...), custom_call_target="tpu_custom_call" | custom-call | tf_op jit(solution)/shard_map/step_two/pallas_call | solution.py:526
  38.4 0.1 copy.8
  38.5 17.3 %all_to_all.5 = f32[64,1,384]{2,1,0:T(1,128)S(1)} all-to-all(f32[64,1,384]{2,1,0:T(1,128)S(1)} %copy.8), channel_id=1, replica_groups=mesh['gx'=8,'gy'=8,'gz'=8] {'gy','gz'}, dimensions={0} | all-to-all | bytes 196608 | tf_op jit(solution)/shard_map/all_to_all | solution.py:543
  55.8 0.9 %sum_slots.1 = f32[16,160]{1,0:T(8,128)} custom-call(f32[64,384]{1,0:T(8,128)S(1)} %bitcast.10), custom_call_target="tpu_custom_call" | custom-call | tf_op jit(solution)/shard_map/sum_slots/pallas_call | solution.py:546
  (4 shorter events, 0.1 us)
Async XLA Ops:
  0.6 0.8 %copy-start.3 = (f32[8,8,128]{2,1,0:T(8,128)S(1)}, f32[8,8,128]{2,1,0:T(8,128)}, u32[]{:S(2)}) copy-start(f32[8,8,128]{2,1,0:T(8,128)} %param.5) | copy-start | bytes 98308
  0.6 0.9 %copy-start = (f32[3,8,8,128]{3,2,1,0:T(8,128)S(1)}, f32[3,8,8,128]{3,2,1,0:T(8,128)}, u32[]{:S(2)}) copy-start(f32[3,8,8,128]{3,2,1,0:T(8,128)} %velocity.3) | copy-start | bytes 294916
  1.6 8.7 %collective-permute-start = (f32[17,8,128]{2,1,0:T(8,128)S(1)}, f32[17,8,128]{2,1,0:T(8,128)S(1)}, u32[]{:S(2)}, u32[]{:S(2)}) collective-permute-start(f32[17,8,128]{2,1,0:T(8,128)S(1)} %get-tuple-element.17), channel_id=1, source_target_pairs={{0,7},{1,2},{2,1},{3,4},{4,3},{5,6},{6,5},{7,0},{8,15},{9,10},{10,... | collective-permute-start | bytes 208904 | tf_op jit(solution)/shard_map/ppermute | solution.py:43
  7.5 5.1 %collective-permute-start.1 = (f32[17,8,128]{2,1,0:T(8,128)S(1)}, f32[17,8,128]{2,1,0:T(8,128)S(1)}, u32[]{:S(2)}, u32[]{:S(2)}) collective-permute-start(f32[17,8,128]{2,1,0:T(8,128)S(1)} %get-tuple-element.18), channel_id=1, source_target_pairs={{0,1},{1,0},{2,3},{3,2},{4,5},{5,4},{6,7},{7,6},{8,9},{9,8},{10,11... | collective-permute-start | bytes 208904 | tf_op jit(solution)/shard_map/ppermute | solution.py:44
  9.4 0.7 %copy-start.1 = (s32[1,1,1,64,1]{3,4,2,1,0:T(1,128)S(1)}, s32[1,1,1,64,1]{3,4,2,1,0:T(1,128)}, u32[]{:S(2)}) copy-start(s32[1,1,1,64,1]{3,4,2,1,0:T(1,128)} %param.8) | copy-start | bytes 772
  9.4 0.7 %copy-start.2 = (s32[1,1,1,64,1]{3,4,2,1,0:T(1,128)S(1)}, s32[1,1,1,64,1]{3,4,2,1,0:T(1,128)}, u32[]{:S(2)}) copy-start(s32[1,1,1,64,1]{3,4,2,1,0:T(1,128)} %param.9) | copy-start | bytes 772
  12.6 5.2 %collective-permute-start.2 = (f32[34,8,128]{2,1,0:T(8,128)S(1)}, f32[34,8,128]{2,1,0:T(8,128)S(1)}, u32[]{:S(2)}, u32[]{:S(2)}) collective-permute-start(f32[34,8,128]{2,1,0:T(8,128)S(1)} %get-tuple-element.21), channel_id=1, source_target_pairs={{0,8},{8,16},{16,24},{24,32},{32,40},{40,48},{48,56},{56,0},{1,9},... | collective-permute-start | bytes 417800 | tf_op jit(solution)/shard_map/ppermute | solution.py:34
  15.8 4.8 %collective-permute-start.3 = (f32[34,8,128]{2,1,0:T(8,128)S(1)}, f32[34,8,128]{2,1,0:T(8,128)S(1)}, u32[]{:S(2)}, u32[]{:S(2)}) collective-permute-start(f32[34,8,128]{2,1,0:T(8,128)S(1)} %get-tuple-element.22), channel_id=1, source_target_pairs={{8,0},{16,8},{24,16},{32,24},{40,32},{48,40},{56,48},{0,56},{9,1},... | collective-permute-start | bytes 417800 | tf_op jit(solution)/shard_map/ppermute | solution.py:35
  21.0 13.8 %collective-permute-start.4 = (f32[5,8,128]{2,1,0:T(8,128)S(1)}, f32[5,8,128]{2,1,0:T(8,128)S(1)}, u32[]{:S(2)}, u32[]{:S(2)}) collective-permute-start(f32[5,8,128]{2,1,0:T(8,128)S(1)} %get-tuple-element.25), channel_id=1, source_target_pairs={{0,448},{64,128},{128,64},{192,256},{256,192},{320,384},{384,320},... | collective-permute-start | bytes 61448 | tf_op jit(solution)/shard_map/ppermute | solution.py:43
  31.3 4.5 %collective-permute-start.5 = (f32[5,8,128]{2,1,0:T(8,128)S(1)}, f32[5,8,128]{2,1,0:T(8,128)S(1)}, u32[]{:S(2)}, u32[]{:S(2)}) collective-permute-start(f32[5,8,128]{2,1,0:T(8,128)S(1)} %get-tuple-element.26), channel_id=1, source_target_pairs={{0,64},{64,0},{128,192},{192,128},{256,320},{320,256},{384,448},{4... | collective-permute-start | bytes 61448 | tf_op jit(solution)/shard_map/ppermute | solution.py:44

commit v7 on v6

--- a/solution.py
+++ b/solution.py
@@ -106,8 +106,7 @@
         low[31 + place] = lower
 
 
-def pack_streamwise(planes, got_below, got_above, window, faces, near, far):
-    even_x = is_even("gx")
+def pack_streamwise(planes, got_below, got_above, window, faces, right, left):
     row = lax.broadcasted_iota(jnp.int32, (8, 128), 0)
     front = row < 4
     lane = lax.broadcasted_iota(jnp.int32, (8, 128), 1)
@@ -142,10 +141,8 @@
         faces[field, 0] = own[0]
         faces[field, 1] = own[1]
         even_spot = lane % 8 < 4
-        to_right = jnp.where(even_spot, own[0], roll(own[1], 4, 1))
-        to_left = jnp.where(even_spot, roll(own[0], -4, 1), own[1])
-        near[field] = jnp.where(even_x, to_right, to_left)
-        far[field] = jnp.where(even_x, to_left, to_right)
+        right[field] = jnp.where(even_spot, own[0], roll(own[1], 4, 1))
+        left[field] = jnp.where(even_spot, roll(own[0], -4, 1), own[1])
 
 
 def place_blocks(owners_in, slots_in, placing, tags, owners, slots, arrived):
@@ -327,26 +324,24 @@
 
 
 def step_two(
-    window, state_one, faces, got_far, got_near, placing, tags, moments_out, relaxation_out, outgoing,
+    window, state_one, faces, from_left, from_right, placing, tags, moments_out, relaxation_out, outgoing,
     state, sums, strip, strip_sums, edge, pooled, moments, relaxations, left_sems,
 ):
-    even_x = is_even("gx")
     lane = lax.broadcasted_iota(jnp.int32, (16, 128), 1)
     first_lane, last_lane = lane == 0, lane == 127
     first_two, last_two = lane < 2, lane >= 126
     quarter = lax.broadcasted_iota(jnp.int32, (8, 128), 1) % 16 // 4
 
     for field in range(5):
-        from_right = jnp.where(even_x, got_near[field], got_far[field])
-        from_left = jnp.where(even_x, got_far[field], got_near[field])
+        got_right, got_left = from_right[field], from_left[field]
         for half in range(2):
             for part in range(2):
                 own = faces[field, part]
                 turn = 8 * half + 4 * part
                 cells = jnp.where(quarter == 0, roll(own, -8 * half, 1), roll(own, 8 - 8 * half, 1))
-                cells = jnp.where(quarter == 1, roll(from_right, 4 - turn, 1), cells)
+                cells = jnp.where(quarter == 1, roll(got_right, 4 - turn, 1), cells)
                 strip[field, half, 8 * part : 8 * part + 8] = jnp.where(
-                    quarter == 2, roll(from_left, 8 - turn, 1), cells
+                    quarter == 2, roll(got_left, 8 - turn, 1), cells
                 )
 
     def strip_above(ref, number, half):
@@ -514,12 +509,12 @@
         pack_spanwise, (f32(5, 16, 8, 128), f32(34, 8, 128), f32(34, 8, 128)), "pack_spanwise"
     )(scalars, velocity, far, near, placing)
     below, above = ring(high, low, "gy")
-    window, faces, near, far = call(
+    window, faces, right, left = call(
         pack_streamwise,
         (f32(5, 16, 16, 128), f32(5, 2, 8, 128), f32(5, 8, 128), f32(5, 8, 128)),
         "pack_streamwise",
     )(planes, below, above)
-    near, far = swap(near, far, "gx")
+    left, right = ring(right, left, "gx")
     state = call(
         step_one, f32(10, 12, 16, 128), "step_one", (pltpu.VMEM((16, 16, 16, 128), jnp.float32),)
     )(window)
@@ -539,7 +534,7 @@
             pltpu.SemaphoreType.DMA((5,)),
         ),
         out_spaces=(pltpu.HBM, pltpu.HBM, pltpu.VMEM),
-    )(window, state, faces, far, near, placing, tags)
+    )(window, state, faces, left, right, placing, tags)
     arrived = lax.all_to_all(
         outgoing.reshape(OWNERS, 1, 384), ("gy", "gz"), split_axis=0, concat_axis=0, tiled=True
     )

time: 57 us -> 55.4 us (0.972)
  waiting for transfers between devices: 7.36 us -> 6.23 us
    ppermute x2 -> x1, starting transfers between devices: 16.3 us -> 5.93 us  [swap(): far = lax.ppermute(far, axis, far_pairs)]
    ppermute x1 -> x2, starting transfers between devices: 0.84 us -> 9.43 us  [ring(): lax.ppermute(low, axis, [((i + 1) % count, i) for i in range(count)])]
    ppermute x1 -> x2, starting transfers between devices: 3.21 us -> 6.91 us  [ring(): lax.ppermute(high, axis, [(i, (i + 1) % count) for i in range(count)])]
    ppermute x2 -> x1, starting transfers between devices: 3.84 us -> 1.92 us  [swap(): return (lax.ppermute(near, axis, near_pairs), far)]
    ppermute x2 -> x1, waiting for transfers between devices: 3.42 us -> 2.29 us  [swap(): return (lax.ppermute(near, axis, near_pairs), far)]
    ppermute x1 -> x2, waiting for transfers between devices: 1.18 us -> 1.18 us  [ring(): lax.ppermute(high, axis, [(i, (i + 1) % count) for i in range(count)])]
    ppermute x1 -> x2, waiting for transfers between devices: 2.75 us -> 2.75 us  [ring(): lax.ppermute(low, axis, [((i + 1) % count, i) for i in range(count)])]
  transfers between devices with their start and end apart: 6 -> 6, of which waited for: 4 -> 3; matrix products, arithmetic and copies ran while one was open for 0% -> 0% of each run, Pallas kernels for 3% -> 3%
where the time goes in v7:
time: 55.4 us; the launch traced here: 55.1 us
  starting transfers between devices  24.2 us (44%)
  blocking collectives  16.8 us (30%)
  waiting for transfers between devices  6.23 us (11%)
  Pallas kernels  5.44 us (10%)
  local copies, waits for them, and re-layouts  0.87 us (2%)
  other arithmetic  0.8 us (1%)
  between operations  0.77 us (1%)
    all_to_all x1, blocking collectives, per_device(): lax.all_to_all(outgoing.reshape(OWNERS, 1, 384), ('gy', 'gz'), split_axis...  16.8 us
    ppermute x2, starting transfers between devices, ring(): lax.ppermute(low, axis, [((i + 1) % count, i) for i in range(count)])  9.43 us
    ppermute x2, starting transfers between devices, ring(): lax.ppermute(high, axis, [(i, (i + 1) % count) for i in range(count)])  6.91 us
    ppermute x1, starting transfers between devices, swap(): far = lax.ppermute(far, axis, far_pairs)  5.93 us
    ppermute x2, waiting for transfers between devices, ring(): lax.ppermute(low, axis, [((i + 1) % count, i) for i in range(count)])  2.75 us
    pallas_call x1, Pallas kernels, per_device(): call(step_two, (f32(10, 8, 8, 128), f32(8, 8, 128), f32(OWNERS, 384)), 's...  2.51 us
    ppermute x1, waiting for transfers between devices, swap(): return (lax.ppermute(near, axis, near_pairs), far)  2.29 us
    ppermute x1, starting transfers between devices, swap(): return (lax.ppermute(near, axis, near_pairs), far)  1.92 us
  transfers between devices with their start and end apart: 6, of which 3 were waited for; matrix products, arithmetic and copies ran while one was open for 0% of the time, Pallas kernels for 3%

profile of v7, /device:TPU:1, one launch (start us, length us, event | category | flops | bytes accessed | tf_op | source)
XLA Modules:
  0.0 55.1 jit_solution(5349098269369395412)
XLA Ops:
  0.6 0.0 copy-start.3
  0.6 0.0 copy-start
  0.7 0.8 %subtract_bitcast_fusion = f32[1,8,8,128]{3,2,1,0:T(8,128)S(1)} fusion(s32[8,8,128]{2,1,0:T(8,128)} %param.7), kind=kLoop, calls=%fused_computation.2 | loop fusion | flops 16384 | bytes 65536 | tf_op jit(solution)/shard_map/sub | solution.py:505
  1.4 0.0 copy-done.3
  1.5 0.1 copy-done
  1.6 5.9 %collective-permute-start = (f32[17,8,128]{2,1,0:T(8,128)S(1)}, f32[17,8,128]{2,1,0:T(8,128)S(1)}, u32[]{:S(2)}, u32[]{:S(2)}) collective-permute-start(f32[17,8,128]{2,1,0:T(8,128)S(1)} %get-tuple-element.17), channel_id=1, source_target_pairs={{0,7},{1,2},{2,1},{3,4},{4,3},{5,6},{6,5},{7,0},{8,15},{9,10},{10,... | collective-permute-start | bytes 208904 | tf_op jit(solution)/shard_map/ppermute | solution.py:43
  7.5 1.9 %collective-permute-start.1 = (f32[17,8,128]{2,1,0:T(8,128)S(1)}, f32[17,8,128]{2,1,0:T(8,128)S(1)}, u32[]{:S(2)}, u32[]{:S(2)}) collective-permute-start(f32[17,8,128]{2,1,0:T(8,128)S(1)} %get-tuple-element.18), channel_id=1, source_target_pairs={{0,1},{1,0},{2,3},{3,2},{4,5},{5,4},{6,7},{7,6},{8,9},{9,8},{10,11... | collective-permute-start | bytes 208904 | tf_op jit(solution)/shard_map/ppermute | solution.py:44
  9.4 0.0 copy-start.1
  9.4 0.0 copy-start.2
  9.5 0.6 %copy-done.1 = s32[1,1,1,64,1]{3,4,2,1,0:T(1,128)S(1)} copy-done((s32[1,1,1,64,1]{3,4,2,1,0:T(1,128)S(1)}, s32[1,1,1,64,1]{3,4,2,1,0:T(1,128)}, u32[]{:S(2)}) %copy-start.1) | copy-done | bytes 280
  10.1 0.0 copy-done.2
  10.1 0.1 place_blocks.1
  10.3 0.0 collective-permute-done.got_far
  10.3 2.3 %collective-permute-done.1.got_near = f32[17,8,128]{2,1,0:T(8,128)S(1)} collective-permute-done((f32[17,8,128]{2,1,0:T(8,128)S(1)}, f32[17,8,128]{2,1,0:T(8,128)S(1)}, u32[]{:S(2)}, u32[]{:S(2)}) %collective-permute-start.1) | collective-permute-done | bytes 69664 | tf_op jit(solution)/shard_map/ppermute | solution.py:44
  12.6 3.2 %collective-permute-start.2 = (f32[34,8,128]{2,1,0:T(8,128)S(1)}, f32[34,8,128]{2,1,0:T(8,128)S(1)}, u32[]{:S(2)}, u32[]{:S(2)}) collective-permute-start(f32[34,8,128]{2,1,0:T(8,128)S(1)} %get-tuple-element.21), channel_id=1, source_target_pairs={{0,8},{8,16},{16,24},{24,32},{32,40},{40,48},{48,56},{56,0},{1,9},... | collective-permute-start | bytes 417800 | tf_op jit(solution)/shard_map/ppermute | solution.py:34
  15.8 0.8 %collective-permute-start.3 = (f32[34,8,128]{2,1,0:T(8,128)S(1)}, f32[34,8,128]{2,1,0:T(8,128)S(1)}, u32[]{:S(2)}, u32[]{:S(2)}) collective-permute-start(f32[34,8,128]{2,1,0:T(8,128)S(1)} %get-tuple-element.22), channel_id=1, source_target_pairs={{8,0},{16,8},{24,16},{32,24},{40,32},{48,40},{56,48},{0,56},{9,1},... | collective-permute-start | bytes 417800 | tf_op jit(solution)/shard_map/ppermute | solution.py:35
  16.7 1.2 %collective-permute-done.2.got_below = f32[34,8,128]{2,1,0:T(8,128)S(1)} collective-permute-done((f32[34,8,128]{2,1,0:T(8,128)S(1)}, f32[34,8,128]{2,1,0:T(8,128)S(1)}, u32[]{:S(2)}, u32[]{:S(2)}) %collective-permute-start.2) | collective-permute-done | bytes 139296 | tf_op jit(solution)/shard_map/ppermute | solution.py:34
  17.8 2.8 %collective-permute-done.3.got_above = f32[34,8,128]{2,1,0:T(8,128)S(1)} collective-permute-done((f32[34,8,128]{2,1,0:T(8,128)S(1)}, f32[34,8,128]{2,1,0:T(8,128)S(1)}, u32[]{:S(2)}, u32[]{:S(2)}) %collective-permute-start.3) | collective-permute-done | bytes 139296 | tf_op jit(solution)/shard_map/ppermute | solution.py:35
  20.6 0.4 pack_streamwise.1
  21.0 3.7 %collective-permute-start.4 = (f32[5,8,128]{2,1,0:T(8,128)S(1)}, f32[5,8,128]{2,1,0:T(8,128)S(1)}, u32[]{:S(2)}, u32[]{:S(2)}) collective-permute-start(f32[5,8,128]{2,1,0:T(8,128)S(1)} %get-tuple-element.25), channel_id=1, source_target_pairs={{0,64},{64,128},{128,192},{192,256},{256,320},{320,384},{384,448},... | collective-permute-start | bytes 61448 | tf_op jit(solution)/shard_map/ppermute | solution.py:34
  24.7 8.6 %collective-permute-start.5 = (f32[5,8,128]{2,1,0:T(8,128)S(1)}, f32[5,8,128]{2,1,0:T(8,128)S(1)}, u32[]{:S(2)}, u32[]{:S(2)}) collective-permute-start(f32[5,8,128]{2,1,0:T(8,128)S(1)} %get-tuple-element.26), channel_id=1, source_target_pairs={{64,0},{128,64},{192,128},{256,192},{320,256},{384,320},{448,384},... | collective-permute-start | bytes 61448 | tf_op jit(solution)/shard_map/ppermute | solution.py:35
  33.3 1.4 %step_one.1.state_one = f32[10,12,16,128]{3,2,1,0:T(8,128)S(1)} custom-call(f32[5,16,16,128]{3,2,1,0:T(8,128)S(1)} %get-tuple-element.23.window), custom_call_target="tpu_custom_call" | custom-call | tf_op jit(solution)/shard_map/step_one/pallas_call | solution.py:518
  34.7 0.0 collective-permute-done.4.from_left
  34.7 0.0 collective-permute-done.5.from_right
  34.7 2.5 %step_two.1 = (f32[10,8,8,128]{3,2,1,0:T(8,128)}, f32[8,8,128]{2,1,0:T(8,128)}, f32[64,384]{1,0:T(8,128)S(1)}) custom-call(f32[5,16,16,128]{3,2,1,0:T(8,128)S(1)} %get-tuple-element.23.window, f32[10,12,16,128]{3,2,1,0:T(8,128)S(1)} %step_one.1.state_one, f32[5,2,8,128]{3,2,1,0:T(8,128)S(1)} %get-tuple-element.24.faces, ...), custom_call_target="tpu_custom_call" | custom-call | tf_op jit(solution)/shard_map/step_two/pallas_call | solution.py:521
  37.3 0.1 copy.8
  37.4 16.8 %all_to_all.5 = f32[64,1,384]{2,1,0:T(1,128)S(1)} all-to-all(f32[64,1,384]{2,1,0:T(1,128)S(1)} %copy.8), channel_id=1, replica_groups=mesh['gx'=8,'gy'=8,'gz'=8] {'gy','gz'}, dimensions={0} | all-to-all | bytes 196608 | tf_op jit(solution)/shard_map/all_to_all | solution.py:538
  54.2 0.9 %sum_slots.1 = f32[16,160]{1,0:T(8,128)} custom-call(f32[64,384]{1,0:T(8,128)S(1)} %bitcast.10), custom_call_target="tpu_custom_call" | custom-call | tf_op jit(solution)/shard_map/sum_slots/pallas_call | solution.py:541
  (4 shorter events, 0.1 us)
Async XLA Ops:
  0.6 0.8 %copy-start.3 = (f32[8,8,128]{2,1,0:T(8,128)S(1)}, f32[8,8,128]{2,1,0:T(8,128)}, u32[]{:S(2)}) copy-start(f32[8,8,128]{2,1,0:T(8,128)} %param.5) | copy-start | bytes 98308
  0.6 0.9 %copy-start = (f32[3,8,8,128]{3,2,1,0:T(8,128)S(1)}, f32[3,8,8,128]{3,2,1,0:T(8,128)}, u32[]{:S(2)}) copy-start(f32[3,8,8,128]{3,2,1,0:T(8,128)} %velocity.3) | copy-start | bytes 294916
  1.6 8.7 %collective-permute-start = (f32[17,8,128]{2,1,0:T(8,128)S(1)}, f32[17,8,128]{2,1,0:T(8,128)S(1)}, u32[]{:S(2)}, u32[]{:S(2)}) collective-permute-start(f32[17,8,128]{2,1,0:T(8,128)S(1)} %get-tuple-element.17), channel_id=1, source_target_pairs={{0,7},{1,2},{2,1},{3,4},{4,3},{5,6},{6,5},{7,0},{8,15},{9,10},{10,... | collective-permute-start | bytes 208904 | tf_op jit(solution)/shard_map/ppermute | solution.py:43
  7.5 5.1 %collective-permute-start.1 = (f32[17,8,128]{2,1,0:T(8,128)S(1)}, f32[17,8,128]{2,1,0:T(8,128)S(1)}, u32[]{:S(2)}, u32[]{:S(2)}) collective-permute-start(f32[17,8,128]{2,1,0:T(8,128)S(1)} %get-tuple-element.18), channel_id=1, source_target_pairs={{0,1},{1,0},{2,3},{3,2},{4,5},{5,4},{6,7},{7,6},{8,9},{9,8},{10,11... | collective-permute-start | bytes 208904 | tf_op jit(solution)/shard_map/ppermute | solution.py:44
  9.4 0.7 %copy-start.1 = (s32[1,1,1,64,1]{3,4,2,1,0:T(1,128)S(1)}, s32[1,1,1,64,1]{3,4,2,1,0:T(1,128)}, u32[]{:S(2)}) copy-start(s32[1,1,1,64,1]{3,4,2,1,0:T(1,128)} %param.8) | copy-start | bytes 772
  9.4 0.7 %copy-start.2 = (s32[1,1,1,64,1]{3,4,2,1,0:T(1,128)S(1)}, s32[1,1,1,64,1]{3,4,2,1,0:T(1,128)}, u32[]{:S(2)}) copy-start(s32[1,1,1,64,1]{3,4,2,1,0:T(1,128)} %param.9) | copy-start | bytes 772
  12.6 5.2 %collective-permute-start.2 = (f32[34,8,128]{2,1,0:T(8,128)S(1)}, f32[34,8,128]{2,1,0:T(8,128)S(1)}, u32[]{:S(2)}, u32[]{:S(2)}) collective-permute-start(f32[34,8,128]{2,1,0:T(8,128)S(1)} %get-tuple-element.21), channel_id=1, source_target_pairs={{0,8},{8,16},{16,24},{24,32},{32,40},{40,48},{48,56},{56,0},{1,9},... | collective-permute-start | bytes 417800 | tf_op jit(solution)/shard_map/ppermute | solution.py:34
  15.8 4.8 %collective-permute-start.3 = (f32[34,8,128]{2,1,0:T(8,128)S(1)}, f32[34,8,128]{2,1,0:T(8,128)S(1)}, u32[]{:S(2)}, u32[]{:S(2)}) collective-permute-start(f32[34,8,128]{2,1,0:T(8,128)S(1)} %get-tuple-element.22), channel_id=1, source_target_pairs={{8,0},{16,8},{24,16},{32,24},{40,32},{48,40},{56,48},{0,56},{9,1},... | collective-permute-start | bytes 417800 | tf_op jit(solution)/shard_map/ppermute | solution.py:35
  21.0 13.8 %collective-permute-start.4 = (f32[5,8,128]{2,1,0:T(8,128)S(1)}, f32[5,8,128]{2,1,0:T(8,128)S(1)}, u32[]{:S(2)}, u32[]{:S(2)}) collective-permute-start(f32[5,8,128]{2,1,0:T(8,128)S(1)} %get-tuple-element.25), channel_id=1, source_target_pairs={{0,64},{64,128},{128,192},{192,256},{256,320},{320,384},{384,448},... | collective-permute-start | bytes 61448 | tf_op jit(solution)/shard_map/ppermute | solution.py:34
  24.7 10.1 %collective-permute-start.5 = (f32[5,8,128]{2,1,0:T(8,128)S(1)}, f32[5,8,128]{2,1,0:T(8,128)S(1)}, u32[]{:S(2)}, u32[]{:S(2)}) collective-permute-start(f32[5,8,128]{2,1,0:T(8,128)S(1)} %get-tuple-element.26), channel_id=1, source_target_pairs={{64,0},{128,64},{192,128},{256,192},{320,256},{384,320},{448,384},... | collective-permute-start | bytes 61448 | tf_op jit(solution)/shard_map/ppermute | solution.py:35

commit v8 on v7

--- a/solution.py
+++ b/solution.py
@@ -6,7 +6,9 @@
 from jax.sharding import PartitionSpec as P
 
 SLOTS = 16
-OWNERS = 64
+SPAN_Y = 8
+SPAN_Z = 8
+OWNERS = SPAN_Y * SPAN_Z
 WALE_COEFF = 0.5
 BASE_VISCOSITY = 0.01
 WALE_FLOOR = 1e-10
@@ -29,11 +31,14 @@
     return lax.rem(lax.axis_index(axis), 2) == 0
 
 
-def ring(high, low, axis):
+def from_lower(high, axis):
     count = lax.axis_size(axis)
-    below = lax.ppermute(high, axis, [(i, (i + 1) % count) for i in range(count)])
-    above = lax.ppermute(low, axis, [((i + 1) % count, i) for i in range(count)])
-    return below, above
+    return lax.ppermute(high, axis, [(i, (i + 1) % count) for i in range(count)])
+
+
+def from_upper(low, axis):
+    count = lax.axis_size(axis)
+    return lax.ppermute(low, axis, [((i + 1) % count, i) for i in range(count)])
 
 
 def swap(near, far, axis):
@@ -106,7 +111,7 @@
         low[31 + place] = lower
 
 
-def pack_streamwise(planes, got_below, got_above, window, faces, right, left):
+def pack_streamwise(planes, got_above, got_below, window, faces, right, left):
     row = lax.broadcasted_iota(jnp.int32, (8, 128), 0)
     front = row < 4
     lane = lax.broadcasted_iota(jnp.int32, (8, 128), 1)
@@ -164,7 +169,7 @@
     earlier = (owner_column == owner_row) & (row < block)
     owner = owner_row.astype(jnp.int32)
     rank = jnp.sum(jnp.where(earlier, 1.0, 0.0), axis=0, keepdims=True).astype(jnp.int32)
-    position = rank * OWNERS + owner
+    position = rank * OWNERS + lax.rem(owner, SPAN_Z) * SPAN_Y + lax.div(owner, SPAN_Z)
     rows = lax.broadcasted_iota(jnp.int32, (128, 128), 0)
     placing[...] = (rows == position).astype(jnp.float32)
     tags[...] = jnp.broadcast_to(0.5 * (slot + 1.0), (16, 128))
@@ -508,13 +513,14 @@
     planes, high, low = call(
         pack_spanwise, (f32(5, 16, 8, 128), f32(34, 8, 128), f32(34, 8, 128)), "pack_spanwise"
     )(scalars, velocity, far, near, placing)
-    below, above = ring(high, low, "gy")
+    above = from_upper(low, "gy")
+    below = from_lower(high, "gy")
     window, faces, right, left = call(
         pack_streamwise,
         (f32(5, 16, 16, 128), f32(5, 2, 8, 128), f32(5, 8, 128), f32(5, 8, 128)),
         "pack_streamwise",
-    )(planes, below, above)
-    left, right = ring(right, left, "gx")
+    )(planes, above, below)
+    right, left = from_lower(right, "gx"), from_upper(left, "gx")
     state = call(
         step_one, f32(10, 12, 16, 128), "step_one", (pltpu.VMEM((16, 16, 16, 128), jnp.float32),)
     )(window)
@@ -534,9 +540,9 @@
             pltpu.SemaphoreType.DMA((5,)),
         ),
         out_spaces=(pltpu.HBM, pltpu.HBM, pltpu.VMEM),
-    )(window, state, faces, left, right, placing, tags)
+    )(window, state, faces, right, left, placing, tags)
     arrived = lax.all_to_all(
-        outgoing.reshape(OWNERS, 1, 384), ("gy", "gz"), split_axis=0, concat_axis=0, tiled=True
+        outgoing.reshape(OWNERS, 1, 384), ("gz", "gy"), split_axis=0, concat_axis=0, tiled=True
     )
     coarse = call(sum_slots, f32(SLOTS, 160), "sum_slots")(arrived.reshape(OWNERS, 384))
     return moments, relaxation, coarse.reshape(1, 1, 1, SLOTS, 160)

time: 55.4 us -> 55.4 us (level)
  waiting for transfers between devices: 6.23 us -> 4.32 us
  blocking collectives: 16.8 us -> 18.5 us
    ppermute x4, waiting for transfers between devices: 3.94 us -> 2.03 us  [the longest x2 1.92 us: from_upper(): return lax.ppermute(low, axis, [((i + 1) % count, i) for i in range(count)])]
    all_to_all x1, blocking collectives: 16.8 us -> 18.5 us  [per_device(): lax.all_to_all(outgoing.reshape(OWNERS, 1, 384), ('gz', 'gy'), split_axis...]
where the time goes in v8:
time: 55.4 us; the launch traced here: 55.1 us
  starting transfers between devices  24.4 us (44%)
  blocking collectives  18.5 us (33%)
  Pallas kernels  5.44 us (10%)
  waiting for transfers between devices  4.32 us (8%)
  local copies, waits for them, and re-layouts  0.87 us (2%)
  other arithmetic  0.8 us (1%)
  between operations  0.77 us (1%)
    all_to_all x1, blocking collectives, per_device(): lax.all_to_all(outgoing.reshape(OWNERS, 1, 384), ('gz', 'gy'), split_axis...  18.5 us
    ppermute x2, starting transfers between devices, from_upper(): return lax.ppermute(low, axis, [((i + 1) % count, i) for i in range(count)])  12.6 us
    ppermute x1, starting transfers between devices, swap(): far = lax.ppermute(far, axis, far_pairs)  5.93 us
    ppermute x2, starting transfers between devices, from_lower(): lax.ppermute(high, axis, [(i, (i + 1) % count) for i in range(count)])  3.89 us
    pallas_call x1, Pallas kernels, per_device(): call(step_two, (f32(10, 8, 8, 128), f32(8, 8, 128), f32(OWNERS, 384)), 's...  2.51 us
    ppermute x1, waiting for transfers between devices, swap(): return (lax.ppermute(near, axis, near_pairs), far)  2.29 us
    ppermute x1, starting transfers between devices, swap(): return (lax.ppermute(near, axis, near_pairs), far)  1.92 us
    ppermute x2, waiting for transfers between devices, from_upper(): return lax.ppermute(low, axis, [((i + 1) % count, i) for i in range(count)])  1.92 us
  transfers between devices with their start and end apart: 6, of which 3 were waited for; matrix products, arithmetic and copies ran while one was open for 0% of the time, Pallas kernels for 3%

profile of v8, /device:TPU:1, one launch (start us, length us, event | category | flops | bytes accessed | tf_op | source)
XLA Modules:
  0.0 55.1 jit_solution(17705046101113123464)
XLA Ops:
  0.6 0.0 copy-start.3
  0.6 0.0 copy-start
  0.7 0.8 %subtract_bitcast_fusion = f32[1,8,8,128]{3,2,1,0:T(8,128)S(1)} fusion(s32[8,8,128]{2,1,0:T(8,128)} %param.7), kind=kLoop, calls=%fused_computation.2 | loop fusion | flops 16384 | bytes 65536 | tf_op jit(solution)/shard_map/sub | solution.py:510
  1.4 0.0 copy-done.3
  1.5 0.1 copy-done
  1.6 5.9 %collective-permute-start = (f32[17,8,128]{2,1,0:T(8,128)S(1)}, f32[17,8,128]{2,1,0:T(8,128)S(1)}, u32[]{:S(2)}, u32[]{:S(2)}) collective-permute-start(f32[17,8,128]{2,1,0:T(8,128)S(1)} %get-tuple-element.17), channel_id=1, source_target_pairs={{0,7},{1,2},{2,1},{3,4},{4,3},{5,6},{6,5},{7,0},{8,15},{9,10},{10,... | collective-permute-start | bytes 208904 | tf_op jit(solution)/shard_map/ppermute | solution.py:48
  7.5 1.9 %collective-permute-start.1 = (f32[17,8,128]{2,1,0:T(8,128)S(1)}, f32[17,8,128]{2,1,0:T(8,128)S(1)}, u32[]{:S(2)}, u32[]{:S(2)}) collective-permute-start(f32[17,8,128]{2,1,0:T(8,128)S(1)} %get-tuple-element.18), channel_id=1, source_target_pairs={{0,1},{1,0},{2,3},{3,2},{4,5},{5,4},{6,7},{7,6},{8,9},{9,8},{10,11... | collective-permute-start | bytes 208904 | tf_op jit(solution)/shard_map/ppermute | solution.py:49
  9.4 0.0 copy-start.1
  9.4 0.0 copy-start.2
  9.5 0.6 %copy-done.1 = s32[1,1,1,64,1]{3,4,2,1,0:T(1,128)S(1)} copy-done((s32[1,1,1,64,1]{3,4,2,1,0:T(1,128)S(1)}, s32[1,1,1,64,1]{3,4,2,1,0:T(1,128)}, u32[]{:S(2)}) %copy-start.1) | copy-done | bytes 280
  10.1 0.0 copy-done.2
  10.1 0.1 place_blocks.1
  10.3 0.0 collective-permute-done.got_far
  10.3 2.3 %collective-permute-done.1.got_near = f32[17,8,128]{2,1,0:T(8,128)S(1)} collective-permute-done((f32[17,8,128]{2,1,0:T(8,128)S(1)}, f32[17,8,128]{2,1,0:T(8,128)S(1)}, u32[]{:S(2)}, u32[]{:S(2)}) %collective-permute-start.1) | collective-permute-done | bytes 69664 | tf_op jit(solution)/shard_map/ppermute | solution.py:49
  12.6 4.0 %collective-permute-start.2 = (f32[34,8,128]{2,1,0:T(8,128)S(1)}, f32[34,8,128]{2,1,0:T(8,128)S(1)}, u32[]{:S(2)}, u32[]{:S(2)}) collective-permute-start(f32[34,8,128]{2,1,0:T(8,128)S(1)} %get-tuple-element.21), channel_id=1, source_target_pairs={{8,0},{16,8},{24,16},{32,24},{40,32},{48,40},{56,48},{0,56},{9,1},... | collective-permute-start | bytes 417800 | tf_op jit(solution)/shard_map/ppermute | solution.py:41
  16.6 0.0 collective-permute-start.3
  16.6 1.9 %collective-permute-done.2.got_above = f32[34,8,128]{2,1,0:T(8,128)S(1)} collective-permute-done((f32[34,8,128]{2,1,0:T(8,128)S(1)}, f32[34,8,128]{2,1,0:T(8,128)S(1)}, u32[]{:S(2)}, u32[]{:S(2)}) %collective-permute-start.2) | collective-permute-done | bytes 139296 | tf_op jit(solution)/shard_map/ppermute | solution.py:41
  18.6 0.1 collective-permute-done.3.got_below
  18.7 0.4 pack_streamwise.1
  19.0 3.9 %collective-permute-start.4 = (f32[5,8,128]{2,1,0:T(8,128)S(1)}, f32[5,8,128]{2,1,0:T(8,128)S(1)}, u32[]{:S(2)}, u32[]{:S(2)}) collective-permute-start(f32[5,8,128]{2,1,0:T(8,128)S(1)} %get-tuple-element.25), channel_id=1, source_target_pairs={{0,64},{64,128},{128,192},{192,256},{256,320},{320,384},{384,448},... | collective-permute-start | bytes 61448 | tf_op jit(solution)/shard_map/ppermute | solution.py:36
  22.9 8.6 %collective-permute-start.5 = (f32[5,8,128]{2,1,0:T(8,128)S(1)}, f32[5,8,128]{2,1,0:T(8,128)S(1)}, u32[]{:S(2)}, u32[]{:S(2)}) collective-permute-start(f32[5,8,128]{2,1,0:T(8,128)S(1)} %get-tuple-element.26), channel_id=1, source_target_pairs={{64,0},{128,64},{192,128},{256,192},{320,256},{384,320},{448,384},... | collective-permute-start | bytes 61448 | tf_op jit(solution)/shard_map/ppermute | solution.py:41
  31.5 1.4 %step_one.1.state_one = f32[10,12,16,128]{3,2,1,0:T(8,128)S(1)} custom-call(f32[5,16,16,128]{3,2,1,0:T(8,128)S(1)} %get-tuple-element.23.window), custom_call_target="tpu_custom_call" | custom-call | tf_op jit(solution)/shard_map/step_one/pallas_call | solution.py:524
  33.0 0.0 collective-permute-done.4.from_left
  33.0 0.0 collective-permute-done.5.from_right
  33.0 2.5 %step_two.1 = (f32[10,8,8,128]{3,2,1,0:T(8,128)}, f32[8,8,128]{2,1,0:T(8,128)}, f32[64,384]{1,0:T(8,128)S(1)}) custom-call(f32[5,16,16,128]{3,2,1,0:T(8,128)S(1)} %get-tuple-element.23.window, f32[10,12,16,128]{3,2,1,0:T(8,128)S(1)} %step_one.1.state_one, f32[5,2,8,128]{3,2,1,0:T(8,128)S(1)} %get-tuple-element.24.faces, ...), custom_call_target="tpu_custom_call" | custom-call | tf_op jit(solution)/shard_map/step_two/pallas_call | solution.py:527
  35.5 0.1 copy.8
  35.6 18.5 %all_to_all.5 = f32[64,1,384]{2,1,0:T(1,128)S(1)} all-to-all(f32[64,1,384]{2,1,0:T(1,128)S(1)} %copy.8), channel_id=1, replica_groups=mesh['gx'=8,'gy'=8,'gz'=8] {'gz','gy'}, dimensions={0} | all-to-all | bytes 196608 | tf_op jit(solution)/shard_map/all_to_all | solution.py:544
  54.2 0.9 %sum_slots.1 = f32[16,160]{1,0:T(8,128)} custom-call(f32[64,384]{1,0:T(8,128)S(1)} %bitcast.10), custom_call_target="tpu_custom_call" | custom-call | tf_op jit(solution)/shard_map/sum_slots/pallas_call | solution.py:547
  (4 shorter events, 0.1 us)
Async XLA Ops:
  0.6 0.8 %copy-start.3 = (f32[8,8,128]{2,1,0:T(8,128)S(1)}, f32[8,8,128]{2,1,0:T(8,128)}, u32[]{:S(2)}) copy-start(f32[8,8,128]{2,1,0:T(8,128)} %param.5) | copy-start | bytes 98308
  0.6 0.9 %copy-start = (f32[3,8,8,128]{3,2,1,0:T(8,128)S(1)}, f32[3,8,8,128]{3,2,1,0:T(8,128)}, u32[]{:S(2)}) copy-start(f32[3,8,8,128]{3,2,1,0:T(8,128)} %velocity.3) | copy-start | bytes 294916
  1.6 8.7 %collective-permute-start = (f32[17,8,128]{2,1,0:T(8,128)S(1)}, f32[17,8,128]{2,1,0:T(8,128)S(1)}, u32[]{:S(2)}, u32[]{:S(2)}) collective-permute-start(f32[17,8,128]{2,1,0:T(8,128)S(1)} %get-tuple-element.17), channel_id=1, source_target_pairs={{0,7},{1,2},{2,1},{3,4},{4,3},{5,6},{6,5},{7,0},{8,15},{9,10},{10,... | collective-permute-start | bytes 208904 | tf_op jit(solution)/shard_map/ppermute | solution.py:48
  7.5 5.1 %collective-permute-start.1 = (f32[17,8,128]{2,1,0:T(8,128)S(1)}, f32[17,8,128]{2,1,0:T(8,128)S(1)}, u32[]{:S(2)}, u32[]{:S(2)}) collective-permute-start(f32[17,8,128]{2,1,0:T(8,128)S(1)} %get-tuple-element.18), channel_id=1, source_target_pairs={{0,1},{1,0},{2,3},{3,2},{4,5},{5,4},{6,7},{7,6},{8,9},{9,8},{10,11... | collective-permute-start | bytes 208904 | tf_op jit(solution)/shard_map/ppermute | solution.py:49
  9.4 0.7 %copy-start.1 = (s32[1,1,1,64,1]{3,4,2,1,0:T(1,128)S(1)}, s32[1,1,1,64,1]{3,4,2,1,0:T(1,128)}, u32[]{:S(2)}) copy-start(s32[1,1,1,64,1]{3,4,2,1,0:T(1,128)} %param.8) | copy-start | bytes 772
  9.4 0.7 %copy-start.2 = (s32[1,1,1,64,1]{3,4,2,1,0:T(1,128)S(1)}, s32[1,1,1,64,1]{3,4,2,1,0:T(1,128)}, u32[]{:S(2)}) copy-start(s32[1,1,1,64,1]{3,4,2,1,0:T(1,128)} %param.9) | copy-start | bytes 772
  12.6 6.0 %collective-permute-start.2 = (f32[34,8,128]{2,1,0:T(8,128)S(1)}, f32[34,8,128]{2,1,0:T(8,128)S(1)}, u32[]{:S(2)}, u32[]{:S(2)}) collective-permute-start(f32[34,8,128]{2,1,0:T(8,128)S(1)} %get-tuple-element.21), channel_id=1, source_target_pairs={{8,0},{16,8},{24,16},{32,24},{40,32},{48,40},{56,48},{0,56},{9,1},... | collective-permute-start | bytes 417800 | tf_op jit(solution)/shard_map/ppermute | solution.py:41
  16.6 2.0 %collective-permute-start.3 = (f32[34,8,128]{2,1,0:T(8,128)S(1)}, f32[34,8,128]{2,1,0:T(8,128)S(1)}, u32[]{:S(2)}, u32[]{:S(2)}) collective-permute-start(f32[34,8,128]{2,1,0:T(8,128)S(1)} %get-tuple-element.22), channel_id=1, source_target_pairs={{0,8},{8,16},{16,24},{24,32},{32,40},{40,48},{48,56},{56,0},{1,9},... | collective-permute-start | bytes 417800 | tf_op jit(solution)/shard_map/ppermute | solution.py:36
  19.0 13.9 %collective-permute-start.4 = (f32[5,8,128]{2,1,0:T(8,128)S(1)}, f32[5,8,128]{2,1,0:T(8,128)S(1)}, u32[]{:S(2)}, u32[]{:S(2)}) collective-permute-start(f32[5,8,128]{2,1,0:T(8,128)S(1)} %get-tuple-element.25), channel_id=1, source_target_pairs={{0,64},{64,128},{128,192},{192,256},{256,320},{320,384},{384,448},... | collective-permute-start | bytes 61448 | tf_op jit(solution)/shard_map/ppermute | solution.py:36
  22.9 10.1 %collective-permute-start.5 = (f32[5,8,128]{2,1,0:T(8,128)S(1)}, f32[5,8,128]{2,1,0:T(8,128)S(1)}, u32[]{:S(2)}, u32[]{:S(2)}) collective-permute-start(f32[5,8,128]{2,1,0:T(8,128)S(1)} %get-tuple-element.26), channel_id=1, source_target_pairs={{64,0},{128,64},{192,128},{256,192},{320,256},{384,320},{448,384},... | collective-permute-start | bytes 61448 | tf_op jit(solution)/shard_map/ppermute | solution.py:41

commit v9 on v8

--- a/solution.py
+++ b/solution.py
@@ -111,7 +111,20 @@
         low[31 + place] = lower
 
 
-def pack_streamwise(planes, got_above, got_below, window, faces, right, left):
+def gather_faces(cells, plane, moved):
+    lane = lax.broadcasted_iota(jnp.int32, (8, 128), 1)
+    return jnp.where(lane // 8 == plane, roll(cells, 8 * plane + 4, 1), moved)
+
+
+def pack_inner(planes, inner_faces):
+    for field in range(5):
+        moved = jnp.zeros((8, 128), jnp.float32)
+        for plane in range(16):
+            moved = gather_faces(planes[field, plane], plane, moved)
+        inner_faces[field] = moved
+
+
+def pack_streamwise(inner_faces, got_above, got_below, outer, faces, right, left):
     row = lax.broadcasted_iota(jnp.int32, (8, 128), 0)
     front = row < 4
     lane = lax.broadcasted_iota(jnp.int32, (8, 128), 1)
@@ -135,14 +148,11 @@
         return jnp.where(front, above, roll(below, 4, 0))
 
     for field in range(5):
-        own = [jnp.zeros((8, 128), jnp.float32) for _ in range(2)]
+        own = [inner_faces[field], jnp.zeros((8, 128), jnp.float32)]
         for plane in range(16):
-            inner, outer = planes[field, plane], outer_rows(field, plane)
-            window[field, plane, 0:8] = inner
-            window[field, plane, 8:16] = outer
-            here = lane // 8 == plane
-            own[0] = jnp.where(here, roll(inner, 8 * plane + 4, 1), own[0])
-            own[1] = jnp.where(here, roll(outer, 8 * plane + 4, 1), own[1])
+            cells = outer_rows(field, plane)
+            outer[field, plane] = cells
+            own[1] = gather_faces(cells, plane, own[1])
         faces[field, 0] = own[0]
         faces[field, 1] = own[1]
         even_spot = lane % 8 < 4
@@ -289,9 +299,9 @@
 PAIRS = ((0, 0), (1, 1), (2, 2), (0, 1), (0, 2), (1, 2))
 
 
-def first_state(ref, where):
-    density = ref[(0,) + where]
-    speed = [ref[(1 + k,) + where] for k in range(3)]
+def first_state(member):
+    density = member(0)
+    speed = [member(1 + k) for k in range(3)]
     momentum = [density * speed[k] for k in range(3)]
     stress = [momentum[one] * speed[two] for one, two in PAIRS]
     return density, speed, momentum, stress
@@ -305,10 +315,13 @@
     return [roll(value, -1, 1) - roll(value, 1, 1) for value in speed]
 
 
-def step_one(window, state, sums):
+def step_one(planes, outer, state, sums):
+    def cells(number, plane):
+        return jnp.concatenate([planes[number, plane], outer[number, plane]], axis=0)
+
     for plane in range(1, 15):
-        density, speed, momentum, stress = first_state(window, (plane,))
-        dz = [window[1 + k, plane + 1] - window[1 + k, plane - 1] for k in range(3)]
+        density, speed, momentum, stress = first_state(lambda number: cells(number, plane))
+        dz = [cells(1 + k, plane + 1) - cells(1 + k, plane - 1) for k in range(3)]
         dy = row_differences(speed)
         dx = lane_differences(speed)
         relaxation = wale([[dz[k], dy[k], dx[k]] for k in range(3)])
@@ -322,14 +335,14 @@
             [sums[k, plane] for k in range(6)],
             [sums[6 + k, plane - 1] for k in range(5)],
             [sums[11 + k, plane + 1] for k in range(5)],
-            window[4, plane],
+            cells(4, plane),
         )
         for k, value in enumerate([density] + momentum + stress):
             state[k, plane - 2] = value
 
 
 def step_two(
-    window, state_one, faces, from_left, from_right, placing, tags, moments_out, relaxation_out, outgoing,
+    planes, state_one, faces, from_left, from_right, placing, tags, moments_out, relaxation_out, outgoing,
     state, sums, strip, strip_sums, edge, pooled, moments, relaxations, left_sems,
 ):
     lane = lax.broadcasted_iota(jnp.int32, (16, 128), 1)
@@ -357,7 +370,7 @@
 
     def strip_pass(step, half):
         if step == 0:
-            density, speed, momentum, stress = first_state(strip, (half,))
+            density, speed, momentum, stress = first_state(lambda number: strip[number, half])
         else:
             density = strip[0, half]
             speed = [strip[1 + k, half] for k in range(3)]
@@ -446,7 +459,7 @@
                 [sums[k, plane] for k in range(6)],
                 [sums[6 + k, plane - 1] for k in range(5)],
                 [sums[11 + k, plane + 1] for k in range(5)],
-                window[4, plane, 0:8],
+                planes[4, plane],
             )
             members = [density] + momentum + [stress[k] + third for k in range(3)] + stress[3:]
             for k in range(10):
@@ -515,15 +528,16 @@
     )(scalars, velocity, far, near, placing)
     above = from_upper(low, "gy")
     below = from_lower(high, "gy")
-    window, faces, right, left = call(
+    (inner_faces,) = call(pack_inner, (f32(5, 8, 128),), "pack_inner")(planes)
+    outer, faces, right, left = call(
         pack_streamwise,
-        (f32(5, 16, 16, 128), f32(5, 2, 8, 128), f32(5, 8, 128), f32(5, 8, 128)),
+        (f32(5, 16, 8, 128), f32(5, 2, 8, 128), f32(5, 8, 128), f32(5, 8, 128)),
         "pack_streamwise",
-    )(planes, above, below)
+    )(inner_faces, above, below)
     right, left = from_lower(right, "gx"), from_upper(left, "gx")
     state = call(
         step_one, f32(10, 12, 16, 128), "step_one", (pltpu.VMEM((16, 16, 16, 128), jnp.float32),)
-    )(window)
+    )(planes, outer)
     moments, relaxation, outgoing = call(
         step_two,
         (f32(10, 8, 8, 128), f32(8, 8, 128), f32(OWNERS, 384)),
@@ -540,7 +554,7 @@
             pltpu.SemaphoreType.DMA((5,)),
         ),
         out_spaces=(pltpu.HBM, pltpu.HBM, pltpu.VMEM),
-    )(window, state, faces, right, left, placing, tags)
+    )(planes, state, faces, right, left, placing, tags)
     arrived = lax.all_to_all(
         outgoing.reshape(OWNERS, 1, 384), ("gz", "gy"), split_axis=0, concat_axis=0, tiled=True
     )

time: 55.4 us -> 55.3 us (level)
  no operation moved by 1% of the time
where the time goes in v9:
time: 55.3 us; the launch traced here: 55 us
  starting transfers between devices  24.4 us (44%)
  blocking collectives  18.5 us (33%)
  Pallas kernels  5.48 us (10%)
  waiting for transfers between devices  4.17 us (8%)
  local copies, waits for them, and re-layouts  0.87 us (2%)
  other arithmetic  0.8 us (1%)
  between operations  0.77 us (1%)
    all_to_all x1, blocking collectives, per_device(): lax.all_to_all(outgoing.reshape(OWNERS, 1, 384), ('gz', 'gy'), split_axis...  18.5 us
    ppermute x2, starting transfers between devices, from_upper(): return lax.ppermute(low, axis, [((i + 1) % count, i) for i in range(count)])  12.6 us
    ppermute x1, starting transfers between devices, swap(): far = lax.ppermute(far, axis, far_pairs)  5.93 us
    ppermute x2, starting transfers between devices, from_lower(): lax.ppermute(high, axis, [(i, (i + 1) % count) for i in range(count)])  3.89 us
    pallas_call x1, Pallas kernels, per_device(): call(step_two, (f32(10, 8, 8, 128), f32(8, 8, 128), f32(OWNERS, 384)), 's...  2.53 us
    ppermute x1, waiting for transfers between devices, swap(): return (lax.ppermute(near, axis, near_pairs), far)  2.29 us
    ppermute x1, starting transfers between devices, swap(): return (lax.ppermute(near, axis, near_pairs), far)  1.92 us
    ppermute x2, waiting for transfers between devices, from_upper(): return lax.ppermute(low, axis, [((i + 1) % count, i) for i in range(count)])  1.77 us
  transfers between devices with their start and end apart: 6, of which 3 were waited for; matrix products, arithmetic and copies ran while one was open for 0% of the time, Pallas kernels for 3%

profile of v9, /device:TPU:1, one launch (start us, length us, event | category | flops | bytes accessed | tf_op | source)
XLA Modules:
  0.0 55.0 jit_solution(15798498384254899537)
XLA Ops:
  0.6 0.0 copy-start.3
  0.6 0.0 copy-start
  0.7 0.8 %subtract_bitcast_fusion = f32[1,8,8,128]{3,2,1,0:T(8,128)S(1)} fusion(s32[8,8,128]{2,1,0:T(8,128)} %param.7), kind=kLoop, calls=%fused_computation.2 | loop fusion | flops 16384 | bytes 65536 | tf_op jit(solution)/shard_map/sub | solution.py:523
  1.4 0.0 copy-done.3
  1.5 0.1 copy-done
  1.6 5.9 %collective-permute-start = (f32[17,8,128]{2,1,0:T(8,128)S(1)}, f32[17,8,128]{2,1,0:T(8,128)S(1)}, u32[]{:S(2)}, u32[]{:S(2)}) collective-permute-start(f32[17,8,128]{2,1,0:T(8,128)S(1)} %get-tuple-element.17), channel_id=1, source_target_pairs={{0,7},{1,2},{2,1},{3,4},{4,3},{5,6},{6,5},{7,0},{8,15},{9,10},{10,... | collective-permute-start | bytes 208904 | tf_op jit(solution)/shard_map/ppermute | solution.py:48
  7.5 1.9 %collective-permute-start.1 = (f32[17,8,128]{2,1,0:T(8,128)S(1)}, f32[17,8,128]{2,1,0:T(8,128)S(1)}, u32[]{:S(2)}, u32[]{:S(2)}) collective-permute-start(f32[17,8,128]{2,1,0:T(8,128)S(1)} %get-tuple-element.18), channel_id=1, source_target_pairs={{0,1},{1,0},{2,3},{3,2},{4,5},{5,4},{6,7},{7,6},{8,9},{9,8},{10,11... | collective-permute-start | bytes 208904 | tf_op jit(solution)/shard_map/ppermute | solution.py:49
  9.4 0.0 copy-start.1
  9.4 0.0 copy-start.2
  9.5 0.6 %copy-done.1 = s32[1,1,1,64,1]{3,4,2,1,0:T(1,128)S(1)} copy-done((s32[1,1,1,64,1]{3,4,2,1,0:T(1,128)S(1)}, s32[1,1,1,64,1]{3,4,2,1,0:T(1,128)}, u32[]{:S(2)}) %copy-start.1) | copy-done | bytes 280
  10.1 0.0 copy-done.2
  10.1 0.1 place_blocks.1
  10.3 0.0 collective-permute-done.got_far
  10.3 2.3 %collective-permute-done.1.got_near = f32[17,8,128]{2,1,0:T(8,128)S(1)} collective-permute-done((f32[17,8,128]{2,1,0:T(8,128)S(1)}, f32[17,8,128]{2,1,0:T(8,128)S(1)}, u32[]{:S(2)}, u32[]{:S(2)}) %collective-permute-start.1) | collective-permute-done | bytes 69664 | tf_op jit(solution)/shard_map/ppermute | solution.py:49
  12.6 4.0 %collective-permute-start.2 = (f32[34,8,128]{2,1,0:T(8,128)S(1)}, f32[34,8,128]{2,1,0:T(8,128)S(1)}, u32[]{:S(2)}, u32[]{:S(2)}) collective-permute-start(f32[34,8,128]{2,1,0:T(8,128)S(1)} %get-tuple-element.21), channel_id=1, source_target_pairs={{8,0},{16,8},{24,16},{32,24},{40,32},{48,40},{56,48},{0,56},{9,1},... | collective-permute-start | bytes 417800 | tf_op jit(solution)/shard_map/ppermute | solution.py:41
  16.6 0.0 collective-permute-start.3
  16.6 0.1 pack_inner.1.inner_faces
  16.8 1.8 %collective-permute-done.2.got_above = f32[34,8,128]{2,1,0:T(8,128)S(1)} collective-permute-done((f32[34,8,128]{2,1,0:T(8,128)S(1)}, f32[34,8,128]{2,1,0:T(8,128)S(1)}, u32[]{:S(2)}, u32[]{:S(2)}) %collective-permute-start.2) | collective-permute-done | bytes 139296 | tf_op jit(solution)/shard_map/ppermute | solution.py:41
  18.6 0.1 collective-permute-done.3.got_below
  18.7 0.2 pack_streamwise.1
  18.9 3.9 %collective-permute-start.4 = (f32[5,8,128]{2,1,0:T(8,128)S(1)}, f32[5,8,128]{2,1,0:T(8,128)S(1)}, u32[]{:S(2)}, u32[]{:S(2)}) collective-permute-start(f32[5,8,128]{2,1,0:T(8,128)S(1)} %get-tuple-element.25), channel_id=1, source_target_pairs={{0,64},{64,128},{128,192},{192,256},{256,320},{320,384},{384,448},... | collective-permute-start | bytes 61448 | tf_op jit(solution)/shard_map/ppermute | solution.py:36
  22.8 8.6 %collective-permute-start.5 = (f32[5,8,128]{2,1,0:T(8,128)S(1)}, f32[5,8,128]{2,1,0:T(8,128)S(1)}, u32[]{:S(2)}, u32[]{:S(2)}) collective-permute-start(f32[5,8,128]{2,1,0:T(8,128)S(1)} %get-tuple-element.26), channel_id=1, source_target_pairs={{64,0},{128,64},{192,128},{256,192},{320,256},{384,320},{448,384},... | collective-permute-start | bytes 61448 | tf_op jit(solution)/shard_map/ppermute | solution.py:41
  31.4 1.5 %step_one.1.state_one = f32[10,12,16,128]{3,2,1,0:T(8,128)S(1)} custom-call(f32[5,16,8,128]{3,2,1,0:T(8,128)S(1)} %get-tuple-element.20.planes, f32[5,16,8,128]{3,2,1,0:T(8,128)S(1)} %get-tuple-element.23.outer), custom_call_target="tpu_custom_call" | custom-call | tf_op jit(solution)/shard_map/step_one/pallas_call | solution.py:538
  32.9 0.0 collective-permute-done.4.from_left
  32.9 0.0 collective-permute-done.5.from_right
  32.9 2.5 %step_two.1 = (f32[10,8,8,128]{3,2,1,0:T(8,128)}, f32[8,8,128]{2,1,0:T(8,128)}, f32[64,384]{1,0:T(8,128)S(1)}) custom-call(f32[5,16,8,128]{3,2,1,0:T(8,128)S(1)} %get-tuple-element.20.planes, f32[10,12,16,128]{3,2,1,0:T(8,128)S(1)} %step_one.1.state_one, f32[5,2,8,128]{3,2,1,0:T(8,128)S(1)} %get-tuple-element.24.faces, ...), custom_call_target="tpu_custom_call" | custom-call | tf_op jit(solution)/shard_map/step_two/pallas_call | solution.py:541
  35.4 0.1 copy.8
  35.5 18.5 %all_to_all.5 = f32[64,1,384]{2,1,0:T(1,128)S(1)} all-to-all(f32[64,1,384]{2,1,0:T(1,128)S(1)} %copy.8), channel_id=1, replica_groups=mesh['gx'=8,'gy'=8,'gz'=8] {'gz','gy'}, dimensions={0} | all-to-all | bytes 196608 | tf_op jit(solution)/shard_map/all_to_all | solution.py:558
  54.0 0.9 %sum_slots.1 = f32[16,160]{1,0:T(8,128)} custom-call(f32[64,384]{1,0:T(8,128)S(1)} %bitcast.10), custom_call_target="tpu_custom_call" | custom-call | tf_op jit(solution)/shard_map/sum_slots/pallas_call | solution.py:561
  (4 shorter events, 0.1 us)
Async XLA Ops:
  0.6 0.8 %copy-start.3 = (f32[8,8,128]{2,1,0:T(8,128)S(1)}, f32[8,8,128]{2,1,0:T(8,128)}, u32[]{:S(2)}) copy-start(f32[8,8,128]{2,1,0:T(8,128)} %param.5) | copy-start | bytes 98308
  0.6 0.9 %copy-start = (f32[3,8,8,128]{3,2,1,0:T(8,128)S(1)}, f32[3,8,8,128]{3,2,1,0:T(8,128)}, u32[]{:S(2)}) copy-start(f32[3,8,8,128]{3,2,1,0:T(8,128)} %velocity.3) | copy-start | bytes 294916
  1.6 8.7 %collective-permute-start = (f32[17,8,128]{2,1,0:T(8,128)S(1)}, f32[17,8,128]{2,1,0:T(8,128)S(1)}, u32[]{:S(2)}, u32[]{:S(2)}) collective-permute-start(f32[17,8,128]{2,1,0:T(8,128)S(1)} %get-tuple-element.17), channel_id=1, source_target_pairs={{0,7},{1,2},{2,1},{3,4},{4,3},{5,6},{6,5},{7,0},{8,15},{9,10},{10,... | collective-permute-start | bytes 208904 | tf_op jit(solution)/shard_map/ppermute | solution.py:48
  7.5 5.1 %collective-permute-start.1 = (f32[17,8,128]{2,1,0:T(8,128)S(1)}, f32[17,8,128]{2,1,0:T(8,128)S(1)}, u32[]{:S(2)}, u32[]{:S(2)}) collective-permute-start(f32[17,8,128]{2,1,0:T(8,128)S(1)} %get-tuple-element.18), channel_id=1, source_target_pairs={{0,1},{1,0},{2,3},{3,2},{4,5},{5,4},{6,7},{7,6},{8,9},{9,8},{10,11... | collective-permute-start | bytes 208904 | tf_op jit(solution)/shard_map/ppermute | solution.py:49
  9.4 0.7 %copy-start.1 = (s32[1,1,1,64,1]{3,4,2,1,0:T(1,128)S(1)}, s32[1,1,1,64,1]{3,4,2,1,0:T(1,128)}, u32[]{:S(2)}) copy-start(s32[1,1,1,64,1]{3,4,2,1,0:T(1,128)} %param.8) | copy-start | bytes 772
  9.4 0.7 %copy-start.2 = (s32[1,1,1,64,1]{3,4,2,1,0:T(1,128)S(1)}, s32[1,1,1,64,1]{3,4,2,1,0:T(1,128)}, u32[]{:S(2)}) copy-start(s32[1,1,1,64,1]{3,4,2,1,0:T(1,128)} %param.9) | copy-start | bytes 772
  12.6 6.0 %collective-permute-start.2 = (f32[34,8,128]{2,1,0:T(8,128)S(1)}, f32[34,8,128]{2,1,0:T(8,128)S(1)}, u32[]{:S(2)}, u32[]{:S(2)}) collective-permute-start(f32[34,8,128]{2,1,0:T(8,128)S(1)} %get-tuple-element.21), channel_id=1, source_target_pairs={{8,0},{16,8},{24,16},{32,24},{40,32},{48,40},{56,48},{0,56},{9,1},... | collective-permute-start | bytes 417800 | tf_op jit(solution)/shard_map/ppermute | solution.py:41
  16.6 2.0 %collective-permute-start.3 = (f32[34,8,128]{2,1,0:T(8,128)S(1)}, f32[34,8,128]{2,1,0:T(8,128)S(1)}, u32[]{:S(2)}, u32[]{:S(2)}) collective-permute-start(f32[34,8,128]{2,1,0:T(8,128)S(1)} %get-tuple-element.22), channel_id=1, source_target_pairs={{0,8},{8,16},{16,24},{24,32},{32,40},{40,48},{48,56},{56,0},{1,9},... | collective-permute-start | bytes 417800 | tf_op jit(solution)/shard_map/ppermute | solution.py:36
  18.9 14.0 %collective-permute-start.4 = (f32[5,8,128]{2,1,0:T(8,128)S(1)}, f32[5,8,128]{2,1,0:T(8,128)S(1)}, u32[]{:S(2)}, u32[]{:S(2)}) collective-permute-start(f32[5,8,128]{2,1,0:T(8,128)S(1)} %get-tuple-element.25), channel_id=1, source_target_pairs={{0,64},{64,128},{128,192},{192,256},{256,320},{320,384},{384,448},... | collective-permute-start | bytes 61448 | tf_op jit(solution)/shard_map/ppermute | solution.py:36
  22.8 10.1 %collective-permute-start.5 = (f32[5,8,128]{2,1,0:T(8,128)S(1)}, f32[5,8,128]{2,1,0:T(8,128)S(1)}, u32[]{:S(2)}, u32[]{:S(2)}) collective-permute-start(f32[5,8,128]{2,1,0:T(8,128)S(1)} %get-tuple-element.26), channel_id=1, source_target_pairs={{64,0},{128,64},{192,128},{256,192},{320,256},{384,320},{448,384},... | collective-permute-start | bytes 61448 | tf_op jit(solution)/shard_map/ppermute | solution.py:41
